TPU v7x, 32 devices: a whole 2x2x4 slice. The times are simulated.
32 devices in a mesh: section: 2 (over y), tensor: 4 (over x, core), dp: 4 (over z).
Axes of the slice: x: 2, y: 2, z: 4, core: 2. Of those that a mesh axis runs over, the one named last changes fastest.
Arguments:
- tokens: bfloat16 [8, 512, 1024], P('dp', 'tensor'), may hold values from -6 to 6
- segment: int32 [8, 512], P('dp'), may hold values from -1 to 15, as said below
- score_grad: float32 [64, 4], P('dp'), may hold values from -96 to 96
- qkv_weight: bfloat16 [2, 1024, 3, 1024], P('section', None, None, 'tensor'), may hold values from -0.1875 to 0.1875
- qkv_bias: bfloat16 [2, 3, 1024], P('section', None, 'tensor'), may hold values from -4 to 4
- out_weight: bfloat16 [2, 1024, 1024], P('section', 'tensor'), may hold values from -3 to 3
- up_weight: bfloat16 [2, 1024, 4096], P('section', None, 'tensor'), may hold values from -0.1875 to 0.1875
- up_bias: bfloat16 [2, 4096], P('section', 'tensor'), may hold values from -4 to 4
- down_weight: bfloat16 [2, 4096, 1024], P('section', 'tensor'), may hold values from -0.09375 to 0.09375
- out_bias: bfloat16 [2, 2, 1024], P('section'), may hold values from -4 to 4
- norm_gain: bfloat16 [2, 2, 1024], P('section'), may hold values from 0.5 to 1.5
- norm_shift: bfloat16 [2, 2, 1024], P('section'), may hold values from -4 to 4
- proj_weight: bfloat16 [1024, 128], replicated, may hold values from -0.1875 to 0.1875
Outputs:
- scores: float32 [64, 4], P('dp', 'section')
- input_grad: float32 [8, 512, 1024], P('dp', 'tensor', 'section')
- qkv_weight_grad: float32 [2, 1024, 3, 1024], P('section', None, None, 'tensor')
- qkv_bias_grad: float32 [2, 3, 1024], P('section', None, 'tensor')
- out_weight_grad: float32 [2, 1024, 1024], P('section', 'tensor')
- up_weight_grad: float32 [2, 1024, 4096], P('section', None, 'tensor')
- up_bias_grad: float32 [2, 4096], P('section', 'tensor')
- down_weight_grad: float32 [2, 4096, 1024], P('section', 'tensor')
- out_bias_grad: float32 [2, 2, 1024], P('section')
- norm_gain_grad: float32 [2, 2, 1024], P('section')
- norm_shift_grad: float32 [2, 2, 1024], P('section')
- proj_weight_grad: float32 [1024, 128], P('section')
Inputs may be any that keep to these rules, and one draw needn't show every extreme that they name: `segment`: block 2g is group g's document: its first L positions are 0 and the rest -1, with 384 < L <= 512; L = 512 in some group and L is the least allowed value in another. Block 2g + 1 is group g's queries: its first c query slots are live, 8 <= c (and c >= 1), c = 16 in some group; live query q marks positions q * 32 to q * 32 + l - 1 with q, where 32 // 2 <= l; every other position is -1.
All inputs are finite; a program needn't handle non-finite values.
Results may differ from a plain program's by a relative error of at most 0.015.
Values may be sent and summed in bfloat16 or wider, within the bound.
No kernel may reach another device: no remote copies, remote signals or barrier semaphores. Data moves between devices by JAX's collectives and lax.ppermute only.
A program may use at most 192 MiB of HBM per device.

v0:
```python
import jax
import jax.numpy as jnp
from jax import lax
from jax.sharding import PartitionSpec as P

D = 1024
HD = 64
PROJ = 128
QLEN = 32


norm_eps = 1e-05
unit_eps = 1e-06
softness_factor = 0.0625
rope_base = 10000.0
hidden_score = -1000000000.0
contract_rows = (((0,), (0,)), ((), ()))
contract_cols = (((1,), (1,)), ((), ()))
contract_inner = (((1,), (0,)), ((), ()))


def from_behind(x, axis, by):
    size = lax.axis_size(axis)
    pairs = [(i, i + by) for i in range(size) if 0 <= i + by < size]
    return lax.ppermute(x, axis, pairs)


def swapped(block, axis, stride):
    count = lax.axis_size(axis)
    route = []
    for low in range(count):
        high = low | 1 << stride
        if high != low and high < count:
            route += [(low, high), (high, low)]
    return lax.ppermute(block, axis, route)


def rope_tables(positions, head_size):
    half_size = head_size // 2
    frequency = jnp.power(rope_base, -2.0 * jnp.arange(half_size, dtype=jnp.float32) / head_size)
    angles = positions.astype(jnp.float32)[:, None] * frequency[None, :]
    return (jnp.cos(angles)[:, None, :], jnp.sin(angles)[:, None, :])


def rotate(vectors, cosine_table, sine_table):
    half_size = vectors.shape[-1] // 2
    lower_half = vectors[..., :half_size]
    upper_half = vectors[..., half_size:]
    return jnp.concatenate(
        [
            lower_half * cosine_table - upper_half * sine_table,
            upper_half * cosine_table + lower_half * sine_table,
        ],
        axis=-1,
    )


def rotate_back(gradient, cosine_table, sine_table):
    half_size = gradient.shape[-1] // 2
    lower_half = gradient[..., :half_size]
    upper_half = gradient[..., half_size:]
    return jnp.concatenate(
        [
            lower_half * cosine_table + upper_half * sine_table,
            upper_half * cosine_table - lower_half * sine_table,
        ],
        axis=-1,
    )


def layer_norm(values, norm_gains, shifts):
    centred = values - jnp.mean(values, axis=-1, keepdims=True)
    inverse = lax.rsqrt(jnp.mean(centred * centred, axis=-1, keepdims=True) + norm_eps)
    normed = centred * inverse
    return (normed * norm_gains + shifts, normed, inverse)


def norm_back(gradient, normed, inverse):
    return inverse * (
        gradient
        - jnp.mean(gradient, axis=-1, keepdims=True)
        - normed * jnp.mean(gradient * normed, axis=-1, keepdims=True)
    )


def gelu_slope(values):
    return (
        0.5 * (1.0 + lax.erf(values * 0.7071067811865476))
        + values * jnp.exp(-0.5 * values * values) * 0.3989422804014327
    )


def tensor_rows(share):
    return lax.all_gather(share, "tensor", axis=0, tiled=True)


def tensor_reduce(product_rows, share_rows):
    return lax.psum_scatter(
        product_rows(jnp.int32(0), share_rows * lax.axis_size("tensor")),
        "tensor",
        scatter_dimension=0,
        tiled=True,
    )


def row_product(left, right, contraction):

    def product_rows(row_start, row_count):
        return lax.dot_general(left, right, contraction, preferred_element_type=jnp.float32)

    return product_rows


def attend(gathered, qkv_weight, qkv_bias, seg_ids, cosine_table, sine_table):
    block_rows, model_width = gathered.shape
    local_width = qkv_weight.shape[-1]
    heads_shape = (block_rows, local_width // HD, HD)
    projected = jnp.dot(
        gathered,
        qkv_weight.reshape(model_width, 3 * local_width),
        preferred_element_type=jnp.float32,
    )
    projected = projected + qkv_bias.reshape(3 * local_width).astype(jnp.float32)
    queries = rotate(
        projected[:, :local_width].reshape(heads_shape), cosine_table, sine_table
    ).astype(jnp.bfloat16)
    key_rows = rotate(
        projected[:, local_width : 2 * local_width].reshape(heads_shape), cosine_table, sine_table
    ).astype(jnp.bfloat16)
    value_rows = projected[:, 2 * local_width :].reshape(heads_shape).astype(jnp.bfloat16)
    scores = jnp.einsum(
        "qhd,khd->hqk", queries, key_rows, preferred_element_type=jnp.float32
    ) * HD ** (-0.5)
    allowed = seg_ids[:, None] == seg_ids[None, :]
    softmax = jax.nn.softmax(jnp.where(allowed[None], scores, hidden_score), axis=-1)
    softmax_low = softmax.astype(jnp.bfloat16)
    mixed_heads = jnp.einsum(
        "hqk,khd->qhd", softmax_low, value_rows, preferred_element_type=jnp.float32
    )
    mixed_heads = mixed_heads.reshape(block_rows, local_width).astype(jnp.bfloat16)
    return (queries, key_rows, value_rows, softmax, softmax_low, mixed_heads)


def feed(hidden_rows, up_weight, up_bias):
    hidden_pre = jnp.dot(
        hidden_rows, up_weight, preferred_element_type=jnp.float32
    ) + up_bias.astype(jnp.float32)
    return (hidden_pre, jax.nn.gelu(hidden_pre, approximate=False).astype(jnp.bfloat16))


def block_forward(section_input, seg_ids, cosine_table, sine_table, weights):
    (
        qkv_weight,
        qkv_bias,
        out_weight,
        up_weight,
        up_bias,
        down_weight,
        out_bias,
        norm_gain,
        norm_shift,
    ) = weights
    share_rows = section_input.shape[0]
    residual = section_input.astype(jnp.float32)
    gathered = tensor_rows(section_input)
    attention = attend(gathered, qkv_weight[0], qkv_bias[0], seg_ids, cosine_table, sine_table)
    attention_sum = tensor_reduce(
        row_product(attention[5], out_weight[0], contract_inner), share_rows
    )
    first_sum = residual + attention_sum + out_bias[0, 0].astype(jnp.float32)
    normed_one = layer_norm(
        first_sum, norm_gain[0, 0].astype(jnp.float32), norm_shift[0, 0].astype(jnp.float32)
    )[0]
    hidden_rows = tensor_rows(normed_one.astype(jnp.bfloat16))
    hidden_pre, hidden_low = feed(hidden_rows, up_weight[0], up_bias[0])
    feed_sum = tensor_reduce(row_product(hidden_low, down_weight[0], contract_inner), share_rows)
    second_sum = normed_one + feed_sum + out_bias[0, 1].astype(jnp.float32)
    output = layer_norm(
        second_sum, norm_gain[0, 1].astype(jnp.float32), norm_shift[0, 1].astype(jnp.float32)
    )[0]
    return (
        output,
        (gathered, first_sum, hidden_rows, second_sum),
        (attention, hidden_pre, hidden_low),
    )


def local_again(record, seg_ids, cosine_table, sine_table, weights):
    attention = attend(record[0], weights[0][0], weights[1][0], seg_ids, cosine_table, sine_table)
    hidden_pre, hidden_low = feed(record[2], weights[3][0], weights[4][0])
    return (attention, hidden_pre, hidden_low)


def feed_back(gradient, record, local_parts, weights):
    up_weight, down_weight, norm_gain, norm_shift = (weights[3], weights[5], weights[7], weights[8])
    first_sum, hidden_rows, second_sum = (record[1], record[2], record[3])
    hidden_pre, hidden_low = (local_parts[1], local_parts[2])
    share_rows = gradient.shape[0]
    norm_gains = norm_gain[0].astype(jnp.float32)
    shifts = norm_shift[0].astype(jnp.float32)
    unit_one, inverse_one = layer_norm(first_sum, norm_gains[0], shifts[0])[1:]
    unit_two, inverse_two = layer_norm(second_sum, norm_gains[1], shifts[1])[1:]
    gain_two = jnp.sum(gradient * unit_two, axis=0)
    shift_two = jnp.sum(gradient, axis=0)
    second_grad = norm_back(gradient * norm_gains[1], unit_two, inverse_two)
    down_bias_grad = jnp.sum(second_grad, axis=0)
    spread = tensor_rows(second_grad.astype(jnp.bfloat16))
    down_grad = lax.dot_general(
        hidden_low, spread, contract_rows, preferred_element_type=jnp.float32
    )
    hidden_grad = lax.dot_general(
        spread, down_weight[0], contract_cols, preferred_element_type=jnp.float32
    ) * gelu_slope(hidden_pre)
    up_bias_grad = jnp.sum(hidden_grad, axis=0)
    hidden_grad_low = hidden_grad.astype(jnp.bfloat16)
    up_grad = lax.dot_general(
        hidden_rows, hidden_grad_low, contract_rows, preferred_element_type=jnp.float32
    )
    normed_grad = second_grad + tensor_reduce(
        row_product(hidden_grad_low, up_weight[0], contract_cols), share_rows
    )
    return (
        normed_grad,
        (unit_one, inverse_one),
        (up_grad, up_bias_grad, down_grad),
        (gain_two, shift_two, down_bias_grad),
    )


def attend_back(normed_grad, norm_state, record, local_parts, weights, cosine_table, sine_table):
    qkv_weight, out_weight, norm_gain = (weights[0], weights[2], weights[7])
    unit_one, inverse_one = norm_state
    gathered = record[0]
    queries, key_rows, value_rows, softmax, softmax_low, mixed_heads = local_parts[0]
    block_rows, local_heads = (queries.shape[0], queries.shape[1])
    local_width = local_heads * HD
    share_rows = normed_grad.shape[0]
    norm_gains = norm_gain[0].astype(jnp.float32)
    gain_one = jnp.sum(normed_grad * unit_one, axis=0)
    shift_one = jnp.sum(normed_grad, axis=0)
    first_grad = norm_back(normed_grad * norm_gains[0], unit_one, inverse_one)
    out_bias_grad = jnp.sum(first_grad, axis=0)
    spread = tensor_rows(first_grad.astype(jnp.bfloat16))
    out_grad = lax.dot_general(
        mixed_heads, spread, contract_rows, preferred_element_type=jnp.float32
    )
    mixed_grad = lax.dot_general(
        spread, out_weight[0], contract_cols, preferred_element_type=jnp.float32
    )
    mixed_grad = mixed_grad.astype(jnp.bfloat16).reshape(block_rows, local_heads, HD)
    soft_grad = jnp.einsum(
        "qhd,khd->hqk", mixed_grad, value_rows, preferred_element_type=jnp.float32
    )
    value_grad = jnp.einsum(
        "hqk,qhd->khd", softmax_low, mixed_grad, preferred_element_type=jnp.float32
    )
    score_slope = softmax * (soft_grad - jnp.sum(soft_grad * softmax, axis=-1, keepdims=True))
    score_slope = score_slope.astype(jnp.bfloat16) * jnp.asarray(HD ** (-0.5), jnp.bfloat16)
    query_grad = rotate_back(
        jnp.einsum("hqk,khd->qhd", score_slope, key_rows, preferred_element_type=jnp.float32),
        cosine_table,
        sine_table,
    )
    key_grad = rotate_back(
        jnp.einsum("hqk,qhd->khd", score_slope, queries, preferred_element_type=jnp.float32),
        cosine_table,
        sine_table,
    )
    projected_grad = jnp.concatenate(
        [
            query_grad.reshape(block_rows, local_width),
            key_grad.reshape(block_rows, local_width),
            value_grad.reshape(block_rows, local_width),
        ],
        axis=1,
    )
    qkv_bias_grad = jnp.sum(projected_grad, axis=0).reshape(3, local_width)
    projected_low = projected_grad.astype(jnp.bfloat16)
    qkv_grad = lax.dot_general(
        gathered, projected_low, contract_rows, preferred_element_type=jnp.float32
    ).reshape(gathered.shape[1], 3, local_width)
    flat_weight = qkv_weight[0].reshape(gathered.shape[1], 3 * local_width)
    input_grad = first_grad + tensor_reduce(
        row_product(projected_low, flat_weight, contract_cols), share_rows
    )
    return (input_grad, (qkv_grad, qkv_bias_grad, out_grad), (gain_one, shift_one, out_bias_grad))


def add_valid(totals, updates, is_valid):
    return tuple(
        (
            (
                jnp.where(is_valid, update, 0.0)
                if running is None
                else running + jnp.where(is_valid, update, 0.0)
            )
            for running, update in zip(totals, updates)
        )
    )


def on_device(
    tokens,
    segment,
    score_grad,
    qkv_weight,
    qkv_bias,
    out_weight,
    up_weight,
    up_bias,
    down_weight,
    out_bias,
    norm_gain,
    norm_shift,
    proj_weight,
):
    weights = (
        qkv_weight,
        qkv_bias,
        out_weight,
        up_weight,
        up_bias,
        down_weight,
        out_bias,
        norm_gain,
        norm_shift,
    )
    section_zero = lax.axis_index("section") == 0
    share_rows = tokens.shape[1]
    tensor_count = lax.axis_size("tensor")
    groups = lax.axis_size("dp")
    block_rows = share_rows * tensor_count
    share_start = lax.axis_index("tensor") * share_rows
    token_index = jnp.arange(block_rows)
    tables = (rope_tables(token_index, HD), rope_tables(token_index % QLEN, HD))

    def section_pick(zero_block, one_block):
        return (
            jnp.where(section_zero, segment[zero_block], segment[one_block]),
            jnp.where(section_zero, tables[zero_block][0], tables[one_block][0]),
            jnp.where(section_zero, tables[zero_block][1], tables[one_block][1]),
        )

    received = jnp.zeros((share_rows, D), jnp.bfloat16)
    inputs_kept, records, outputs = ([], [], [])
    for forward_step in range(3):
        seg_ids, cosine_table, sine_table = section_pick(
            min(forward_step, 1), max(forward_step - 1, 0)
        )
        section_input = jnp.where(section_zero, tokens[min(forward_step, 1)], received)
        output, record, local_parts = block_forward(
            section_input, seg_ids, cosine_table, sine_table, weights
        )
        inputs_kept.append(section_input)
        records.append(record)
        outputs.append(output)
        if forward_step < 2:
            received = from_behind(output.astype(jnp.bfloat16), "section", 1)

    def embed(values):
        values_low = values.astype(jnp.bfloat16)
        projected = jnp.dot(values_low, proj_weight, preferred_element_type=jnp.float32)
        inverse = lax.rsqrt(jnp.sum(projected * projected, axis=-1, keepdims=True) + unit_eps)
        return (values_low, inverse, projected * inverse)

    def embed_back(values_low, inverse, unit_rows, gradient):
        projected_low = (
            inverse * (gradient - unit_rows * jnp.sum(gradient * unit_rows, axis=-1, keepdims=True))
        ).astype(jnp.bfloat16)
        return (
            lax.dot_general(
                projected_low, proj_weight, contract_cols, preferred_element_type=jnp.float32
            ),
            lax.dot_general(
                values_low, projected_low, contract_rows, preferred_element_type=jnp.float32
            ),
        )

    doc_low, doc_inverse, doc_units = embed(outputs[1])
    query_low, query_inverse, query_units = embed(outputs[2])
    doc_alive = (lax.dynamic_slice_in_dim(segment[0], share_start, share_rows) == 0).astype(
        jnp.bfloat16
    )
    all_units, all_alive = (
        lax.all_gather(doc_units.astype(jnp.bfloat16), ("tensor", "dp"), axis=0, tiled=True),
        lax.all_gather(doc_alive, ("tensor", "dp"), axis=0, tiled=True),
    )
    unit_blocks = all_units.reshape(tensor_count, groups, share_rows, PROJ)
    alive_blocks = all_alive.reshape(tensor_count, groups, share_rows)
    query_slots = score_grad.shape[0]
    slot_ids = jnp.arange(query_slots)
    member_share = (
        lax.dynamic_slice_in_dim(segment[1], share_start, share_rows)[:, None] == slot_ids[None, :]
    ).astype(jnp.float32)
    token_weights = jnp.dot(member_share, score_grad, precision=lax.Precision.HIGHEST)
    query_units_low = query_units.astype(jnp.bfloat16)

    def per_document(carried, doc_index):
        query_total, doc_total = carried
        key_units = lax.dynamic_index_in_dim(unit_blocks, doc_index, 1, keepdims=False).reshape(
            block_rows, PROJ
        )
        key_present = lax.dynamic_index_in_dim(alive_blocks, doc_index, 1, keepdims=False).reshape(
            block_rows
        )
        similarity_matrix = lax.dot_general(
            query_units_low, key_units, contract_cols, preferred_element_type=jnp.float32
        )
        score_logits = jnp.where(
            key_present[None, :] > 0, similarity_matrix / softness_factor, hidden_score
        )
        row_peak = jnp.max(score_logits, axis=-1, keepdims=True)
        exp_values = jnp.exp(score_logits - row_peak)
        exponent_sum = jnp.sum(exp_values, axis=-1, keepdims=True)
        smooth_maxima = softness_factor * (row_peak + jnp.log(exponent_sum))
        column = jnp.sum(member_share * smooth_maxima, axis=0)
        weight_column = lax.dynamic_index_in_dim(token_weights, doc_index, 1, keepdims=True)
        similar_grad = (exp_values / exponent_sum * weight_column).astype(jnp.bfloat16)
        query_total = query_total + jnp.dot(
            similar_grad, key_units, preferred_element_type=jnp.float32
        )
        doc_term = lax.dot_general(
            similar_grad, query_units_low, contract_rows, preferred_element_type=jnp.float32
        )
        doc_total = lax.dynamic_update_slice_in_dim(
            doc_total, doc_term.reshape(tensor_count, 1, share_rows, PROJ), doc_index, 1
        )
        return ((query_total, doc_total), column)

    initial = (
        jnp.zeros((share_rows, PROJ), jnp.float32),
        jnp.zeros((tensor_count, groups, share_rows, PROJ), jnp.float32),
    )
    (query_unit_grad, doc_terms), columns = lax.scan(per_document, initial, jnp.arange(groups))
    doc_unit_grad = lax.psum_scatter(
        doc_terms.reshape(tensor_count * groups * share_rows, PROJ),
        ("tensor", "dp"),
        scatter_dimension=0,
        tiled=True,
    )
    doc_back, doc_projection = embed_back(doc_low, doc_inverse, doc_units, doc_unit_grad)
    query_back, query_projection = embed_back(
        query_low, query_inverse, query_units, query_unit_grad
    )
    proj_grad = doc_projection + query_projection
    zero_ticks, one_ticks = ((1, 1, 0), (2, 1, 1))
    zero_blocks, one_blocks = ((1, 1, 0), (1, 0, 0))
    own_grads = (query_back, doc_back, doc_back)
    received_grad = jnp.zeros((share_rows, D), jnp.float32)
    input_grads = [None, None]
    feed_totals = (None, None, None)
    attend_totals = (None, None, None)
    small_totals = (None, None, None)
    for backward_step in range(3):
        seg_ids, cosine_table, sine_table = section_pick(
            zero_blocks[backward_step], one_blocks[backward_step]
        )
        zero_tick, one_tick = (zero_ticks[backward_step], one_ticks[backward_step])
        is_valid = jnp.where(section_zero, backward_step >= 1, backward_step <= 1)
        gradient = jnp.where(section_zero, received_grad, own_grads[backward_step])
        record = jax.tree.map(
            lambda zero_part, one_part: jnp.where(section_zero, zero_part, one_part),
            records[zero_tick],
            records[one_tick],
        )
        local_parts = local_again(record, seg_ids, cosine_table, sine_table, weights)
        normed_grad, norm_state, feed_grads, feed_small = feed_back(
            gradient, record, local_parts, weights
        )
        feed_totals = add_valid(feed_totals, feed_grads, is_valid)
        input_grad, attend_grads, attend_small = attend_back(
            normed_grad, norm_state, record, local_parts, weights, cosine_table, sine_table
        )
        attend_totals = add_valid(attend_totals, attend_grads, is_valid)
        small_parts = (
            jnp.stack([attend_small[0], feed_small[0]]),
            jnp.stack([attend_small[1], feed_small[1]]),
            jnp.stack([attend_small[2], feed_small[2]]),
        )
        small_totals = add_valid(small_totals, small_parts, is_valid)
        if backward_step < 2:
            received_grad = from_behind(input_grad.astype(jnp.bfloat16), "section", -1).astype(
                jnp.float32
            )
        if backward_step >= 1:
            input_grads[2 - backward_step] = input_grad
    summed = lax.psum(
        (
            attend_totals[0],
            attend_totals[1],
            attend_totals[2],
            feed_totals[0],
            feed_totals[1],
            feed_totals[2],
        ),
        "dp",
    )
    attend_totals = summed[:3]
    feed_totals = summed[3:]
    score_board = lax.dynamic_update_index_in_dim(
        jnp.zeros((groups, query_slots, groups), jnp.float32), columns.T, lax.axis_index("dp"), 0
    )
    gain_sum, shift_sum, bias_sum, proj_sum, board_sum = lax.psum(
        (small_totals[0], small_totals[1], small_totals[2], proj_grad, score_board),
        ("tensor", "dp"),
    )
    scores_full = lax.dynamic_index_in_dim(board_sum, lax.axis_index("dp"), 0, keepdims=False)
    input_stack = jnp.stack(input_grads)
    half_model = D // 2
    half_docs = groups // 2
    sent_input, sent_scores, sent_proj = swapped(
        (input_stack[:, :, half_model:], scores_full[:, :half_docs], proj_sum[:half_model]),
        "section",
        0,
    )
    scores_out = jnp.where(section_zero, sent_scores, scores_full[:, half_docs:])
    input_out = jnp.where(section_zero, input_stack[:, :, :half_model], sent_input)
    proj_out = jnp.where(section_zero, sent_proj, proj_sum[half_model:])
    return (
        scores_out,
        input_out,
        attend_totals[0][None],
        attend_totals[1][None],
        attend_totals[2][None],
        feed_totals[0][None],
        feed_totals[1][None],
        feed_totals[2][None],
        bias_sum[None],
        gain_sum[None],
        shift_sum[None],
        proj_out,
    )


def solution(mesh):
    return jax.shard_map(
        on_device,
        mesh=mesh,
        in_specs=(
            P("dp", "tensor", None),
            P("dp", None),
            P("dp", None),
            P("section", None, None, "tensor"),
            P("section", None, "tensor"),
            P("section", "tensor", None),
            P("section", None, "tensor"),
            P("section", "tensor"),
            P("section", "tensor", None),
            P("section", None, None),
            P("section", None, None),
            P("section", None, None),
            P(),
        ),
        out_specs=(
            P("dp", "section"),
            P("dp", "tensor", "section"),
            P("section", None, None, "tensor"),
            P("section", None, "tensor"),
            P("section", "tensor", None),
            P("section", None, "tensor"),
            P("section", "tensor"),
            P("section", "tensor", None),
            P("section", None, None),
            P("section", None, None),
            P("section", None, None),
            P("section", None),
        ),
        check_vma=False,
    )
```

profile of v0, /device:TPU:0, one launch (start us, length us, event | category | flops | bytes accessed | tf_op | source)
XLA Modules:
  0.0 1584.7 jit_solution(16772851444703420044)
XLA Ops:
  15.1 14.5 all-gather.37.cloned.1.call-done
  36.5 4.9 fusion.562
  46.2 31.4 %reduce-scatter.14.cloned.1.call-done = f32[128,1024]{1,0:T(8,128)} async-done(((f32[512,1024]{1,0:T(8,128)}), f32[128,1024]{1,0:T(8,128)}) %reduce-scatter.14.cloned.1.call-update) | async-done | bytes 524304 | tf_op jit(solution)/shard_map/reduce_scatter | solution.py:98
  80.1 16.8 %all-gather.15.cloned.1.call-done = bf16[512,1024]{1,0:T(8,128)(2,1)} async-done(((bf16[128,1024]{1,0:T(8,128)(2,1)}), bf16[512,1024]{1,0:T(8,128)(2,1)}) %all-gather.15.cloned.1.call-update) | async-done | bytes 1048592 | tf_op jit(solution)/shard_map/all_gather | solution.py:94
  96.9 9.5 fusion.68
  106.7 31.3 %reduce-scatter.16.cloned.1.call-done = f32[128,1024]{1,0:T(8,128)} async-done(((f32[512,1024]{1,0:T(8,128)}), f32[128,1024]{1,0:T(8,128)}) %reduce-scatter.16.cloned.1.call-update) | async-done | bytes 524304 | tf_op jit(solution)/shard_map/reduce_scatter | solution.py:98
  143.8 5.5 collective-permute-done
  152.3 15.6 all-gather.17.cloned.1.call-done
  179.9 5.5 fusion.563
  190.7 31.6 %reduce-scatter.18.cloned.1.call-done = f32[128,1024]{1,0:T(8,128)} async-done(((f32[512,1024]{1,0:T(8,128)}), f32[128,1024]{1,0:T(8,128)}) %reduce-scatter.18.cloned.1.call-update) | async-done | bytes 524304 | tf_op jit(solution)/shard_map/reduce_scatter | solution.py:98
  226.0 16.8 %all-gather.19.cloned.1.call-done = bf16[512,1024]{1,0:T(8,128)(2,1)} async-done(((bf16[128,1024]{1,0:T(8,128)(2,1)}), bf16[512,1024]{1,0:T(8,128)(2,1)}) %all-gather.19.cloned.1.call-update) | async-done | bytes 1048592 | tf_op jit(solution)/shard_map/all_gather | solution.py:94
  242.8 8.0 fusion.33
  254.4 31.5 %reduce-scatter.20.cloned.1.call-done = f32[128,1024]{1,0:T(8,128)} async-done(((f32[512,1024]{1,0:T(8,128)}), f32[128,1024]{1,0:T(8,128)}) %reduce-scatter.20.cloned.1.call-update) | async-done | bytes 524304 | tf_op jit(solution)/shard_map/reduce_scatter | solution.py:98
  293.5 5.5 collective-permute-done.1
  302.4 16.2 %all-gather.21.cloned.1.call-done = bf16[512,1024]{1,0:T(8,128)(2,1)} async-done(((bf16[128,1024]{1,0:T(8,128)(2,1)}), bf16[512,1024]{1,0:T(8,128)(2,1)}) %all-gather.21.cloned.1.call-update) | async-done | bytes 1048592 | tf_op jit(solution)/shard_map/all_gather | solution.py:94
  340.9 4.9 fusion.564
  350.5 31.5 %reduce-scatter.22.cloned.1.call-done = f32[128,1024]{1,0:T(8,128)} async-done(((f32[512,1024]{1,0:T(8,128)}), f32[128,1024]{1,0:T(8,128)}) %reduce-scatter.22.cloned.1.call-update) | async-done | bytes 524304 | tf_op jit(solution)/shard_map/reduce_scatter | solution.py:98
  389.2 10.3 reduce-scatter.24.cloned.1.call-start
  399.5 6.5 all-gather.23.cloned.1.call-done
  406.0 9.5 fusion.64
  416.3 31.4 %all-gather = bf16[1,2048]{1,0:T(2,128)(2,1)S(1)} all-gather(bf16[1,128]{1,0:T(2,128)(2,1)S(1)} %compare_convert_fusion), channel_id=2, replica_groups=mesh['section'=2,'tensor'=4,'dp'=4] {'tensor','dp'}, dimensions={1}, use_global_device_ids=true | all-gather | bytes 4352 | tf_op jit(solution)/shard_map/all_gather | solution.py:386
  450.5 35.7 %all_gather.47 = bf16[2048,128]{0,1:T(8,128)(2,1)} all-gather(bf16[128,128]{0,1:T(8,128)(2,1)S(1)} %multiply_convert_fusion.9), channel_id=1, replica_groups=mesh['section'=2,'tensor'=4,'dp'=4] {'tensor','dp'}, dimensions={0}, use_global_device_ids=true | all-gather | bytes 557056 | tf_op jit(solution)/shard_map/all_gather | solution.py:385
  497.7 68.1 %while.15 = (s32[]{:T(128)}, f32[128,128]{1,0:T(8,128)}, f32[4,4,128,128]{2,1,0,3:T(4,128)}, f32[4,16]{1,0:T(4,128)}, s32[4]{0:T(128)S(1)}, /*index=5*/bf16[4,4,...) while((s32[]{:T(128)}, f32[128,128]{1,0:T(8,128)}, ...), condition=%wide.region_30.31_spmd.clone, body=%wide.region_26.30_spmd.clone.sunk | while | flops 51223028 | bytes 3090833 | solution.py:434
  505.1 7.6 dynamic_update_slice.17
  522.3 7.6 dynamic_update_slice.17
  539.6 7.6 dynamic_update_slice.17
  556.8 7.6 dynamic_update_slice.17
  573.2 3.8 fusion.78
  577.0 12.3 all-gather.25.cloned.1.call-done
  589.3 5.0 fusion.569
  599.9 29.7 %reduce-scatter.26.cloned.1.call-done = f32[128,1024]{1,0:T(8,128)} async-done(((f32[512,1024]{1,0:T(8,128)}), f32[128,1024]{1,0:T(8,128)}) %reduce-scatter.26.cloned.1.call-update) | async-done | bytes 524304 | tf_op jit(solution)/shard_map/reduce_scatter | solution.py:98
  636.4 5.0 fusion.565
  641.4 8.5 all-gather.27.cloned.1.call-done
  656.7 8.6 fusion.186
  665.3 8.3 fusion.191
  681.3 28.8 %reduce-scatter.28.cloned.1.call-done = f32[128,1024]{1,0:T(8,128)} async-done(((f32[512,1024]{1,0:T(8,128)}), f32[128,1024]{1,0:T(8,128)}) %reduce-scatter.28.cloned.1.call-update) | async-done | bytes 524304 | tf_op jit(solution)/shard_map/reduce_scatter | solution.py:98
  713.3 57.7 %reduce-scatter.30.cloned.1.call-done = f32[128,128]{0,1:T(8,128)} async-done(((f32[2048,128]{0,1:T(8,128)}), f32[128,128]{0,1:T(8,128)}) %reduce-scatter.30.cloned.1.call-update) | async-done | bytes 65552 | tf_op jit(solution)/shard_map/reduce_scatter | solution.py:435
  776.0 15.8 all-gather.29.cloned.1.call-done
  791.8 5.0 fusion.568
  800.7 31.4 %reduce-scatter.32.cloned.1.call-done = f32[128,1024]{1,0:T(8,128)} async-done(((f32[512,1024]{1,0:T(8,128)}), f32[128,1024]{1,0:T(8,128)}) %reduce-scatter.32.cloned.1.call-update) | async-done | bytes 524304 | tf_op jit(solution)/shard_map/reduce_scatter | solution.py:98
  835.4 16.8 %all-gather.31.cloned.1.call-done = bf16[512,1024]{1,0:T(8,128)(2,1)} async-done(((bf16[128,1024]{1,0:T(8,128)(2,1)}), bf16[512,1024]{1,0:T(8,128)(2,1)}) %all-gather.31.cloned.1.call-update) | async-done | bytes 1048592 | tf_op jit(solution)/shard_map/all_gather | solution.py:94
  859.7 7.9 fusion.196
  867.6 8.4 fusion.201
  881.3 30.9 %reduce-scatter.34.cloned.1.call-done = f32[128,1024]{1,0:T(8,128)} async-done(((f32[512,1024]{1,0:T(8,128)}), f32[128,1024]{1,0:T(8,128)}) %reduce-scatter.34.cloned.1.call-update) | async-done | bytes 524304 | tf_op jit(solution)/shard_map/reduce_scatter | solution.py:98
  916.4 8.4 collective-permute-done.4
  927.9 3.8 fusion.72
  931.7 12.1 all-gather.33.cloned.1.call-done
  943.8 5.0 fusion.567
  965.2 5.5 fusion.566
  973.6 10.5 reduce-scatter.36.cloned.1.call-done
  993.9 4.7 fusion.326
  998.7 7.1 fusion.225
  1015.0 3.7 fusion.229
  1021.5 8.7 fusion.206
  1030.2 8.3 fusion.211
  1054.1 7.0 add_bitcast_fusion
  1063.9 3.7 copy.180
  1070.6 27.5 %all-reduce.6.cloned.1.call-done = f32[1024,128]{1,0:T(8,128)} async-done(((f32[1024,128]{1,0:T(8,128)}), f32[1024,128]{1,0:T(8,128)}) %all-reduce.6.cloned.1.call-update) | async-done | bytes 524304 | tf_op jit(solution)/shard_map/psum | solution.py:503
  1100.8 7.2 collective-permute-done.6
  1112.9 19.6 %reduce-scatter.38.cloned.1.call-done = f32[128,1024]{1,0:T(8,128)} async-done(((f32[512,1024]{1,0:T(8,128)}), f32[128,1024]{1,0:T(8,128)}) %reduce-scatter.38.cloned.1.call-update) | async-done | bytes 524304 | tf_op jit(solution)/shard_map/reduce_scatter | solution.py:98
  1136.2 74.1 %all-reduce = (f32[4,16,4]{1,2,0:T(4,128)S(1)}, f32[1,2,1024]{2,1,0:T(2,128)}, f32[1,2,1024]{2,1,0:T(2,128)}, f32[1,2,1024]{2,1,0:T(2,128)}) all-reduce(f32[4,16,4]{1,2,0:T(4,128)S(1)} %bitcast_dynamic-update-slice_fusion, f32[1,2,1024]{2,1,0:T(2,128)S(1)} %get-tuple-element.345, ...), channel_id=1, replica_groups=mesh['section'=2,'tensor'=4,'dp'=4] {'tensor','dp'}, use_global_device_ids=true, to_apply=%region_31.32 | all-reduce | flops 6400 | bytes 51200 | tf_op jit(solution)/shard_map/psum | solution.py:503
  1212.0 16.2 %all-reduce.1 = (f32[1,3,256]{2,0,1:T(1,128)}, f32[1,1024]{1,0:T(1,128)}) all-reduce(f32[1,3,256]{2,0,1:T(1,128)S(1)} %broadcast_in_dim.146, f32[1,1024]{1,0:T(1,128)S(1)} %bitcast.425), channel_id=1, replica_groups=mesh['section'=2,'tensor'=4,'dp'=4] {'dp'}, use_global_device_ids=true, to_apply=%region_72.73 | all-reduce | flops 1792 | bytes 14336 | tf_op jit(solution)/shard_map/psum | solution.py:487
  1229.6 337.4 %all-reduce.8.cloned.1.call-done = (f32[1,1024,3,256]{3,1,2,0:T(8,128)}, f32[1,256,1024]{2,1,0:T(8,128)}, f32[1,1024,1024]{2,1,0:T(8,128)}, f32[1,1024,1024]{2,1,0:T(8,128)}) async-done(((f32[1,1024,3,256]{3,1,2,0:T(8,128)}, f32[1,256,1024]{2,1,0:T(8,128)}, f32[1,1024,1024]{2,1,0:T(8,128)}, f32[1,1024,1024]{2,1,0:T(8,128)}), (f32[1,1024,3,256]{3,1,2,0:T(8,128)}, f32[1,256,1024]{2,1,0:T(8,128)}, ...) | async-done | bytes 12582928 | tf_op jit(solution)/shard_map/psum | solution.py:487
  1567.0 3.9 copy.290
  (661 shorter events, 296.5 us)
Async XLA Ops:
  7.2 89.7 %copy-start = (bf16[1,1024,1024]{2,1,0:T(8,128)(2,1)S(1)}, bf16[1,1024,1024]{2,1,0:T(8,128)(2,1)}, u32[]{:S(2)}) copy-start(bf16[1,1024,1024]{2,1,0:T(8,128)(2,1)} %param.21) | copy-start | bytes 6291460
  7.2 22.4 %all-gather.37.cloned.1.call-start = ((), (), s32[]{:S(2)}) async-start(), calls=%async_computation.38 | async-start | bytes 1310720 | tf_op jit(solution)/shard_map/all_gather | solution.py:94
  9.1 68.5 %reduce-scatter.14.cloned.1.call-start = ((), (), s32[]{:S(2)}) async-start(), calls=%async_computation.13 | async-start | bytes 2621440 | tf_op jit(solution)/shard_map/reduce_scatter | solution.py:98
  15.1 323.0 %copy-start.82 = (f32[512,32]{0,1:T(8,128)}, f32[512,32]{0,1:T(8,128)S(1)}, u32[]{:S(2)}) copy-start(f32[512,32]{0,1:T(8,128)S(1)} %get-tuple-element.317) | copy-start | bytes 196612
  15.1 323.0 %copy-start.84 = (f32[512,32]{0,1:T(8,128)}, f32[512,32]{0,1:T(8,128)S(1)}, u32[]{:S(2)}) copy-start(f32[512,32]{0,1:T(8,128)S(1)} %get-tuple-element.319) | copy-start | bytes 196612
  46.0 34.1 %copy-start.144 = (bf16[1,1024]{1,0:T(2,128)(2,1)S(1)}, bf16[1,1024]{1,0:T(2,128)(2,1)}, u32[]{:S(2)}) copy-start(bf16[1,1024]{1,0:T(2,128)(2,1)} %param.22) | copy-start | bytes 6148
  46.0 50.9 %all-gather.15.cloned.1.call-start = ((), (), s32[]{:S(2)}) async-start(), calls=%async_computation.14 | async-start | bytes 1310720 | tf_op jit(solution)/shard_map/all_gather | solution.py:94
  46.1 60.3 %copy-start.106 = (f32[1,1,1024]{2,1,0:T(1,128)}, f32[1,1,1024]{2,1,0:T(1,128)S(1)}, u32[]{:S(2)}) copy-start(f32[1,1,1024]{2,1,0:T(1,128)S(1)} %get-tuple-element.315) | copy-start | bytes 12292
  46.1 91.9 %copy-start.103 = (f32[1,1,1024]{2,1,0:T(1,128)}, f32[1,1,1024]{2,1,0:T(1,128)S(1)}, u32[]{:S(2)}) copy-start(f32[1,1,1024]{2,1,0:T(1,128)S(1)} %get-tuple-element.316) | copy-start | bytes 12292
  46.1 243.0 %copy-start.101 = (f32[1,1,1024]{2,1,0:T(1,128)}, f32[1,1,1024]{2,1,0:T(1,128)S(1)}, u32[]{:S(2)}) copy-start(f32[1,1,1024]{2,1,0:T(1,128)S(1)} %get-tuple-element.311) | copy-start | bytes 12292
  80.0 58.0 %reduce-scatter.16.cloned.1.call-start = ((), (), s32[]{:S(2)}) async-start(), calls=%async_computation.15 | async-start | bytes 2621440 | tf_op jit(solution)/shard_map/reduce_scatter | solution.py:98
  80.0 26.3 %copy-start.145 = (f32[1,1024]{1,0:T(1,128)}, f32[1,1024]{1,0:T(1,128)S(1)}, u32[]{:S(2)}) copy-start(f32[1,1024]{1,0:T(1,128)S(1)} %add.669) | copy-start | bytes 12292
  106.4 61.5 %all-gather.17.cloned.1.call-start = ((), (), s32[]{:S(2)}) async-start(), calls=%async_computation.16 | async-start | bytes 1310720 | tf_op jit(solution)/shard_map/all_gather | solution.py:94
  140.4 8.9 collective-permute-start
  150.1 72.1 %reduce-scatter.18.cloned.1.call-start = ((), (), s32[]{:S(2)}) async-start(), calls=%async_computation.17 | async-start | bytes 2621440 | tf_op jit(solution)/shard_map/reduce_scatter | solution.py:98
  188.8 33.4 %copy-start.40 = (bf16[128,1024]{1,0:T(8,128)(2,1)S(1)}, bf16[128,1024]{1,0:T(8,128)(2,1)}, u32[]{:S(2)}) copy-start(bf16[128,1024]{1,0:T(8,128)(2,1)} %bitcast_select_fusion.4) | copy-start | bytes 786436
  190.6 52.2 %all-gather.19.cloned.1.call-start = ((), (), s32[]{:S(2)}) async-start(), calls=%async_computation.18 | async-start | bytes 1310720 | tf_op jit(solution)/shard_map/all_gather | solution.py:94
  224.8 61.2 %copy-start.125 = (f32[128]{0:T(128)}, f32[128]{0:T(128)S(1)}, u32[]{:S(2)}) copy-start(f32[128]{0:T(128)S(1)} %broadcast_multiply_fusion.19) | copy-start | bytes 1540
  225.0 60.9 %copy-start.127 = (f32[128]{0:T(128)}, f32[128]{0:T(128)S(1)}, u32[]{:S(2)}) copy-start(f32[128]{0:T(128)S(1)} %add_rsqrt_fusion.9) | copy-start | bytes 1540
  225.9 60.0 %reduce-scatter.20.cloned.1.call-start = ((), (), s32[]{:S(2)}) async-start(), calls=%async_computation.19 | async-start | bytes 2621440 | tf_op jit(solution)/shard_map/reduce_scatter | solution.py:98
  254.4 31.6 %copy-start.104 = (f32[1,1,1024]{2,1,0:T(1,128)S(1)}, f32[1,1,1024]{2,1,0:T(1,128)}, u32[]{:S(2)}) copy-start(f32[1,1,1024]{2,1,0:T(1,128)} %copy-done.103) | copy-start | bytes 12292
  254.4 64.2 %all-gather.21.cloned.1.call-start = ((), (), s32[]{:S(2)}) async-start(), calls=%async_computation.20 | async-start | bytes 1310720 | tf_op jit(solution)/shard_map/all_gather | solution.py:94
  290.2 159.0 %copy-start.38 = (bf16[128,1024]{1,0:T(8,128)(2,1)}, bf16[128,1024]{1,0:T(8,128)(2,1)S(1)}, u32[]{:S(2)}) copy-start(bf16[128,1024]{1,0:T(8,128)(2,1)S(1)} %add_convert_fusion.2) | copy-start | bytes 786436
  290.2 8.8 collective-permute-start.1
  300.7 81.4 %reduce-scatter.22.cloned.1.call-start = ((), (), s32[]{:S(2)}) async-start(), calls=%async_computation.21 | async-start | bytes 2621440 | tf_op jit(solution)/shard_map/reduce_scatter | solution.py:98
  348.7 33.4 %copy-start.107 = (f32[1,1,1024]{2,1,0:T(1,128)S(1)}, f32[1,1,1024]{2,1,0:T(1,128)}, u32[]{:S(2)}) copy-start(f32[1,1,1024]{2,1,0:T(1,128)} %copy-done.106) | copy-start | bytes 12292
  350.5 55.6 %copy-start.146 = (f32[1,1024]{1,0:T(1,128)S(1)}, f32[1,1024]{1,0:T(1,128)}, u32[]{:S(2)}) copy-start(f32[1,1024]{1,0:T(1,128)} %copy-done.145) | copy-start | bytes 12292
  350.5 55.6 %all-gather.23.cloned.1.call-start = ((), (), s32[]{:S(2)}) async-start(), calls=%async_computation.22 | async-start | bytes 1310720 | tf_op jit(solution)/shard_map/all_gather | solution.py:94
  389.2 99.1 %reduce-scatter.24.cloned.1.call-start = ((), (), s32[]{:S(2)}) async-start(), calls=%async_computation.23 | async-start | bytes 2621440 | tf_op jit(solution)/shard_map/reduce_scatter | solution.py:98
  415.6 32.8 %copy-start.157 = (f32[16,4]{0,1:T(4,128)S(1)}, f32[16,4]{0,1:T(4,128)}, u32[]{:S(2)}) copy-start(f32[16,4]{0,1:T(4,128)} %param.17) | copy-start | bytes 772
  415.6 33.6 %copy-start.109 = (bf16[1,2,1024]{2,1,0:T(2,128)(2,1)S(1)}, bf16[1,2,1024]{2,1,0:T(2,128)(2,1)}, u32[]{:S(2)}) copy-start(bf16[1,2,1024]{2,1,0:T(2,128)(2,1)} %param.25) | copy-start | bytes 12292
  415.6 72.6 %copy-start.105 = (f32[1,1,1024]{2,1,0:T(1,128)S(1)}, f32[1,1,1024]{2,1,0:T(1,128)}, u32[]{:S(2)}) copy-start(f32[1,1,1024]{2,1,0:T(1,128)} %copy-done.103) | copy-start | bytes 12292
  415.6 173.7 %all-gather.25.cloned.1.call-start = ((), (), s32[]{:S(2)}) async-start(), calls=%async_computation.24 | async-start | bytes 1310720 | tf_op jit(solution)/shard_map/all_gather | solution.py:94
  497.7 68.1 %copy-start.153 = (f32[128]{0:T(128)S(1)}, f32[128]{0:T(128)}, u32[]{:S(2)}) copy-start(f32[128]{0:T(128)} %get-tuple-element.225) | copy-start | bytes 1540
  573.1 56.5 %reduce-scatter.26.cloned.1.call-start = ((), (), s32[]{:S(2)}) async-start(), calls=%async_computation.25 | async-start | bytes 2621440 | tf_op jit(solution)/shard_map/reduce_scatter | solution.py:98
  598.0 51.9 %all-gather.27.cloned.1.call-start = ((), (), s32[]{:S(2)}) async-start(), calls=%async_computation.26 | async-start | bytes 1310720 | tf_op jit(solution)/shard_map/all_gather | solution.py:94
  633.0 77.0 %reduce-scatter.28.cloned.1.call-start = ((), (), s32[]{:S(2)}) async-start(), calls=%async_computation.27 | async-start | bytes 2621440 | tf_op jit(solution)/shard_map/reduce_scatter | solution.py:98
  641.4 23.9 %copy-start.166 = (f32[4,512]{1,0:T(4,128)}, f32[4,512]{1,0:T(4,128)S(1)}, u32[]{:S(2)}) copy-start(f32[4,512]{1,0:T(4,128)S(1)} %get-tuple-element.334) | copy-start | bytes 24580
  678.5 92.5 %reduce-scatter.30.cloned.1.call-start = ((), (), s32[]{:S(2)}) async-start(), calls=%async_computation.28 | async-start | bytes 1114112 | tf_op jit(solution)/shard_map/reduce_scatter | solution.py:435
  678.5 94.2 %copy-start.44 = (bf16[1024,128]{1,0:T(8,128)(2,1)S(1)}, bf16[1024,128]{1,0:T(8,128)(2,1)}, u32[]{:S(2)}) copy-start(bf16[1024,128]{1,0:T(8,128)(2,1)} %param.27) | copy-start | bytes 786436
  678.5 94.2 %copy-start.130 = (f32[128]{0:T(128)S(1)}, f32[128]{0:T(128)}, u32[]{:S(2)}) copy-start(f32[128]{0:T(128)} %copy-done.129) | copy-start | bytes 1540
  678.5 94.2 %copy-start.134 = (f32[128]{0:T(128)S(1)}, f32[128]{0:T(128)}, u32[]{:S(2)}) copy-start(f32[128]{0:T(128)} %copy-done.133) | copy-start | bytes 1540
  681.2 110.6 %all-gather.29.cloned.1.call-start = ((), (), s32[]{:S(2)}) async-start(), calls=%async_computation.29 | async-start | bytes 1310720 | tf_op jit(solution)/shard_map/all_gather | solution.py:94
  712.0 60.7 %collective-permute-start.3 = (bf16[128,1024]{1,0:T(8,128)(2,1)}, bf16[128,1024]{1,0:T(8,128)(2,1)}, u32[]{:S(2)}, u32[]{:S(2)}) collective-permute-start(bf16[128,1024]{1,0:T(8,128)(2,1)} %get-tuple-element.283), channel_id=1, source_target_pairs={{16,0},{17,1},{18,2},{19,3},{20,4},{21,5},{22,6},{23,7},{24,8},{25... | collective-permute-start | bytes 786440 | tf_op jit(solution)/shard_map/ppermute | solution.py:25
  775.9 56.1 %reduce-scatter.32.cloned.1.call-start = ((), (), s32[]{:S(2)}) async-start(), calls=%async_computation.30 | async-start | bytes 2621440 | tf_op jit(solution)/shard_map/reduce_scatter | solution.py:98
  800.5 31.6 %copy-start.126 = (f32[128]{0:T(128)S(1)}, f32[128]{0:T(128)}, u32[]{:S(2)}) copy-start(f32[128]{0:T(128)} %copy-done.125) | copy-start | bytes 1540
  800.5 31.6 %copy-start.128 = (f32[128]{0:T(128)S(1)}, f32[128]{0:T(128)}, u32[]{:S(2)}) copy-start(f32[128]{0:T(128)} %copy-done.127) | copy-start | bytes 1540
  800.5 51.8 %all-gather.31.cloned.1.call-start = ((), (), s32[]{:S(2)}) async-start(), calls=%async_computation.31 | async-start | bytes 1310720 | tf_op jit(solution)/shard_map/all_gather | solution.py:94
  835.4 76.9 %reduce-scatter.34.cloned.1.call-start = ((), (), s32[]{:S(2)}) async-start(), calls=%async_computation.32 | async-start | bytes 2621440 | tf_op jit(solution)/shard_map/reduce_scatter | solution.py:98
  880.6 31.6 %copy-start.45 = (f32[128,1024]{1,0:T(8,128)S(1)}, f32[128,1024]{1,0:T(8,128)}, u32[]{:S(2)}) copy-start(f32[128,1024]{1,0:T(8,128)} %get-tuple-element.212) | copy-start | bytes 1572868
  880.6 35.5 %copy-start.8 = (f32[128,1024]{1,0:T(8,128)S(1)}, f32[128,1024]{1,0:T(8,128)}, u32[]{:S(2)}) copy-start(f32[128,1024]{1,0:T(8,128)} %get-tuple-element.209) | copy-start | bytes 1572868
  880.7 63.1 %all-gather.33.cloned.1.call-start = ((), (), s32[]{:S(2)}) async-start(), calls=%async_computation.33 | async-start | bytes 1310720 | tf_op jit(solution)/shard_map/all_gather | solution.py:94
  914.8 9.9 collective-permute-start.4
  927.8 56.3 %reduce-scatter.36.cloned.1.call-start = ((), (), s32[]{:S(2)}) async-start(), calls=%async_computation.34 | async-start | bytes 2621440 | tf_op jit(solution)/shard_map/reduce_scatter | solution.py:98
  952.5 60.6 %all-gather.35.cloned.1.call-start = ((), (), s32[]{:S(2)}) async-start(), calls=%async_computation.35 | async-start | bytes 1310720 | tf_op jit(solution)/shard_map/all_gather | solution.py:94
  987.6 110.5 %all-reduce.6.cloned.1.call-start = ((), (), s32[]{:S(2)}) async-start(), calls=%async_computation.37 | async-start | bytes 1048576 | tf_op jit(solution)/shard_map/psum | solution.py:503
  993.9 138.6 %reduce-scatter.38.cloned.1.call-start = ((), (), s32[]{:S(2)}) async-start(), calls=%async_computation.36 | async-start | bytes 2621440 | tf_op jit(solution)/shard_map/reduce_scatter | solution.py:98
  1043.4 523.6 %all-reduce.8.cloned.1.call-start = ((), (), s32[]{:S(2)}) async-start(), calls=%async_computation.39 | async-start | bytes 25165824 | tf_op jit(solution)/shard_map/psum | solution.py:487
  1070.6 30.2 %copy-start.150 = (f32[4,16]{1,0:T(4,128)S(1)}, f32[4,16]{1,0:T(4,128)}, u32[]{:S(2)}) copy-start(f32[4,16]{1,0:T(4,128)} %get-tuple-element.66) | copy-start | bytes 772
  1070.6 39.3 %copy-start.15 = (f32[512,4,64]{0,2,1:T(8,128)S(1)}, f32[512,4,64]{0,2,1:T(8,128)}, u32[]{:S(2)}) copy-start(f32[512,4,64]{0,2,1:T(8,128)} %copy-done.13) | copy-start | bytes 1572868
  1070.6 39.3 %copy-start.18 = (f32[512,4,64]{0,2,1:T(8,128)S(1)}, f32[512,4,64]{0,2,1:T(8,128)}, u32[]{:S(2)}) copy-start(f32[512,4,64]{0,2,1:T(8,128)} %copy-done.16) | copy-start | bytes 1572868
  1099.2 8.8 collective-permute-start.6
  1134.6 94.1 %collective-permute-start.5 = (f32[2,128,512]{2,1,0:T(8,128)}, f32[2,128,512]{2,1,0:T(8,128)}, u32[]{:S(2)}, u32[]{:S(2)}) collective-permute-start(f32[2,128,512]{2,1,0:T(8,128)} %pad_maximum_fusion.3), channel_id=1, source_target_pairs={{0,16},{16,0},{1,17},{17,1},{2,18},{18,2},{3,19},{19,3},{4,20},{20... | collective-permute-start | bytes 1572872 | tf_op jit(solution)/shard_map/ppermute | solution.py:35
  1210.4 17.8 %collective-permute-start.2 = (f32[16,2]{0,1:T(2,128)S(1)}, f32[16,2]{0,1:T(2,128)S(1)}, u32[]{:S(2)}, u32[]{:S(2)}) collective-permute-start(f32[16,2]{0,1:T(2,128)S(1)} %slice.269), channel_id=1, source_target_pairs={{0,16},{16,0},{1,17},{17,1},{2,18},{18,2},{3,19},{19,3},{4,20},{20... | collective-permute-start | bytes 392 | tf_op jit(solution)/shard_map/ppermute | solution.py:35
  (138 other events, 956.7 us)
Sparse Core Ops, SparseCore 0:
  10.2 19.4 all-gather.36
  46.1 31.4 reduce-scatter.13
  80.1 16.7 all-gather.14
  106.5 31.4 reduce-scatter.15
  150.2 17.6 all-gather.16
  190.7 31.4 reduce-scatter.17
  226.1 16.6 all-gather.18
  254.5 31.4 reduce-scatter.19
  300.8 17.7 all-gather.20
  350.6 31.4 reduce-scatter.21
  389.3 16.7 all-gather.22
  415.7 31.4 reduce-scatter.23
  573.2 16.0 all-gather.24
  598.1 31.4 reduce-scatter.25
  633.2 16.7 all-gather.26
  678.6 31.4 reduce-scatter.27
  713.5 57.4 reduce-scatter.29
  776.0 15.7 all-gather.28
  800.6 31.4 reduce-scatter.31
  835.5 16.7 all-gather.30
  880.8 31.4 reduce-scatter.33
  927.9 15.8 all-gather.32
  952.7 31.4 reduce-scatter.35
  987.7 16.7 all-gather.34
  1007.9 90.1 all-reduce.5
  1100.5 31.9 reduce-scatter.37
  1136.0 430.9 all-reduce.7
where the time goes:
time: 1600 us; the launch traced here: 1580 us
  waiting for transfers between devices  910 us (57%)
  matrix products  254 us (16%)
  blocking collectives  157 us (10%)
  local copies, waits for them, and re-layouts  126 us (8%)
  other arithmetic  86.4 us (5%)
  starting transfers between devices  26.6 us (2%)
  between operations  16.6 us (1%)
    psum x1, waiting for transfers between devices, on_device(): lax.psum((attend_totals[0], attend_totals[1], attend_totals[2], feed_tota...  337 us
    reduce_scatter x12, waiting for transfers between devices, tensor_reduce(): lax.psum_scatter(product_rows(jnp.int32(0), share_rows * lax.axis_size('t...  308 us
    all_gather x12, waiting for transfers between devices, tensor_rows(): return lax.all_gather(share, 'tensor', axis=0, tiled=True)  152 us
    psum x1, blocking collectives, on_device(): lax.psum((small_totals[0], small_totals[1], small_totals[2], proj_grad, s...  74.1 us
    reduce_scatter x1, waiting for transfers between devices, on_device(): lax.psum_scatter(doc_terms.reshape(tensor_count * groups * share_rows, PR...  57.7 us
    dot_general x12, matrix products, product_rows(): lax.dot_general(left, right, contraction, preferred_element_type=jnp.floa...  41.9 us
    all_gather x1, blocking collectives, on_device(): lax.all_gather(doc_units.astype(jnp.bfloat16), ('tensor', 'dp'), axis=0,...  35.7 us
    dynamic_update_slice x8, local copies, waits for them, and re-layouts, per_document(): lax.dynamic_update_slice_in_dim(doc_total, doc_term.reshape(tensor_count,...  34.8 us
  transfers between devices with their start and end apart: 34, of which 29 were waited for; matrix products, arithmetic and copies ran while one was open for 9% of the time, Pallas kernels for 0%

commit v1 on v0

v1 whole, which is shorter than its diff:
```python
import jax
import jax.numpy as jnp
import numpy as np
from jax import lax
from jax.sharding import PartitionSpec as P

HD = 64
QLEN = 32

norm_eps = 1e-05
unit_eps = 1e-06
softness_factor = 0.0625
rope_base = 10000.0
hidden_score = -1000000000.0
contract_rows = (((0,), (0,)), ((), ()))
contract_cols = (((1,), (1,)), ((), ()))
bf16 = jnp.bfloat16
f32 = jnp.float32


def dot(left, right, contraction=(((1,), (0,)), ((), ()))):
    return lax.dot_general(left, right, contraction, preferred_element_type=f32)


def flip(value, bit):
    count = lax.axis_size("tensor")
    return lax.ppermute(value, "tensor", [(i, i ^ (1 << bit)) for i in range(count)])


def chip_bits():
    return range(1, lax.axis_size("tensor").bit_length() - 1)


def core_other(value):
    return flip(value, 0)


def chips_gather(value, chip):
    for bit in chip_bits():
        other = flip(value, bit)
        upper = (chip >> (bit - 1)) % 2 == 1
        value = jnp.concatenate([jnp.where(upper, other, value), jnp.where(upper, value, other)], axis=0)
    return value


def chips_sum(value):
    for bit in chip_bits():
        low = value.astype(bf16)
        value = low.astype(f32) + flip(low, bit).astype(f32)
    return value


def to_section(value, pairs):
    return lax.ppermute(value, "section", pairs)


def rope_tables(positions):
    half = HD // 2
    frequency = np.power(np.float32(rope_base), (-2.0 * np.arange(half) / HD).astype(np.float32)).astype(np.float32)
    angles = (positions.astype(np.float32)[:, None] * frequency[None, :]).astype(np.float32)
    cosine, sine = np.cos(angles), np.sin(angles)
    return np.concatenate([cosine, cosine], 1).astype(np.float32), np.concatenate([-sine, sine], 1).astype(np.float32)


def halves_swapped(v):
    half = HD // 2
    return jnp.concatenate([v[..., half:], v[..., :half]], axis=-1)


def rotate(v, tables):
    return v * tables[0][:, None, :] + halves_swapped(v) * tables[1][:, None, :]


def rotate_back(v, tables):
    return v * tables[0][:, None, :] - halves_swapped(v) * tables[1][:, None, :]


def norm(values):
    centred = values - jnp.mean(values, axis=-1, keepdims=True)
    inverse = lax.rsqrt(jnp.mean(centred * centred, axis=-1, keepdims=True) + norm_eps)
    return centred * inverse, inverse


def norm_back(gradient, normed, inverse):
    return inverse * (
        gradient
        - jnp.mean(gradient, axis=-1, keepdims=True)
        - normed * jnp.mean(gradient * normed, axis=-1, keepdims=True)
    )


def gelu_slope(values):
    return 0.5 * (1.0 + lax.erf(values * 0.7071067811865476)) + values * jnp.exp(-0.5 * values * values) * 0.3989422804014327


def sum_over_tensor(rows_in, weight, contraction, half):
    other_part = dot(rows_in[half:], weight, contraction).astype(bf16)
    arrived = core_other(other_part)
    own_part = dot(rows_in[:half], weight, contraction) + arrived.astype(f32)
    return chips_sum(own_part)


def both_cores(rows):
    return jnp.concatenate([rows, core_other(rows)], axis=0)


def attend(h_all, w, seg_ids, tables):
    rows = h_all.shape[0]
    width = w["qkv"].shape[-1]
    shape = (rows, width // HD, HD)
    projected = dot(h_all, w["qkv"].reshape(h_all.shape[1], 3 * width)) + w["qkv_b"].reshape(3 * width)
    q = rotate(projected[:, :width].reshape(shape), tables).astype(bf16)
    k = rotate(projected[:, width : 2 * width].reshape(shape), tables).astype(bf16)
    v = projected[:, 2 * width :].reshape(shape).astype(bf16)
    scores = jnp.einsum("qhd,khd->hqk", q, k, preferred_element_type=f32) * HD ** (-0.5)
    allowed = seg_ids[:, None] == seg_ids[None, :]
    a = jax.nn.softmax(jnp.where(allowed[None], scores, hidden_score), axis=-1)
    a_low = a.astype(bf16)
    o = jnp.einsum("hqk,khd->qhd", a_low, v, preferred_element_type=f32).reshape(rows, width).astype(bf16)
    return q, k, v, a, a_low, o


def forward(h_own, w, seg_ids, tables):
    half = h_own.shape[0]
    h_all = both_cores(h_own)
    heads = attend(h_all, w, seg_ids, tables)
    s1 = h_own.astype(f32) + sum_over_tensor(heads[5], w["out"], (((1,), (0,)), ((), ())), half) + w["out_b"][0]
    n1, r1 = norm(s1)
    h1 = n1 * w["gain"][0] + w["shift"][0]
    h1_all = both_cores(h1.astype(bf16))
    u = dot(h1_all, w["up"]) + w["up_b"]
    g = jax.nn.gelu(u, approximate=False).astype(bf16)
    s2 = h1 + sum_over_tensor(g, w["down"], (((1,), (0,)), ((), ())), half) + w["out_b"][1]
    n2, r2 = norm(s2)
    y = n2 * w["gain"][1] + w["shift"][1]
    return y, (h_all, heads, n1, r1, h1_all, u, g, n2, r2)


def backward(dy, w, tables, record):
    h_all, (q, k, v, a, a_low, o), n1, r1, h1_all, u, g, n2, r2 = record
    half = dy.shape[0]
    rows, width = o.shape
    shape = (rows, width // HD, HD)
    gain2, shift2 = jnp.sum(dy * n2, axis=0), jnp.sum(dy, axis=0)
    ds2 = norm_back(dy * w["gain"][1], n2, r2)
    bias2 = jnp.sum(ds2, axis=0)
    f_all = both_cores(ds2.astype(bf16))
    du = dot(f_all, w["down"], contract_cols) * gelu_slope(u)
    u_low = du.astype(bf16)
    dh1 = ds2 + sum_over_tensor(u_low, w["up"], contract_cols, half)
    d_down = dot(g, f_all, contract_rows)
    d_up = dot(h1_all, u_low, contract_rows)
    d_up_b = jnp.sum(du, axis=0)
    gain1, shift1 = jnp.sum(dh1 * n1, axis=0), jnp.sum(dh1, axis=0)
    ds1 = norm_back(dh1 * w["gain"][0], n1, r1)
    bias1 = jnp.sum(ds1, axis=0)
    o_all = both_cores(ds1.astype(bf16))
    do = dot(o_all, w["out"], contract_cols).astype(bf16).reshape(shape)
    d_out = dot(o, o_all, contract_rows)
    da = jnp.einsum("qhd,khd->hqk", do, v, preferred_element_type=f32)
    dv = jnp.einsum("hqk,qhd->khd", a_low, do, preferred_element_type=f32)
    ds = a * (da - jnp.sum(da * a, axis=-1, keepdims=True))
    ds = ds.astype(bf16) * jnp.asarray(HD ** (-0.5), bf16)
    dq = rotate_back(jnp.einsum("hqk,khd->qhd", ds, k, preferred_element_type=f32), tables)
    dk = rotate_back(jnp.einsum("hqk,qhd->khd", ds, q, preferred_element_type=f32), tables)
    dp = jnp.concatenate([part.reshape(rows, width) for part in (dq, dk, dv)], axis=1)
    d_qkv_b = jnp.sum(dp, axis=0)
    dp_low = dp.astype(bf16)
    dh = ds1 + sum_over_tensor(dp_low, w["qkv"].reshape(w["qkv"].shape[0], 3 * width), contract_cols, half)
    d_qkv = dot(h_all, dp_low, contract_rows)
    return dh, (d_down, d_up, d_out, d_qkv), (d_up_b, d_qkv_b), jnp.stack([bias1, bias2, gain1, gain2, shift1, shift2])


def on_device(tokens, segment, score_grad, qkv_weight, qkv_bias, out_weight, up_weight, up_bias, down_weight, out_bias, norm_gain, norm_shift, proj_weight):
    w = dict(
        qkv=qkv_weight[0], qkv_b=qkv_bias[0].astype(f32), out=out_weight[0], up=up_weight[0], up_b=up_bias[0].astype(f32),
        down=down_weight[0], out_b=out_bias[0].astype(f32), gain=norm_gain[0].astype(f32), shift=norm_shift[0].astype(f32),
    )
    first = lax.axis_index("section") == 0
    device = lax.axis_index("tensor")
    core, chip = device % 2, device // 2
    blocks, share, model = tokens.shape
    chips = lax.axis_size("tensor") // 2
    groups = lax.axis_size("dp")
    half = share * chips
    rows = 2 * half
    proj = proj_weight.shape[1]

    def own_first(by_token):
        parts = by_token.reshape((chips, 2, share) + by_token.shape[1:])
        even = parts[:, 0].reshape((half,) + by_token.shape[1:])
        odd = parts[:, 1].reshape((half,) + by_token.shape[1:])
        return jnp.concatenate([jnp.where(core == 0, even, odd), jnp.where(core == 0, odd, even)], axis=0)

    index = np.arange(rows)
    tables = [tuple(own_first(jnp.asarray(part)) for part in rope_tables(p)) for p in (index, index % QLEN)]
    segments = [own_first(segment[b]) for b in range(2)]
    entering = [chips_gather(tokens[b], chip) for b in range(2)]

    def pick(zero, one):
        return (
            jnp.where(first, segments[zero], segments[one]),
            tuple(jnp.where(first, x, y) for x, y in zip(tables[zero], tables[one])),
        )

    contexts = [pick(0, 0), pick(1, 0), pick(1, 1)]
    received = jnp.zeros((half, model), bf16)
    records, outputs = [], []
    for tick in range(3):
        h_own = jnp.where(first, entering[min(tick, 1)], received)
        y, record = forward(h_own, w, *contexts[tick])
        records.append(record)
        outputs.append(y)
        if tick < 2:
            received = to_section(y.astype(bf16), [(0, 1)])

    def embed(y):
        low = y.astype(bf16)
        z = dot(low, proj_weight)
        inverse = lax.rsqrt(jnp.sum(z * z, axis=-1, keepdims=True) + unit_eps)
        return low, inverse, z * inverse

    def embed_back(low, inverse, units, gradient):
        dz = (inverse * (gradient - units * jnp.sum(gradient * units, axis=-1, keepdims=True))).astype(bf16)
        return dot(dz, proj_weight, contract_cols), dot(low, dz, contract_rows)

    doc = embed(outputs[1])
    query = embed(outputs[2])
    units_own = lax.all_gather(doc[2].astype(bf16), "dp", axis=0)
    units = jnp.stack([units_own, core_other(units_own)], axis=1).reshape(groups * rows, proj)
    alive_all = lax.all_gather((segments[0] == 0).astype(f32), "dp", axis=0).reshape(1, groups * rows)
    slots = score_grad.shape[0]
    member = (segments[1][:half, None] == jnp.arange(slots)[None, :]).astype(f32)
    token_grad = jnp.dot(member, score_grad, precision=lax.Precision.HIGHEST)
    query_low = query[2].astype(bf16)
    logits = jnp.where(alive_all > 0, dot(query_low, units, contract_cols) / softness_factor, hidden_score)
    logits = logits.reshape(half, groups, rows)
    peak = jnp.max(logits, axis=-1, keepdims=True)
    exps = jnp.exp(logits - peak)
    total = jnp.sum(exps, axis=-1, keepdims=True)
    smooth = softness_factor * (peak + jnp.log(total))[:, :, 0]
    board = lax.dot_general(member, smooth, contract_rows, precision=lax.Precision.HIGHEST, preferred_element_type=f32)
    pull = (exps / total * token_grad[:, :, None]).astype(bf16).reshape(half, groups * rows)
    query_grad = dot(pull, units)
    doc_terms = dot(pull, query_low, contract_rows).reshape(groups, 2, half, proj)
    doc_terms = doc_terms[:, 0] + core_other(doc_terms[:, 1])
    doc_grad = lax.psum_scatter(doc_terms, "dp", scatter_dimension=0)
    doc_back, doc_proj = embed_back(*doc, doc_grad)
    query_back, query_proj = embed_back(*query, query_grad)
    proj_grad = doc_proj + query_proj
    own = (query_back, doc_back, jnp.zeros_like(doc_back))
    received = jnp.zeros((half, model), bf16)
    totals, biases, small = None, None, None
    input_grads = [None, None]
    for step in range(3):
        dy = jnp.where(first, received.astype(f32), own[step])
        dh, weights, bias, vectors = backward(dy, w, contexts[2 - step][1], records[2 - step])
        totals = weights if totals is None else [p + q for p, q in zip(totals, weights)]
        biases = bias if biases is None else [p + q for p, q in zip(biases, bias)]
        small = vectors if small is None else small + vectors
        if step < 2:
            received = to_section(dh.astype(bf16), [(1, 0)])
        if step >= 1:
            input_grads[2 - step] = lax.dynamic_slice_in_dim(dh, chip * share, share, 0)
    totals = [lax.psum(part.astype(bf16), "dp").astype(f32) for part in totals]
    small = small + core_other(small)
    proj_grad = proj_grad + core_other(proj_grad)
    board = board + core_other(board)
    d_up_b, d_qkv_b, small, proj_grad = lax.psum((biases[0], biases[1], small, proj_grad), "dp")
    stack = jnp.stack(input_grads)
    swap = [(0, 1), (1, 0)]
    mid, docs = model // 2, groups // 2
    sent_input = to_section(stack[:, :, mid:], swap)
    sent_board, sent_proj = to_section((board[:, :docs], proj_grad[:mid]), swap)
    d_down, d_up, d_out, d_qkv = totals
    width = qkv_weight.shape[-1]
    return (
        jnp.where(first, sent_board, board[:, docs:]),
        jnp.where(first, stack[:, :, :mid], sent_input),
        d_qkv.reshape(1, model, 3, width),
        d_qkv_b.reshape(1, 3, width),
        d_out[None],
        d_up[None],
        d_up_b[None],
        d_down[None],
        small[0:2][None],
        small[2:4][None],
        small[4:6][None],
        jnp.where(first, sent_proj, proj_grad[mid:]),
    )


def solution(mesh):
    return jax.shard_map(
        on_device,
        mesh=mesh,
        in_specs=(
            P("dp", "tensor", None),
            P("dp", None),
            P("dp", None),
            P("section", None, None, "tensor"),
            P("section", None, "tensor"),
            P("section", "tensor", None),
            P("section", None, "tensor"),
            P("section", "tensor"),
            P("section", "tensor", None),
            P("section", None, None),
            P("section", None, None),
            P("section", None, None),
            P(),
        ),
        out_specs=(
            P("dp", "section"),
            P("dp", "tensor", "section"),
            P("section", None, None, "tensor"),
            P("section", None, "tensor"),
            P("section", "tensor", None),
            P("section", None, "tensor"),
            P("section", "tensor"),
            P("section", "tensor", None),
            P("section", None, None),
            P("section", None, None),
            P("section", None, None),
            P("section", None),
        ),
        check_vma=False,
    )
```

time: 1600 us -> 804 us (0.50)
  waiting for transfers between devices: 910 us -> 363 us
  blocking collectives: 157 us -> 52.6 us
  matrix products: 254 us -> 183 us
  local copies, waits for them, and re-layouts: 126 us -> 76.6 us
  other arithmetic: 86.4 us -> 67 us
    reduce_scatter x13 -> x1, waiting for transfers between devices: 366 us -> 1.75 us  [on_device(): doc_grad = lax.psum_scatter(doc_terms, 'dp', scatter_dimension=0)]
    psum x2, waiting for transfers between devices: 365 us -> 160 us  [the longest x1 160 us: on_device(): totals = [lax.psum(part.astype(bf16), 'dp').astype(f32) for part in totals]]
    ppermute x7 -> x50, waiting for transfers between devices: 26.7 us -> 201 us  [the longest x43 157 us: flip(): lax.ppermute(value, 'tensor', [(i, i ^ 1 << bit) for i in range(count)])]
    all_gather x12 -> x0, waiting for transfers between devices: 152 us -> none  [tensor_rows(): return lax.all_gather(share, 'tensor', axis=0, tiled=True)]
    psum x2 -> x1, blocking collectives: 90.3 us -> 25.7 us  [on_device(): lax.psum((biases[0], biases[1], small, proj_grad), 'dp')]
    dot_general x74, matrix products: 228 us -> 168 us  [the longest x57 96.3 us: dot(): return lax.dot_general(left, right, contraction, preferred_element_type=f32)]
    all_gather x2, blocking collectives: 67.1 us -> 27 us  [the longest x1 14.2 us: on_device(): units_own = lax.all_gather(doc[2].astype(bf16), 'dp', axis=0)]
    dynamic_update_slice x13 -> x0, local copies, waits for them, and re-layouts: 40 us -> none  [the longest x8 34.8 us: per_document(): lax.dynamic_update_slice_in_dim(doc_total, doc_term.reshape(tensor_count,...]
  transfers between devices with their start and end apart: 34 -> 53, of which waited for: 29 -> 40; matrix products, arithmetic and copies ran while one was open for 9% -> 18% of each run, Pallas kernels for 0% -> 0%
where the time goes in v1:
time: 804 us; the launch traced here: 795 us
  waiting for transfers between devices  363 us (45%)
  matrix products  183 us (23%)
  local copies, waits for them, and re-layouts  76.6 us (10%)
  other arithmetic  67 us (8%)
  blocking collectives  52.6 us (7%)
  starting transfers between devices  34.7 us (4%)
  between operations  17.5 us (2%)
    psum x1, waiting for transfers between devices, on_device(): totals = [lax.psum(part.astype(bf16), 'dp').astype(f32) for part in totals]  160 us
    ppermute x43, waiting for transfers between devices, flip(): lax.ppermute(value, 'tensor', [(i, i ^ 1 << bit) for i in range(count)])  157 us
    dot_general x57, matrix products, dot(): return lax.dot_general(left, right, contraction, preferred_element_type=f32)  96.3 us
    ppermute x7, waiting for transfers between devices, to_section(): return lax.ppermute(value, 'section', pairs)  44.3 us
    unnamed x517, local copies, waits for them, and re-layouts  25.9 us
    psum x1, blocking collectives, on_device(): lax.psum((biases[0], biases[1], small, proj_grad), 'dp')  25.7 us
    dot_general x3, matrix products, backward(): jnp.einsum('hqk,qhd->khd', ds, q, preferred_element_type=f32)  25.2 us
    dot_general x3, matrix products, backward(): jnp.einsum('hqk,khd->qhd', ds, k, preferred_element_type=f32)  25.2 us
  transfers between devices with their start and end apart: 53, of which 40 were waited for; matrix products, arithmetic and copies ran while one was open for 18% of the time, Pallas kernels for 0%

profile of v1, /device:TPU:0, one launch (start us, length us, event | category | flops | bytes accessed | tf_op | source)
XLA Modules:
  0.0 794.7 jit_solution(6561071212809449830)
XLA Ops:
  9.1 2.9 collective-permute-start
  16.6 2.6 copy.101
  19.4 4.9 collective-permute-done.1
  38.4 4.8 fusion.435
  43.2 2.8 convolution_convert_fusion.11
  50.6 12.2 %collective-permute-done.4 = bf16[256,1024]{1,0:T(8,128)(2,1)S(1)} collective-permute-done((bf16[256,1024]{1,0:T(8,128)(2,1)S(1)}, bf16[256,1024]{1,0:T(8,128)(2,1)S(1)}, u32[]{:S(2)}, u32[]{:S(2)}) %collective-permute-start.4) | collective-permute-done | bytes 524320 | tf_op jit(solution)/shard_map/ppermute | solution.py:27
  65.7 6.9 fusion.21
  77.9 12.2 %collective-permute-done.7 = bf16[256,1024]{1,0:T(8,128)(2,1)S(1)} collective-permute-done((bf16[256,1024]{1,0:T(8,128)(2,1)S(1)}, bf16[256,1024]{1,0:T(8,128)(2,1)S(1)}, u32[]{:S(2)}, u32[]{:S(2)}) %collective-permute-start.7) | collective-permute-done | bytes 524320 | tf_op jit(solution)/shard_map/ppermute | solution.py:27
  91.3 4.0 collective-permute-start.8
  95.3 10.4 %collective-permute-done.8 = bf16[256,1024]{1,0:T(8,128)(2,1)S(1)} collective-permute-done((bf16[256,1024]{1,0:T(8,128)(2,1)S(1)}, bf16[256,1024]{1,0:T(8,128)(2,1)S(1)}, u32[]{:S(2)}, u32[]{:S(2)}) %collective-permute-start.8) | collective-permute-done | bytes 524320 | tf_op jit(solution)/shard_map/ppermute | solution.py:54
  118.2 4.8 fusion.436
  123.0 2.7 convolution_convert_fusion.10
  130.6 12.6 %collective-permute-done.11 = bf16[256,1024]{1,0:T(8,128)(2,1)S(1)} collective-permute-done((bf16[256,1024]{1,0:T(8,128)(2,1)S(1)}, bf16[256,1024]{1,0:T(8,128)(2,1)S(1)}, u32[]{:S(2)}, u32[]{:S(2)}) %collective-permute-start.11) | collective-permute-done | bytes 524320 | tf_op jit(solution)/shard_map/ppermute | solution.py:27
  146.2 6.9 fusion.24
  158.1 12.5 %collective-permute-done.14 = bf16[256,1024]{1,0:T(8,128)(2,1)S(1)} collective-permute-done((bf16[256,1024]{1,0:T(8,128)(2,1)S(1)}, bf16[256,1024]{1,0:T(8,128)(2,1)S(1)}, u32[]{:S(2)}, u32[]{:S(2)}) %collective-permute-start.14) | collective-permute-done | bytes 524320 | tf_op jit(solution)/shard_map/ppermute | solution.py:27
  171.7 5.0 collective-permute-start.15
  176.7 10.2 %collective-permute-done.15 = bf16[256,1024]{1,0:T(8,128)(2,1)S(1)} collective-permute-done((bf16[256,1024]{1,0:T(8,128)(2,1)S(1)}, bf16[256,1024]{1,0:T(8,128)(2,1)S(1)}, u32[]{:S(2)}, u32[]{:S(2)}) %collective-permute-start.15) | collective-permute-done | bytes 524320 | tf_op jit(solution)/shard_map/ppermute | solution.py:54
  201.3 4.9 fusion.437
  206.7 2.7 convolution_convert_fusion.9
  213.7 12.5 %collective-permute-done.18 = bf16[256,1024]{1,0:T(8,128)(2,1)S(1)} collective-permute-done((bf16[256,1024]{1,0:T(8,128)(2,1)S(1)}, bf16[256,1024]{1,0:T(8,128)(2,1)S(1)}, u32[]{:S(2)}, u32[]{:S(2)}) %collective-permute-start.18) | collective-permute-done | bytes 524320 | tf_op jit(solution)/shard_map/ppermute | solution.py:27
  227.9 12.7 %all-gather.1 = f32[4,1,512]{2,1,0:T(1,128)} all-gather(f32[1,1,512]{2,1,0:T(1,128)S(1)} %fusion.353), channel_id=1, replica_groups=mesh['section'=2,'tensor'=4,'dp'=4] {'dp'}, dimensions={0}, use_global_device_ids=true | all-gather | bytes 10240 | tf_op jit(solution)/shard_map/all_gather | solution.py:231
  240.6 7.0 fusion.27
  253.4 14.2 %all-gather = bf16[1024,128]{0,1:T(8,128)(2,1)S(1)} all-gather(bf16[256,128]{0,1:T(8,128)(2,1)S(1)} %multiply_convert_fusion.5), channel_id=2, replica_groups=mesh['section'=2,'tensor'=4,'dp'=4] {'dp'}, dimensions={0}, use_global_device_ids=true | all-gather | bytes 327680 | tf_op jit(solution)/shard_map/all_gather | solution.py:229
  279.7 3.8 reshape.630
  285.5 2.7 exponential_reduce_fusion
  300.1 3.3 fusion.411
  308.3 2.6 copy.149
  310.9 11.3 %collective-permute-done.27 = bf16[256,1024]{1,0:T(8,128)(2,1)} collective-permute-done((bf16[256,1024]{1,0:T(8,128)(2,1)}, bf16[256,1024]{1,0:T(8,128)(2,1)}, u32[]{:S(2)}, u32[]{:S(2)}) %collective-permute-start.27) | collective-permute-done | bytes 524320 | tf_op jit(solution)/shard_map/ppermute | solution.py:27
  322.2 3.1 multiply_reduce_fusion.8
  331.5 2.8 fusion.438
  334.3 8.9 %fusion.173 = f32[512,4,64]{0,2,1:T(8,128)} fusion(bf16[512,4,64]{0,2,1:T(8,128)(2,1)} %get-tuple-element.125, f32[4,512,512]{1,2,0:T(8,128)} %fusion.438, f32[4,512,512]{1,2,0:T(8,128)} %get-tuple-element.168, f32[4,512]{1,0:T(4,128)S(1)} %copy-done.254), kind=kOutput, calls=%fused_computation.190 | convolution fusion | flops 144706048 | bytes 9183232 | tf_op jit(solution)/shard_map/hqk,khd->qhd/dot_general | solution.py:164
  343.2 8.6 %fusion.178 = f32[512,4,64]{0,2,1:T(8,128)} fusion(bf16[512,4,64]{0,2,1:T(8,128)(2,1)} %get-tuple-element.126, f32[4,512,512]{1,2,0:T(8,128)} %fusion.438, f32[4,512,512]{1,2,0:T(8,128)} %get-tuple-element.168, f32[4,512]{1,0:T(4,128)S(1)} %copy-done.254), kind=kOutput, calls=%fused_computation.191 | convolution fusion | flops 144706048 | bytes 9183232 | tf_op jit(solution)/shard_map/hqk,qhd->khd/dot_general | solution.py:165
  362.7 13.6 %collective-permute-done.30 = bf16[256,1024]{1,0:T(8,128)(2,1)S(1)} collective-permute-done((bf16[256,1024]{1,0:T(8,128)(2,1)S(1)}, bf16[256,1024]{1,0:T(8,128)(2,1)S(1)}, u32[]{:S(2)}, u32[]{:S(2)}) %collective-permute-start.30) | collective-permute-done | bytes 524320 | tf_op jit(solution)/shard_map/ppermute | solution.py:27
  382.3 10.7 %collective-permute-done.31 = bf16[256,1024]{1,0:T(8,128)(2,1)} collective-permute-done((bf16[256,1024]{1,0:T(8,128)(2,1)}, bf16[256,1024]{1,0:T(8,128)(2,1)}, u32[]{:S(2)}, u32[]{:S(2)}) %collective-permute-start.31) | collective-permute-done | bytes 524320 | tf_op jit(solution)/shard_map/ppermute | solution.py:54
  393.0 2.7 multiply_reduce_fusion.5
  398.2 3.3 fusion.410
  405.8 13.4 %collective-permute-done.35 = bf16[256,1024]{1,0:T(8,128)(2,1)S(1)} collective-permute-done((bf16[256,1024]{1,0:T(8,128)(2,1)S(1)}, bf16[256,1024]{1,0:T(8,128)(2,1)S(1)}, u32[]{:S(2)}, u32[]{:S(2)}) %collective-permute-start.35) | collective-permute-done | bytes 524320 | tf_op jit(solution)/shard_map/ppermute | solution.py:27
  424.7 2.8 fusion.439
  427.4 7.7 fusion.183
  435.2 8.3 %fusion.188 = f32[512,4,64]{0,2,1:T(8,128)} fusion(bf16[512,4,64]{0,2,1:T(8,128)(2,1)} %get-tuple-element.130, f32[4,512,512]{1,2,0:T(8,128)} %fusion.439, f32[4,512,512]{1,2,0:T(8,128)} %get-tuple-element.162, f32[4,512]{1,0:T(4,128)S(1)} %copy-done.252), kind=kOutput, calls=%fused_computation.193 | convolution fusion | flops 144706048 | bytes 9183232 | tf_op jit(solution)/shard_map/hqk,qhd->khd/dot_general | solution.py:165
  450.3 3.3 fusion.238
  454.5 9.3 %collective-permute-done.38 = bf16[256,1024]{1,0:T(8,128)(2,1)S(1)} collective-permute-done((bf16[256,1024]{1,0:T(8,128)(2,1)S(1)}, bf16[256,1024]{1,0:T(8,128)(2,1)S(1)}, u32[]{:S(2)}, u32[]{:S(2)}) %collective-permute-start.38) | collective-permute-done | bytes 524320 | tf_op jit(solution)/shard_map/ppermute | solution.py:27
  466.5 3.3 fusion.237
  470.8 4.2 fusion.239
  474.9 5.6 collective-permute-done.39
  488.8 3.2 fusion.412
  494.7 2.7 fusion.241
  498.8 2.7 fusion.44
  501.4 11.1 %collective-permute-done.42 = bf16[256,1024]{1,0:T(8,128)(2,1)S(1)} collective-permute-done((bf16[256,1024]{1,0:T(8,128)(2,1)S(1)}, bf16[256,1024]{1,0:T(8,128)(2,1)S(1)}, u32[]{:S(2)}, u32[]{:S(2)}) %collective-permute-start.42) | collective-permute-done | bytes 524320 | tf_op jit(solution)/shard_map/ppermute | solution.py:27
  516.2 2.7 fusion.43
  521.1 2.8 fusion.440
  523.9 8.5 %fusion.193 = f32[512,4,64]{0,2,1:T(8,128)} fusion(bf16[512,4,64]{0,2,1:T(8,128)(2,1)} %get-tuple-element.133, f32[4,512,512]{1,2,0:T(8,128)} %fusion.440, f32[4,512,512]{1,2,0:T(8,128)} %get-tuple-element.158, f32[4,512]{1,0:T(4,128)S(1)} %copy-done.250), kind=kOutput, calls=%fused_computation.194 | convolution fusion | flops 144706048 | bytes 9183232 | tf_op jit(solution)/shard_map/hqk,khd->qhd/dot_general | solution.py:164
  532.4 8.3 %fusion.198 = f32[512,4,64]{0,2,1:T(8,128)} fusion(bf16[512,4,64]{0,2,1:T(8,128)(2,1)} %get-tuple-element.134, f32[4,512,512]{1,2,0:T(8,128)} %fusion.440, f32[4,512,512]{1,2,0:T(8,128)} %get-tuple-element.158, f32[4,512]{1,0:T(4,128)} %copy-done.249), kind=kOutput, calls=%fused_computation.195 | convolution fusion | flops 144706048 | bytes 9183232 | tf_op jit(solution)/shard_map/hqk,qhd->khd/dot_general | solution.py:165
  545.8 3.7 add_convert_fusion.2
  549.6 2.6 copy.130
  555.5 3.0 convolution_convert_fusion.3
  560.4 3.6 collective-permute-done.24
  567.3 3.1 add_convert_fusion.3
  571.0 3.9 collective-permute-done.49
  579.4 4.6 collective-permute-done.45
  589.7 25.7 %all-reduce = (f32[1,3,256]{2,0,1:T(1,128)}, f32[1,1024]{1,0:T(1,128)}, f32[6,1024]{1,0:T(8,128)S(1)}) all-reduce(f32[1,3,256]{2,0,1:T(1,128)S(1)} %reshape.645, f32[1,1024]{1,0:T(1,128)S(1)} %bitcast.496, f32[6,1024]{1,0:T(8,128)S(1)} %add.541), channel_id=1, replica_groups=mesh['section'=2,'tensor'=4,'dp'=4] {'dp'}, use_global_device_ids=true, to_apply=%region_44.45 | all-reduce | flops 7936 | bytes 63488 | tf_op jit(solution)/shard_map/psum | solution.py:269
  617.9 160.2 %all-reduce.7.cloned.1.call-done = (bf16[1,1024,3,256]{3,1,2,0:T(8,128)(2,1)}, bf16[1,256,1024]{2,1,0:T(8,128)(2,1)}, bf16[1,1024,1024]{2,1,0:T(8,128)(2,1)}, bf16[1,1024,1024]{2,1,0:T(8,128)(2,1)}) async-done(((bf16[1,1024,3,256]{3,1,2,0:T(8,128)(2,1)}, bf16[1,256,1024]{2,1,0:T(8,128)(2,1)}, bf16[1,1024,1024]{2,1,0:T(8,128)(2,1)}, bf16[1,1024,1024]{2,1,0:T(8,128)(2,1)}), ...) | async-done | bytes 6291472 | tf_op jit(solution)/shard_map/psum | solution.py:265
  782.7 2.5 broadcast_in_dim.68
  785.2 2.5 broadcast_in_dim.71
  (808 shorter events, 212.0 us)
Async XLA Ops:
  7.2 58.5 %copy-start = (bf16[1,1024,1024]{2,1,0:T(8,128)(2,1)S(1)}, bf16[1,1024,1024]{2,1,0:T(8,128)(2,1)}, u32[]{:S(2)}) copy-start(bf16[1,1024,1024]{2,1,0:T(8,128)(2,1)} %param.23) | copy-start | bytes 6291460
  7.2 373.1 %reduce-scatter.2.cloned.1.call-start = ((), (), s32[]{:S(2)}) async-start(), calls=%async_computation.1 | async-start | bytes 655360 | tf_op jit(solution)/shard_map/reduce_scatter | solution.py:247
  9.1 10.3 %collective-permute-start = (bf16[128,1024]{1,0:T(8,128)(2,1)}, bf16[128,1024]{1,0:T(8,128)(2,1)S(1)}, u32[]{:S(2)}, u32[]{:S(2)}) collective-permute-start(bf16[128,1024]{1,0:T(8,128)(2,1)} %get-tuple-element.111), channel_id=1, source_target_pairs={{0,8},{4,12},{8,0},{12,4},{1,9},{5,13},{9,1},{13,5},{2,10},{6,14},... | collective-permute-start | bytes 786440 | tf_op jit(solution)/shard_map/ppermute | solution.py:27
  12.1 12.2 %collective-permute-start.1 = (bf16[128,1024]{1,0:T(8,128)(2,1)S(1)}, bf16[128,1024]{1,0:T(8,128)(2,1)}, u32[]{:S(2)}, u32[]{:S(2)}) collective-permute-start(bf16[128,1024]{1,0:T(8,128)(2,1)S(1)} %get-tuple-element.112), channel_id=1, source_target_pairs={{0,8},{4,12},{8,0},{12,4},{1,9},{5,13},{9,1},{13,5},{2,10},{6,14},... | collective-permute-start | bytes 786440 | tf_op jit(solution)/shard_map/ppermute | solution.py:27
  26.2 36.6 %copy-start.35 = (bf16[256,1024]{1,0:T(8,128)(2,1)}, bf16[256,1024]{1,0:T(8,128)(2,1)S(1)}, u32[]{:S(2)}) copy-start(bf16[256,1024]{1,0:T(8,128)(2,1)S(1)} %maximum_select_fusion) | copy-start | bytes 1572868
  26.2 2.0 collective-permute-start.2
  26.9 80.0 %copy-start.89 = (f32[512,64]{0,1:T(8,128)}, f32[512,64]{0,1:T(8,128)S(1)}, u32[]{:S(2)}) copy-start(f32[512,64]{0,1:T(8,128)S(1)} %bitcast_dynamic-update-slice_fusion) | copy-start | bytes 393220
  46.4 2.0 collective-permute-start.3
  48.7 14.1 %collective-permute-start.4 = (bf16[256,1024]{1,0:T(8,128)(2,1)S(1)}, bf16[256,1024]{1,0:T(8,128)(2,1)S(1)}, u32[]{:S(2)}, u32[]{:S(2)}) collective-permute-start(bf16[256,1024]{1,0:T(8,128)(2,1)S(1)} %add_convert_fusion.18), channel_id=1, source_target_pairs={{0,8},{4,12},{8,0},{12,4},{1,9},{5,13},{9,1},{13,5},{2,10},{6,14},... | collective-permute-start | bytes 1572872 | tf_op jit(solution)/shard_map/ppermute | solution.py:27
  50.5 39.5 %copy-start.155 = (f32[1,1,1024]{2,1,0:T(1,128)}, f32[1,1,1024]{2,1,0:T(1,128)S(1)}, u32[]{:S(2)}) copy-start(f32[1,1,1024]{2,1,0:T(1,128)S(1)} %get-tuple-element.149) | copy-start | bytes 12292
  63.1 27.0 %copy-start.1 = (f32[256,1024]{1,0:T(8,128)}, f32[256,1024]{1,0:T(8,128)S(1)}, u32[]{:S(2)}) copy-start(f32[256,1024]{1,0:T(8,128)S(1)} %get-tuple-element.72) | copy-start | bytes 3145732
  63.1 27.0 %copy-start.161 = (f32[256]{0:T(256)}, f32[256]{0:T(256)S(1)}, u32[]{:S(2)}) copy-start(f32[256]{0:T(256)S(1)} %broadcast_multiply_fusion.17) | copy-start | bytes 3076
  63.4 26.7 %copy-start.168 = (f32[256]{0:T(256)}, f32[256]{0:T(256)S(1)}, u32[]{:S(2)}) copy-start(f32[256]{0:T(256)S(1)} %add_rsqrt_fusion.7) | copy-start | bytes 3076
  63.7 2.0 collective-permute-start.5
  73.3 2.0 collective-permute-start.6
  76.1 14.0 %collective-permute-start.7 = (bf16[256,1024]{1,0:T(8,128)(2,1)S(1)}, bf16[256,1024]{1,0:T(8,128)(2,1)S(1)}, u32[]{:S(2)}, u32[]{:S(2)}) collective-permute-start(bf16[256,1024]{1,0:T(8,128)(2,1)S(1)} %add_convert_fusion.17), channel_id=1, source_target_pairs={{0,8},{4,12},{8,0},{12,4},{1,9},{5,13},{9,1},{13,5},{2,10},{6,14},... | collective-permute-start | bytes 1572872 | tf_op jit(solution)/shard_map/ppermute | solution.py:27
  91.3 14.4 %collective-permute-start.8 = (bf16[256,1024]{1,0:T(8,128)(2,1)S(1)}, bf16[256,1024]{1,0:T(8,128)(2,1)S(1)}, u32[]{:S(2)}, u32[]{:S(2)}) collective-permute-start(bf16[256,1024]{1,0:T(8,128)(2,1)S(1)} %add_convert_fusion.16), channel_id=1, source_target_pairs={{0,16},{1,17},{2,18},{3,19},{4,20},{5,21},{6,22},{7,23},{8,24},{9,... | collective-permute-start | bytes 1572872 | tf_op jit(solution)/shard_map/ppermute | solution.py:54
  106.0 2.0 collective-permute-start.9
  126.8 2.0 collective-permute-start.10
  129.1 14.2 %collective-permute-start.11 = (bf16[256,1024]{1,0:T(8,128)(2,1)S(1)}, bf16[256,1024]{1,0:T(8,128)(2,1)S(1)}, u32[]{:S(2)}, u32[]{:S(2)}) collective-permute-start(bf16[256,1024]{1,0:T(8,128)(2,1)S(1)} %add_convert_fusion.15), channel_id=1, source_target_pairs={{0,8},{4,12},{8,0},{12,4},{1,9},{5,13},{9,1},{13,5},{2,10},{6,14},... | collective-permute-start | bytes 1572872 | tf_op jit(solution)/shard_map/ppermute | solution.py:27
  143.6 27.0 %copy-start.163 = (f32[256]{0:T(256)}, f32[256]{0:T(256)S(1)}, u32[]{:S(2)}) copy-start(f32[256]{0:T(256)S(1)} %broadcast_multiply_fusion.15) | copy-start | bytes 3076
  144.2 2.0 collective-permute-start.12
  153.8 2.0 collective-permute-start.13
  156.5 14.0 %collective-permute-start.14 = (bf16[256,1024]{1,0:T(8,128)(2,1)S(1)}, bf16[256,1024]{1,0:T(8,128)(2,1)S(1)}, u32[]{:S(2)}, u32[]{:S(2)}) collective-permute-start(bf16[256,1024]{1,0:T(8,128)(2,1)S(1)} %add_convert_fusion.14), channel_id=1, source_target_pairs={{0,8},{4,12},{8,0},{12,4},{1,9},{5,13},{9,1},{13,5},{2,10},{6,14},... | collective-permute-start | bytes 1572872 | tf_op jit(solution)/shard_map/ppermute | solution.py:27
  171.7 15.2 %collective-permute-start.15 = (bf16[256,1024]{1,0:T(8,128)(2,1)S(1)}, bf16[256,1024]{1,0:T(8,128)(2,1)S(1)}, u32[]{:S(2)}, u32[]{:S(2)}) collective-permute-start(bf16[256,1024]{1,0:T(8,128)(2,1)S(1)} %add_convert_fusion.13), channel_id=1, source_target_pairs={{0,16},{1,17},{2,18},{3,19},{4,20},{5,21},{6,22},{7,23},{8,24},{9,... | collective-permute-start | bytes 1572872 | tf_op jit(solution)/shard_map/ppermute | solution.py:54
  187.1 2.0 collective-permute-start.16
  209.8 2.0 collective-permute-start.17
  212.2 14.0 %collective-permute-start.18 = (bf16[256,1024]{1,0:T(8,128)(2,1)S(1)}, bf16[256,1024]{1,0:T(8,128)(2,1)S(1)}, u32[]{:S(2)}, u32[]{:S(2)}) collective-permute-start(bf16[256,1024]{1,0:T(8,128)(2,1)S(1)} %add_convert_fusion.12), channel_id=1, source_target_pairs={{0,8},{4,12},{8,0},{12,4},{1,9},{5,13},{9,1},{13,5},{2,10},{6,14},... | collective-permute-start | bytes 1572872 | tf_op jit(solution)/shard_map/ppermute | solution.py:27
  227.8 12.8 %collective-permute-start.19 = (bf16[256,1024]{1,0:T(8,128)(2,1)S(1)}, bf16[256,1024]{1,0:T(8,128)(2,1)S(1)}, u32[]{:S(2)}, u32[]{:S(2)}) collective-permute-start(bf16[256,1024]{1,0:T(8,128)(2,1)S(1)} %fusion.232), channel_id=1, source_target_pairs={{0,4},{4,0},{8,12},{12,8},{1,5},{5,1},{9,13},{13,9},{2,6},{6,2},{1... | collective-permute-start | bytes 1572872 | tf_op jit(solution)/shard_map/ppermute | solution.py:27
  248.4 2.0 collective-permute-start.20
  251.9 21.0 %collective-permute-start.21 = (bf16[256,1024]{1,0:T(8,128)(2,1)}, bf16[256,1024]{1,0:T(8,128)(2,1)}, u32[]{:S(2)}, u32[]{:S(2)}) collective-permute-start(bf16[256,1024]{1,0:T(8,128)(2,1)} %add_convert_fusion.11), channel_id=1, source_target_pairs={{0,8},{4,12},{8,0},{12,4},{1,9},{5,13},{9,1},{13,5},{2,10},{6,14},... | collective-permute-start | bytes 1572872 | tf_op jit(solution)/shard_map/ppermute | solution.py:27
  268.5 4.4 collective-permute-start.22
  297.9 2.1 collective-permute-start.25
  304.2 2.0 collective-permute-start.26
  307.7 14.5 %collective-permute-start.27 = (bf16[256,1024]{1,0:T(8,128)(2,1)}, bf16[256,1024]{1,0:T(8,128)(2,1)}, u32[]{:S(2)}, u32[]{:S(2)}) collective-permute-start(bf16[256,1024]{1,0:T(8,128)(2,1)} %add_convert_fusion.9), channel_id=1, source_target_pairs={{0,8},{4,12},{8,0},{12,4},{1,9},{5,13},{9,1},{13,5},{2,10},{6,14},... | collective-permute-start | bytes 1572872 | tf_op jit(solution)/shard_map/ppermute | solution.py:27
  326.3 2.0 collective-permute-start.28
  327.9 29.6 %collective-permute-start.32 = (f32[4,256,128]{1,2,0:T(8,128)}, f32[4,256,128]{1,2,0:T(8,128)}, u32[]{:S(2)}, u32[]{:S(2)}) collective-permute-start(f32[4,256,128]{1,2,0:T(8,128)} %slice_bitcast_fusion), channel_id=1, source_target_pairs={{0,4},{4,0},{8,12},{12,8},{1,5},{5,1},{9,13},{13,9},{2,6},{6,2},{1... | collective-permute-start | bytes 1572872 | tf_op jit(solution)/shard_map/ppermute | solution.py:27
  357.5 2.3 collective-permute-start.29
  359.4 206.7 %all-reduce.5.cloned.1.call-start = ((), (), s32[]{:S(2)}) async-start(), calls=%async_computation.2 | async-start | bytes 1048576 | tf_op jit(solution)/shard_map/psum | solution.py:269
  362.1 31.0 %copy-start.194 = (f32[256]{0:T(256)S(1)}, f32[256]{0:T(256)}, u32[]{:S(2)}) copy-start(f32[256]{0:T(256)} %copy-done.193) | copy-start | bytes 3076
  362.1 31.0 %copy-start.202 = (f32[256]{0:T(256)S(1)}, f32[256]{0:T(256)}, u32[]{:S(2)}) copy-start(f32[256]{0:T(256)} %copy-done.201) | copy-start | bytes 3076
  362.1 14.2 %collective-permute-start.30 = (bf16[256,1024]{1,0:T(8,128)(2,1)S(1)}, bf16[256,1024]{1,0:T(8,128)(2,1)S(1)}, u32[]{:S(2)}, u32[]{:S(2)}) collective-permute-start(bf16[256,1024]{1,0:T(8,128)(2,1)S(1)} %add_convert_fusion.8), channel_id=1, source_target_pairs={{0,8},{4,12},{8,0},{12,4},{1,9},{5,13},{9,1},{13,5},{2,10},{6,14},... | collective-permute-start | bytes 1572872 | tf_op jit(solution)/shard_map/ppermute | solution.py:27
  377.3 15.7 %collective-permute-start.31 = (bf16[256,1024]{1,0:T(8,128)(2,1)}, bf16[256,1024]{1,0:T(8,128)(2,1)}, u32[]{:S(2)}, u32[]{:S(2)}) collective-permute-start(bf16[256,1024]{1,0:T(8,128)(2,1)} %add_convert_fusion.7), channel_id=1, source_target_pairs={{16,0},{17,1},{18,2},{19,3},{20,4},{21,5},{22,6},{23,7},{24,8},{25... | collective-permute-start | bytes 1572872 | tf_op jit(solution)/shard_map/ppermute | solution.py:54
  396.3 2.0 collective-permute-start.33
  402.4 2.0 collective-permute-start.34
  405.2 14.0 %collective-permute-start.35 = (bf16[256,1024]{1,0:T(8,128)(2,1)S(1)}, bf16[256,1024]{1,0:T(8,128)(2,1)S(1)}, u32[]{:S(2)}, u32[]{:S(2)}) collective-permute-start(bf16[256,1024]{1,0:T(8,128)(2,1)S(1)} %add_convert_fusion.6), channel_id=1, source_target_pairs={{0,8},{4,12},{8,0},{12,4},{1,9},{5,13},{9,1},{13,5},{2,10},{6,14},... | collective-permute-start | bytes 1572872 | tf_op jit(solution)/shard_map/ppermute | solution.py:27
  420.9 2.0 collective-permute-start.36
  447.1 2.0 collective-permute-start.37
  449.7 14.0 %collective-permute-start.38 = (bf16[256,1024]{1,0:T(8,128)(2,1)S(1)}, bf16[256,1024]{1,0:T(8,128)(2,1)S(1)}, u32[]{:S(2)}, u32[]{:S(2)}) collective-permute-start(bf16[256,1024]{1,0:T(8,128)(2,1)S(1)} %add_convert_fusion.5), channel_id=1, source_target_pairs={{0,8},{4,12},{8,0},{12,4},{1,9},{5,13},{9,1},{13,5},{2,10},{6,14},... | collective-permute-start | bytes 1572872 | tf_op jit(solution)/shard_map/ppermute | solution.py:27
  454.4 15.4 %collective-permute-start.48 = (f32[1024,128]{1,0:T(8,128)S(1)}, f32[1024,128]{1,0:T(8,128)S(1)}, u32[]{:S(2)}, u32[]{:S(2)}) collective-permute-start(f32[1024,128]{1,0:T(8,128)S(1)} %convolution_add_fusion.4), channel_id=1, source_target_pairs={{0,4},{4,0},{8,12},{12,8},{1,5},{5,1},{9,13},{13,9},{2,6},{6,2},{1... | collective-permute-start | bytes 1572872 | tf_op jit(solution)/shard_map/ppermute | solution.py:27
  465.2 15.3 %collective-permute-start.39 = (bf16[256,1024]{1,0:T(8,128)(2,1)}, bf16[256,1024]{1,0:T(8,128)(2,1)}, u32[]{:S(2)}, u32[]{:S(2)}) collective-permute-start(bf16[256,1024]{1,0:T(8,128)(2,1)} %get-tuple-element.56), channel_id=1, source_target_pairs={{16,0},{17,1},{18,2},{19,3},{20,4},{21,5},{22,6},{23,7},{24,8},{25... | collective-permute-start | bytes 1572872 | tf_op jit(solution)/shard_map/ppermute | solution.py:54
  470.7 307.3 %all-reduce.7.cloned.1.call-start = ((), (), s32[]{:S(2)}) async-start(), calls=%async_computation.3 | async-start | bytes 12582912 | tf_op jit(solution)/shard_map/psum | solution.py:265
  485.0 2.8 collective-permute-start.40
  492.8 4.6 collective-permute-start.41
  498.2 14.3 %collective-permute-start.42 = (bf16[256,1024]{1,0:T(8,128)(2,1)S(1)}, bf16[256,1024]{1,0:T(8,128)(2,1)S(1)}, u32[]{:S(2)}, u32[]{:S(2)}) collective-permute-start(bf16[256,1024]{1,0:T(8,128)(2,1)S(1)} %add_convert_fusion.4), channel_id=1, source_target_pairs={{0,8},{4,12},{8,0},{12,4},{1,9},{5,13},{9,1},{13,5},{2,10},{6,14},... | collective-permute-start | bytes 1572872 | tf_op jit(solution)/shard_map/ppermute | solution.py:27
  514.1 4.7 collective-permute-start.43
  558.4 8.9 %collective-permute-start.44 = (bf16[256,1024]{1,0:T(8,128)(2,1)}, bf16[256,1024]{1,0:T(8,128)(2,1)}, u32[]{:S(2)}, u32[]{:S(2)}) collective-permute-start(bf16[256,1024]{1,0:T(8,128)(2,1)} %convolution_convert_fusion.3), channel_id=1, source_target_pairs={{0,4},{4,0},{8,12},{12,8},{1,5},{5,1},{9,13},{13,9},{2,6},{6,2},{1... | collective-permute-start | bytes 1572872 | tf_op jit(solution)/shard_map/ppermute | solution.py:27
  558.7 1.6 collective-permute-start.23
  560.4 3.6 collective-permute-start.24
  567.2 7.7 collective-permute-start.49
  570.4 13.6 %collective-permute-start.45 = (bf16[256,1024]{1,0:T(8,128)(2,1)}, bf16[256,1024]{1,0:T(8,128)(2,1)}, u32[]{:S(2)}, u32[]{:S(2)}) collective-permute-start(bf16[256,1024]{1,0:T(8,128)(2,1)} %add_convert_fusion.3), channel_id=1, source_target_pairs={{0,8},{4,12},{8,0},{12,4},{1,9},{5,13},{9,1},{13,5},{2,10},{6,14},... | collective-permute-start | bytes 1572872 | tf_op jit(solution)/shard_map/ppermute | solution.py:27
  579.3 10.2 %collective-permute-start.47 = (f32[6,1024]{1,0:T(8,128)S(1)}, f32[6,1024]{1,0:T(8,128)S(1)}, u32[]{:S(2)}, u32[]{:S(2)}) collective-permute-start(f32[6,1024]{1,0:T(8,128)S(1)} %add_add_fusion.10), channel_id=1, source_target_pairs={{0,4},{4,0},{8,12},{12,8},{1,5},{5,1},{9,13},{13,9},{2,6},{6,2},{1... | collective-permute-start | bytes 73736 | tf_op jit(solution)/shard_map/ppermute | solution.py:27
  587.7 28.3 %copy-start.34 = (f32[1,128,1024]{2,1,0:T(8,128)S(1)}, f32[1,128,1024]{2,1,0:T(8,128)}, u32[]{:S(2)}) copy-start(f32[1,128,1024]{2,1,0:T(8,128)} %copy-done.33) | copy-start | bytes 1572868
  587.7 28.3 %collective-permute-start.46 = (f32[2,128,512]{2,1,0:T(8,128)}, f32[2,128,512]{2,1,0:T(8,128)S(1)}, u32[]{:S(2)}, u32[]{:S(2)}) collective-permute-start(f32[2,128,512]{2,1,0:T(8,128)} %pad_maximum_fusion.45), channel_id=1, source_target_pairs={{0,16},{16,0},{1,17},{17,1},{2,18},{18,2},{3,19},{19,3},{4,20},{20... | collective-permute-start | bytes 1572872 | tf_op jit(solution)/shard_map/ppermute | solution.py:54
  (244 other events, 1571.2 us)
Sparse Core Ops, SparseCore 0:
  359.6 20.7 reduce-scatter.1
  470.8 38.1 all-reduce.4
  555.5 222.4 all-reduce.6

commit v2 on v1

v2 whole, which is shorter than its diff:
```python
import functools

import jax
import jax.numpy as jnp
import numpy as np
from jax import lax
from jax.experimental import pallas as pl
from jax.experimental.pallas import tpu as pltpu
from jax.sharding import PartitionSpec as P

HD = 64
QLEN = 32
LANES = 128

norm_eps = 1e-05
unit_eps = 1e-06
softness_factor = 0.0625
rope_base = 10000.0
hidden_score = -1000000000.0
contract_rows = (((0,), (0,)), ((), ()))
contract_cols = (((1,), (1,)), ((), ()))
contract_inner = (((1,), (0,)), ((), ()))
bf16 = jnp.bfloat16
f32 = jnp.float32


def dot(left, right, contraction=contract_inner):
    return lax.dot_general(left, right, contraction, preferred_element_type=f32)


def flip(value, bit):
    count = lax.axis_size("tensor")
    return lax.ppermute(value, "tensor", [(i, i ^ (1 << bit)) for i in range(count)])


def chip_bits():
    return range(1, lax.axis_size("tensor").bit_length() - 1)


def core_other(value):
    return flip(value, 0)


def chips_gather(value, chip):
    for bit in chip_bits():
        other = flip(value, bit)
        upper = (chip >> (bit - 1)) % 2 == 1
        value = jnp.concatenate([jnp.where(upper, other, value), jnp.where(upper, value, other)], axis=0)
    return value


def chips_other(low):
    bits = list(chip_bits())
    if not bits:
        return low, jnp.zeros_like(low)
    for bit in bits[:-1]:
        low = (low.astype(f32) + flip(low, bit).astype(f32)).astype(bf16)
    return low, flip(low, bits[-1])


def to_section(value, pairs):
    return lax.ppermute(value, "section", pairs)


def dp_gather(value):
    count = lax.axis_size("dp")
    me = lax.axis_index("dp")
    value = value[None]
    step = 1
    while step < count:
        other = lax.ppermute(value, "dp", [(i, i ^ step) for i in range(count)])
        upper = (me // step) % 2 == 1
        value = jnp.concatenate([jnp.where(upper, other, value), jnp.where(upper, value, other)], axis=0)
        step *= 2
    return value


def dp_sum(value):
    count = lax.axis_size("dp")
    step = 1
    while step < count:
        value = value + lax.ppermute(value, "dp", [(i, i ^ step) for i in range(count)])
        step *= 2
    return value


def add_kernel(x, y, *refs):
    refs[-1][...] = (x[...].astype(f32) + y[...].astype(f32)).astype(bf16)


def add_step(x, y, following=None, after=()):
    extra = ([following] if following is not None else []) + list(after)

    def body(x_ref, y_ref, *refs):
        add_kernel(x_ref, y_ref, refs[-1])

    handed = [jax.ShapeDtypeStruct(following.shape, following.dtype)] if following is not None else []
    out = pl.pallas_call(
        body,
        in_specs=[VMEM, VMEM] + [ANY] * len(extra),
        out_specs=[ANY] * len(handed) + [VMEM],
        out_shape=handed + [jax.ShapeDtypeStruct(x.shape, bf16)],
        input_output_aliases={2: 0} if handed else {},
        compiler_params=pltpu.CompilerParams(vmem_limit_bytes=16 * 1024 * 1024),
    )(x, y, *extra)
    return out[-1], (out[0] if handed else None)


class LineSum:

    def __init__(self):
        self.waiting, self.flying, self.side, self.results, self.last = [], [], None, [], ()

    def put(self, chunks):
        self.waiting += chunks
        while len(self.flying) < 2 and self.waiting:
            self.launch(self.waiting.pop(0))

    def launch(self, chunk):
        self.flying.append((chunk, lax.ppermute(chunk, "dp", [(0, 1), (3, 2)])))

    def step(self, after=()):
        before = self.side
        after = tuple(after) + tuple(back for _, back in self.results[-2:-1])
        if self.flying:
            chunk, arrived = self.flying.pop(0)
            following = self.waiting.pop(0) if self.waiting else None
            side, following = add_step(chunk, arrived, following, tuple(after) + self.last)
            self.last = (side,)
            if following is not None:
                self.launch(following)
            self.side = (side, lax.ppermute(side, "dp", [(1, 2), (2, 1)]))
        else:
            self.side = None
        if before is not None:
            total, _ = add_step(*before, None, self.last)
            self.last = (total,)
            self.results.append((total, lax.ppermute(total, "dp", [(1, 0), (2, 3)])))
        return self.last

    def busy(self):
        return bool(self.flying or self.side is not None)


def gathered_line(results):
    me = lax.axis_index("dp")
    totals = jnp.concatenate([t for t, _ in results], axis=0)
    backs = jnp.concatenate([r for _, r in results], axis=0)
    return jnp.where((me == 0) | (me == 3), backs, totals).astype(f32)


def rope_tables(positions):
    half = HD // 2
    frequency = np.power(np.float32(rope_base), (-2.0 * np.arange(half) / HD).astype(np.float32)).astype(np.float32)
    angles = (positions.astype(np.float32)[:, None] * frequency[None, :]).astype(np.float32)
    cosine, sine = np.cos(angles), np.sin(angles)
    head = (np.concatenate([cosine, cosine], 1), np.concatenate([-sine, sine], 1))
    return tuple(np.tile(part, (1, LANES // HD)).astype(np.float32) for part in head)


VMEM = pl.BlockSpec(memory_space=pltpu.VMEM)
ANY = pl.BlockSpec(memory_space=pl.ANY)
SMEM = pl.BlockSpec(memory_space=pltpu.SMEM)


def held(x):
    return pltpu.with_memory_space_constraint(x, pltpu.HBM)


def call(kernel, ins, outs, scratch=(), after=(), smem=(), keep=(), limit=16):
    n = len(ins)

    def body(*refs):
        kernel(*refs[:n], *refs[n + len(after) :])

    return pl.pallas_call(
        body,
        in_specs=[SMEM if i in smem else VMEM for i in range(n)] + [ANY] * len(after),
        out_specs=[VMEM] * len(outs),
        out_shape=[pltpu.HBM(*out) if i in keep else jax.ShapeDtypeStruct(*out) for i, out in enumerate(outs)],
        scratch_shapes=list(scratch),
        compiler_params=pltpu.CompilerParams(vmem_limit_bytes=limit * 1024 * 1024),
    )(*ins, *after)


def load_kernel(own, oth, out, sem, axis):
    size = own.shape[axis]
    places = [out.at[:, :size], out.at[:, size:]] if axis else [out.at[:size], out.at[size:]]
    copies = [pltpu.make_async_copy(x, place, sem.at[i]) for i, (x, place) in enumerate(zip((own, oth), places))]
    for copy in copies:
        copy.start()
    for copy in copies:
        copy.wait()


def chip_weight(own, axis):
    other = core_other(own)
    shape = tuple(2 * n if i == axis else n for i, n in enumerate(own.shape))
    return pl.pallas_call(
        functools.partial(load_kernel, axis=axis),
        in_specs=[ANY, ANY],
        out_specs=VMEM,
        out_shape=pltpu.VMEM(shape, own.dtype),
        scratch_shapes=[pltpu.SemaphoreType.DMA((2,))],
        compiler_params=pltpu.CompilerParams(vmem_limit_bytes=16 * 1024 * 1024),
    )(own, other)


def half_rows(ref, c):
    size = ref.shape[0] // 2
    return ref[c * size : (c + 1) * size, :]


def half_lanes(ref, c):
    size = ref.shape[1] // 2
    return ref[:, c * size : (c + 1) * size]


def merge(out, before, value):
    size = value.shape[0]
    out[:size, :] = before[...]
    out[size:, :] = value


def swap_halves(tile):
    lane = lax.broadcasted_iota(jnp.int32, tile.shape, 1)
    return jnp.where(lane % HD < HD // 2, pltpu.roll(tile, LANES - HD // 2, 1), pltpu.roll(tile, HD // 2, 1))


def qkv_kernel(flag, entering, received_a, received_b, w, b, cos, sin, h_ref, q_ref, kv_ref):
    received = jnp.concatenate([received_a[...], received_b[...]], axis=0)
    h = jnp.where(flag[0, 0] == 1, entering[...], received)
    h_ref[...] = h
    width = w.shape[1] // 6
    c, s = cos[...], sin[...]
    for place in range(2):
        at = slice(place * 3 * width, (place + 1) * 3 * width)
        p = dot(h, w[:, at]) + b[:, at]
        for t in range(0, width, LANES):
            at = slice(place * width + t, place * width + t + LANES)
            tile = p[:, t : t + LANES]
            q_ref[:, at] = (tile * c + swap_halves(tile) * s).astype(bf16)
            tile = p[:, width + t : width + t + LANES]
            kv_ref[:, at] = (tile * c + swap_halves(tile) * s).astype(bf16)
        kv_ref[:, 2 * width + place * width : 2 * width + (place + 1) * width] = p[:, 2 * width :].astype(bf16)


def qkv_step(flag, entering, received, w, tables, after=()):
    rows, model = entering.shape
    features = w["qkv"].shape[1] // 3
    return call(
        qkv_kernel,
        [flag, entering, *received, w["qkv"], w["qkv_b"], *tables],
        [((rows, model), bf16), ((rows, features), bf16), ((rows, 2 * features), bf16)],
        after=after,
        smem=(0,),
        keep=(0, 1, 2),
    )


def head_rows(tile, place):
    row = lax.broadcasted_iota(jnp.int32, tile.shape, 0)
    return jnp.where(row // HD == place, tile, 0.0).astype(bf16)


def head_lanes(tile, place):
    lane = lax.broadcasted_iota(jnp.int32, tile.shape, 1)
    return jnp.where(lane // HD == place, tile, 0.0).astype(bf16)


def tile_at(j, features, base=0):
    return slice(base + j * LANES, base + (j + 1) * LANES)


def partner_tile(j, features):
    tiles = features // LANES
    return (j + tiles // 2) % tiles


def partner_base(j, features, base=0):
    return tile_at(partner_tile(j, features), features, base)


def attend_kernel(*refs, c):
    q_ref, kv_own, kv_oth, bias_ref, w = refs[:5]
    if c:
        o_before, v_t, refs = refs[5], refs[6], refs[7:]
        o_own, o_oth, lse_ref, low_ref, o_t, s_all = refs
    else:
        o_first, k_t, v_t, lse_ref, low_ref, o_t, s_all = refs[5:]
    features = q_ref.shape[1]
    rows = kv_own.shape[0]
    some = rows // 2
    q_half = half_rows(q_ref, c)
    for j in range(features // LANES):
        at = tile_at(j, features)
        q_t = q_half[:, at].astype(f32).T * HD ** (-0.5)
        k_here, k_there = kv_own[:, at], kv_oth[:, partner_base(j, features)]
        for place in range(2):
            q_one = head_rows(q_t, place)
            s_all[2 * j + place, :rows, :] = dot(k_here, q_one)
            s_all[2 * j + place, rows:, :] = dot(k_there, q_one)
        if not c:
            v_here, v_there = kv_own[:, tile_at(j, features, features)], kv_oth[:, partner_base(j, features, features)]
            v_t[at, :rows] = v_here.astype(f32).T.astype(bf16)
            v_t[at, rows:] = v_there.astype(f32).T.astype(bf16)
            k_t[at, :rows] = k_here.astype(f32).T.astype(bf16)
            k_t[at, rows:] = k_there.astype(f32).T.astype(bf16)
    bias = bias_ref[:, c * some : (c + 1) * some]
    for h in range(features // HD):
        s = s_all[h] + bias
        peak = jnp.max(s, axis=0, keepdims=True)
        e = jnp.exp(s - peak)
        total = jnp.sum(e, axis=0, keepdims=True)
        s_all[h] = e * (1.0 / total)
        lse_ref[h : h + 1, :] = peak + jnp.log(total)
    for h in range(features // HD):
        o_t[h * HD : (h + 1) * HD, :] = dot(v_t[h * HD : (h + 1) * HD, :], s_all[h].astype(bf16))
    o = o_t[...].T.astype(bf16)
    half = features // 2
    if c:
        merge(o_own, o_before[:, :half], o[:, :half])
        merge(o_oth, o_before[:, half:], o[:, half:])
    else:
        o_first[...] = o
    low_ref[...] = dot(o, w[...]).astype(bf16)


def attend_step(c, q, kv, kv_other, bias, w, before=(), after=()):
    rows, features = q.shape
    model = w["out"].shape[1]
    some = rows // 2
    heads = features // HD
    if c:
        kept = [((rows, features // 2), bf16)] * 2
    else:
        kept = [((some, features), bf16), ((features, 2 * rows), bf16), ((features, 2 * rows), bf16)]
    return call(
        functools.partial(attend_kernel, c=c),
        [q, kv, kv_other, bias, w["out"], *before],
        kept + [((heads, some), f32), ((some, model), bf16)],
        scratch=[pltpu.VMEM((features, some), f32), pltpu.VMEM((heads, 2 * rows, some), f32)],
        after=after,
        keep=(0, 1, 2) if c else (0, 1, 2, 3),
    )


def normed(values):
    centred = values - jnp.mean(values, axis=-1, keepdims=True)
    inverse = lax.rsqrt(jnp.mean(centred * centred, axis=-1, keepdims=True) + norm_eps)
    return centred * inverse, inverse


def norm_back(gradient, n, inverse):
    return inverse * (gradient - jnp.mean(gradient, axis=-1, keepdims=True) - n * jnp.mean(gradient * n, axis=-1, keepdims=True))


def feed_kernel(*refs, c):
    h, low, recv, vec, up, b, down = refs[:7]
    before, refs = (refs[7:10], refs[10:]) if c else (None, refs[7:])
    n_ref, r_ref, sl_ref, low_ref, h1_ref, g_own, g_oth = refs
    s1 = half_rows(h, c).astype(f32) + (low[...].astype(f32) + recv[...].astype(f32)) + vec[0:1, :]
    n, r = normed(s1)
    n_ref[...] = n
    r_ref[...] = r
    h1 = (n * vec[1:2, :] + vec[2:3, :]).astype(bf16)
    u = dot(h1, up[...]) + b[...]
    phi = 0.5 * (1.0 + lax.erf(u * 0.7071067811865476))
    g = (u * phi).astype(bf16)
    sl_ref[...] = (phi + u * jnp.exp(-0.5 * u * u) * 0.3989422804014327).astype(bf16)
    low_ref[...] = dot(g, down[...]).astype(bf16)
    units = up.shape[1] // 2
    for place, value in enumerate((h1, g[:, :units], g[:, units:])):
        out = (h1_ref, g_own, g_oth)[place]
        if c:
            merge(out, before[place], value)
        else:
            out[...] = value


def feed_step(c, h, low, recv, vec, w, before=(), after=()):
    rows, model = h.shape
    units = w["up"].shape[1]
    some = rows // 2
    kept = rows if c else some
    return call(
        functools.partial(feed_kernel, c=c),
        [h, low, recv, vec, w["up"], w["up_b"], w["down"], *before],
        [
            ((some, model), f32), ((some, 1), f32), ((some, units), bf16), ((some, model), bf16),
            ((kept, model), bf16), ((kept, units // 2), bf16), ((kept, units // 2), bf16),
        ],
        after=after,
        keep=(0, 1, 2, 4, 5, 6),
    )


def output_kernel(n1, low, recv, vec, n_ref, r_ref, y_ref):
    s2 = n1[...] * vec[0:1, :] + vec[1:2, :] + (low[...].astype(f32) + recv[...].astype(f32)) + vec[2:3, :]
    n, r = normed(s2)
    n_ref[...] = n
    r_ref[...] = r
    y_ref[...] = (n * vec[3:4, :] + vec[4:5, :]).astype(bf16)


def output_step(n1, low, recv, vec, after=()):
    return call(output_kernel, [n1, low, recv, vec], [(n1.shape, f32), ((n1.shape[0], 1), f32), (n1.shape, bf16)], after=after, keep=(0, 1))


def feed_back_kernel(*refs, c):
    flag, received, own, n2, r2, gain, up, down, sl = refs[:9]
    before, refs = (refs[9:12], refs[12:]) if c else (None, refs[9:])
    ds_ref, low_ref, vec_ref, ub_ref, f_ref, u_own, u_oth = refs
    dy = jnp.where(flag[0, 0] == 1, received[...].astype(f32), half_rows(own, c))
    n = n2[...]
    ds = norm_back(dy * gain[...], n, r2[...])
    ds_ref[...] = ds
    vec_ref[0:1, :] = jnp.sum(ds, axis=0, keepdims=True)
    vec_ref[1:2, :] = jnp.sum(dy * n, axis=0, keepdims=True)
    vec_ref[2:3, :] = jnp.sum(dy, axis=0, keepdims=True)
    f = ds.astype(bf16)
    du = dot(f, down[...], contract_cols) * sl[...].astype(f32)
    ub_ref[...] = jnp.sum(du, axis=0, keepdims=True)
    u = du.astype(bf16)
    low_ref[...] = dot(u, up[...], contract_cols).astype(bf16)
    units = up.shape[1] // 2
    for place, value in enumerate((f, u[:, :units], u[:, units:])):
        out = (f_ref, u_own, u_oth)[place]
        if c:
            merge(out, before[place], value)
        else:
            out[...] = value


def feed_back_step(c, flag, received, own, n2, r2, gain, w, sl, before=(), after=()):
    some, model = n2.shape
    units = w["up"].shape[1]
    kept = 2 * some if c else some
    return call(
        functools.partial(feed_back_kernel, c=c),
        [flag, received, own, n2, r2, gain, w["up"], w["down"], sl, *before],
        [
            ((some, model), f32), ((some, model), bf16), ((3, model), f32), ((1, units), f32),
            ((kept, model), bf16), ((kept, units // 2), bf16), ((kept, units // 2), bf16),
        ],
        after=after,
        smem=(0,),
        keep=(0, 2, 3, 4, 5, 6),
    )


def attend_back_kernel(*refs, c):
    (ds2, low, recv, n1, r1, gain, w, q_ref, kv_own, kv_oth, k_t, bias_ref, lse_ref), refs = refs[:13], refs[13:]
    if c:
        (own_before, oth_before, out_before), refs = refs[:3], refs[3:]
    ds_ref, dq_ref, vec_ref, dkv_ref, dkv_send, out_ref, dq_t, s_all, d_all, a_all, slopes = refs
    features = q_ref.shape[1]
    rows = kv_own.shape[0]
    some = rows // 2
    dh1 = ds2[...] + (low[...].astype(f32) + recv[...].astype(f32))
    n = n1[...]
    ds1 = norm_back(dh1 * gain[...], n, r1[...])
    ds_ref[...] = ds1
    vec_ref[0:1, :] = jnp.sum(ds1, axis=0, keepdims=True)
    vec_ref[1:2, :] = jnp.sum(dh1 * n, axis=0, keepdims=True)
    vec_ref[2:3, :] = jnp.sum(dh1, axis=0, keepdims=True)
    spread = ds1.astype(bf16)
    if c:
        merge(out_ref, out_before, spread)
    else:
        out_ref[...] = spread
    q_half = half_rows(q_ref, c)
    for j in range(features // LANES):
        at = tile_at(j, features)
        q_t = q_half[:, at].astype(f32).T * HD ** (-0.5)
        k_here, k_there = kv_own[:, at], kv_oth[:, partner_base(j, features)]
        for place in range(2):
            q_one = head_rows(q_t, place)
            s_all[2 * j + place, :rows, :] = dot(k_here, q_one)
            s_all[2 * j + place, rows:, :] = dot(k_there, q_one)
    mixed = dot(spread, w[...], contract_cols).astype(bf16).astype(f32)
    for j in range(features // LANES):
        do_t = mixed[:, tile_at(j, features)].T
        v_here, v_there = kv_own[:, tile_at(j, features, features)], kv_oth[:, partner_base(j, features, features)]
        for place in range(2):
            do_one = head_rows(do_t, place)
            d_all[2 * j + place, :rows, :] = dot(v_here, do_one)
            d_all[2 * j + place, rows:, :] = dot(v_there, do_one)
    bias = bias_ref[:, c * some : (c + 1) * some]
    for h in range(features // HD):
        a = jnp.exp(s_all[h] + bias - lse_ref[h : h + 1, :])
        da = d_all[h]
        slope = a * (da - jnp.sum(da * a, axis=0, keepdims=True))
        slopes[h] = slope.astype(bf16) * jnp.asarray(HD ** (-0.5), bf16)
        a_all[h] = a.astype(bf16)
    for h in range(features // HD):
        dq_t[h * HD : (h + 1) * HD, :] = dot(k_t[h * HD : (h + 1) * HD, :], slopes[h])
    for j in range(features // LANES):
        at, v_at = tile_at(j, features), tile_at(j, features, features)
        theirs, v_theirs = partner_base(j, features), partner_base(j, features, features)
        q, do = q_half[:, at].astype(f32), mixed[:, at]
        dk = dot(slopes[2 * j], head_lanes(q, 0)) + dot(slopes[2 * j + 1], head_lanes(q, 1))
        dv = dot(a_all[2 * j], head_lanes(do, 0)) + dot(a_all[2 * j + 1], head_lanes(do, 1))
        if c:
            dkv_ref[:, at] = dk[:rows] + own_before[:, at]
            dkv_ref[:, v_at] = dv[:rows] + own_before[:, v_at]
            dkv_send[:, theirs] = (dk[rows:] + oth_before[:, theirs]).astype(bf16)
            dkv_send[:, v_theirs] = (dv[rows:] + oth_before[:, v_theirs]).astype(bf16)
        else:
            dkv_ref[:, at] = dk[:rows]
            dkv_ref[:, v_at] = dv[:rows]
            dkv_send[:, theirs] = dk[rows:]
            dkv_send[:, v_theirs] = dv[rows:]
    dq_ref[...] = dq_t[...].T


def attend_back_step(c, ds2, low, recv, n1, r1, gain, w, q, kv, kv_other, k_t, bias, lse, before=(), after=()):
    some, model = ds2.shape
    features = q.shape[1]
    rows = 2 * some
    heads = features // HD
    all_heads = (heads, 2 * rows, some)
    return call(
        functools.partial(attend_back_kernel, c=c),
        [ds2, low, recv, n1, r1, gain, w["out"], q, kv, kv_other, k_t, bias, lse, *before],
        [
            ((some, model), f32), ((some, features), f32), ((3, model), f32),
            ((rows, 2 * features), f32), ((rows, 2 * features), bf16 if c else f32), ((rows if c else some, model), bf16),
        ],
        scratch=[
            pltpu.VMEM((features, some), f32), pltpu.VMEM(all_heads, f32), pltpu.VMEM(all_heads, f32), pltpu.VMEM(all_heads, bf16),
            pltpu.VMEM(all_heads, bf16),
        ],
        after=after,
        keep=(0, 1, 2, 3, 5) if c else (0, 1, 2, 3, 4, 5),
        limit=24,
    )


def qkv_back_kernel(*refs, c):
    dq, dkv_ref, arrived_ref, cos, sin, w = refs[:6]
    before, refs = (refs[6:8], refs[8:]) if c else (None, refs[6:])
    low_ref, b_ref, p_own, p_oth = refs
    some, features = dq.shape
    width = features // 2
    cosine, sine = half_rows(cos, c), half_rows(sin, c)
    dkv = half_rows(dkv_ref, c) + half_rows(arrived_ref, c).astype(f32)
    total = None
    for place, p_ref in enumerate((p_own, p_oth)):
        base = place * 3 * width
        rows_at = slice(some, 2 * some) if c else slice(0, some)
        for t in range(0, width, LANES):
            at = slice(place * width + t, place * width + t + LANES)
            v_at = slice(features + place * width + t, features + place * width + t + LANES)
            gq, gk, gv = dq[:, at], dkv[:, at], dkv[:, v_at]
            gq = gq * cosine - swap_halves(gq) * sine
            gk = gk * cosine - swap_halves(gk) * sine
            for part, g in enumerate((gq, gk, gv)):
                to = part * width + t
                p_ref[rows_at, to : to + LANES] = g.astype(bf16)
                b_ref[0:1, base + to : base + to + LANES] = jnp.sum(g, axis=0, keepdims=True)
        if c:
            p_ref[:some, :] = before[place][...]
        part = dot(p_ref[rows_at, :], w[:, base : base + 3 * width], contract_cols)
        total = part if total is None else total + part
    low_ref[...] = total.astype(bf16)


def qkv_back_step(c, dq, dkv, arrived, tables, w, before=(), after=()):
    some, features = dq.shape
    model, wide = w["qkv"].shape
    kept = 2 * some if c else some
    return call(
        functools.partial(qkv_back_kernel, c=c),
        [dq, dkv, arrived, *tables, w["qkv"], *before],
        [((some, model), bf16), ((1, wide), f32), ((kept, wide // 2), bf16), ((kept, wide // 2), bf16)],
        after=after,
        keep=(1, 2, 3),
    )


def whole(x):
    return x, pl.BlockSpec(x.shape, lambda *i: (0,) * len(x.shape))


def steps_of_rows(x, steps):
    return x, pl.BlockSpec((x.shape[0] // steps, x.shape[1]), lambda i: (i, 0))


def steps_of_lanes(x, steps):
    return x, pl.BlockSpec((x.shape[0], x.shape[1] // steps), lambda i: (0, i))


def weight_kernel(*refs, pieces, before, chunks):
    lefts, rights, refs = refs[:pieces], refs[pieces : 2 * pieces], refs[2 * pieces :]
    left = jnp.concatenate([x[...] for x in lefts], axis=0)
    right = jnp.concatenate([x[...] for x in rights], axis=0)
    total = dot(left, right, contract_rows)
    if before:
        total = total + refs[0][...]
    outs = refs[before:]
    if not chunks:
        outs[0][...] = total.astype(outs[0].dtype)
        return
    for i, out in enumerate(outs):

        @pl.when(pl.program_id(0) == i)
        def _(out=out):
            out[...] = total.astype(out.dtype)


def weight_step(lefts, rights, before=None, chunks=False, steps=2, after=()):
    shape = (lefts[0].shape[1], rights[0].shape[1])
    steps = min(steps, shape[0] // LANES)
    ins = [steps_of_lanes(held(x), steps) for x in lefts] + [whole(held(x)) for x in rights]
    if before is not None:
        ins.append(steps_of_rows(held(before), steps))
    n = len(ins)
    some = (shape[0] // steps, shape[1])
    kernel = functools.partial(weight_kernel, pieces=len(lefts), before=int(before is not None), chunks=chunks)

    def body(*refs):
        kernel(*refs[:n], *refs[n + len(after) :])

    return pl.pallas_call(
        body,
        grid=(steps,),
        in_specs=[spec for _, spec in ins] + [ANY] * len(after),
        out_specs=[pl.BlockSpec(some, lambda i: (0, 0))] * steps if chunks else pl.BlockSpec(some, lambda i: (i, 0)),
        out_shape=[jax.ShapeDtypeStruct(some, bf16)] * steps if chunks else pltpu.HBM(shape, f32),
        compiler_params=pltpu.CompilerParams(vmem_limit_bytes=24 * 1024 * 1024),
    )(*[x for x, _ in ins], *after)


def scores_kernel(y_a, y_b, proj, units, alive, grad_t, z_ref, m_ref, dy_ref, terms_ref, groups):
    low = jnp.concatenate([y_a[...], y_b[...]], axis=0)
    z = dot(low, proj[...])
    inverse = lax.rsqrt(jnp.sum(z * z, axis=-1, keepdims=True) + unit_eps)
    e = z * inverse
    e_low = e.astype(bf16)
    e_t = e_low.astype(f32).T.astype(bf16)
    block = units.shape[0] // groups
    back = None
    for d in range(groups):
        at = slice(d * block, (d + 1) * block)
        docs = units[at, :]
        logits = jnp.where(alive[at, :] > 0, dot(docs, e_t) / softness_factor, hidden_score)
        peak = jnp.max(logits, axis=0, keepdims=True)
        x = jnp.exp(logits - peak)
        total = jnp.sum(x, axis=0, keepdims=True)
        m_ref[d : d + 1, :] = softness_factor * (peak + jnp.log(total))
        pull = (x * (grad_t[d : d + 1, :] / total)).astype(bf16)
        terms_ref[at, :] = dot(pull, e_low)
        part = dot(docs.astype(f32).T.astype(bf16), pull)
        back = part if back is None else back + part
    de = back.T
    dz = (inverse * (de - e * jnp.sum(de * e, axis=-1, keepdims=True))).astype(bf16)
    z_ref[...] = dz
    dy_ref[...] = dot(dz, proj[...], contract_cols)


def scores_step(y, proj, units, alive, grad_t):
    rows, model = 2 * y[0].shape[0], y[0].shape[1]
    groups, width = grad_t.shape[0], proj.shape[1]
    return call(
        functools.partial(scores_kernel, groups=groups),
        [*y, proj, units, alive, grad_t],
        [((rows, width), bf16), ((groups, rows), f32), ((rows, model), f32), ((units.shape[0], width), f32)],
        limit=32,
    )


def forward(flag, entering, received, w, bias, tables, after=()):
    h, q, kv = qkv_step(flag, entering, received, w, tables, after)
    kv_other = held(core_other(kv))
    h_here, q, kv = held(h), held(q), held(kv)
    o_a, k_t, v_t, lse_a, low_a = attend_step(0, q, kv, kv_other, bias, w)
    sum_a = chips_other(low_a)
    o, o_o, lse_b, low_b = attend_step(1, q, kv, kv_other, bias, w, (held(o_a), held(v_t)))
    sum_b = chips_other(low_b)
    n1_a, r1_a, sl_a, low_a, *before = feed_step(0, h_here, *sum_a, w["vec_feed"], w)
    sum_a = chips_other(low_a)
    n1_b, r1_b, sl_b, low_b, h1, g, g_o = feed_step(1, h_here, *sum_b, w["vec_feed"], w, [held(x) for x in before])
    sum_b = chips_other(low_b)
    n1_a, n1_b = held(n1_a), held(n1_b)
    n2_a, r2_a, y_a = output_step(n1_a, *sum_a, w["vec_out"])
    n2_b, r2_b, y_b = output_step(n1_b, *sum_b, w["vec_out"])
    kept = ((g, core_other(g_o)), (h1, core_other(h1)), (o, core_other(o_o)), (h, core_other(h)))
    a = (held(lse_a), n1_a, held(r1_a), held(sl_a), held(n2_a), held(r2_a))
    b = (held(lse_b), n1_b, held(r1_b), held(sl_b), held(n2_b), held(r2_b))
    return (y_a, y_b), ((q, kv, kv_other, held(k_t)), (a, b)), kept


def backward(flag, received, own, w, bias, tables, record, hook, after):
    (q, kv, kv_other, k_t), halves = record
    parts, vectors, ubs, before, ds2s = [], [], [], (), []
    for c in range(2):
        lse, n1, r1, sl, n2, r2 = halves[c]
        ds2, low, vec, ub, *before = feed_back_step(
            c, flag, received[c], own, n2, r2, w["gain"][1:2], w, sl, [held(x) for x in before], after if c == 0 else ()
        )
        ds2s.append(held(ds2))
        parts.append(chips_other(low))
        vectors.append(vec)
        ubs.append(ub)
    f, u, u_o = before
    after = hook("feed", (f, core_other(f)), (u, core_other(u_o)))
    before, vectors_1, ds1s, dqs = (), [], [], []
    for c in range(2):
        lse, n1, r1, sl, n2, r2 = halves[c]
        ds1, dq, vec, dkv, send, out = attend_back_step(
            c, ds2s[c], *parts[c], n1, r1, w["gain"][0:1], w, q, kv, kv_other, k_t, bias, lse, before, after
        )
        before = (held(dkv), held(send), held(out)) if c == 0 else ()
        ds1s.append(ds1)
        dqs.append(held(dq))
        vectors_1.append(vec)
        if c == 0:
            after = hook("between", dq, None)
    arrived, dkv = held(core_other(send)), held(dkv)
    after = hook("between", send, None)
    nexts, pbs, before = [], [], ()
    for c in range(2):
        low, pb, *before = qkv_back_step(c, dqs[c], dkv, arrived, tables, w, [held(x) for x in before], after if c == 0 else ())
        nexts.append(chips_other(low))
        pbs.append(pb)
    p, p_o = before
    after = hook("attend", (out, core_other(out)), (p, core_other(p_o)))
    dh = [ds1s[c] + (nexts[c][0].astype(f32) + nexts[c][1].astype(f32)) for c in range(2)]
    vectors = jnp.stack([vectors_1[0] + vectors_1[1], vectors[0] + vectors[1]], axis=1)
    return dh, vectors, ubs[0] + ubs[1], pbs[0] + pbs[1], after


def on_device(tokens, segment, score_grad, qkv_weight, qkv_bias, out_weight, up_weight, up_bias, down_weight, out_bias, norm_gain, norm_shift, proj_weight):
    blocks, share, model = tokens.shape
    wide = 3 * qkv_weight.shape[-1]
    width = wide // 3
    gain, shift, bias = norm_gain[0].astype(f32), norm_shift[0].astype(f32), out_bias[0].astype(f32)
    first = lax.axis_index("section") == 0
    flag = first.astype(jnp.int32).reshape(1, 1)
    device = lax.axis_index("tensor")
    core, chip = device % 2, device // 2
    chips = lax.axis_size("tensor") // 2
    groups = lax.axis_size("dp")
    half = share * chips
    rows = 2 * half
    proj = proj_weight.shape[1]
    entering = [chips_gather(tokens[b], chip) for b in range(2)]

    def both(own):
        return jnp.concatenate([own, core_other(own)], axis=1)

    w = dict(
        qkv=chip_weight(qkv_weight[0].reshape(model, wide), 1), qkv_b=both(qkv_bias[0].reshape(1, wide).astype(f32)),
        out=chip_weight(out_weight[0], 0), up=chip_weight(up_weight[0], 1), up_b=both(up_bias.astype(f32)),
        down=chip_weight(down_weight[0], 0), gain=gain,
        vec_feed=jnp.stack([bias[0], gain[0], shift[0]]),
        vec_out=jnp.stack([gain[0], shift[0], bias[1], gain[1], shift[1]]),
    )

    def own_first(by_token):
        parts = by_token.reshape((chips, 2, share) + by_token.shape[1:])
        even = parts[:, 0].reshape((half,) + by_token.shape[1:])
        odd = parts[:, 1].reshape((half,) + by_token.shape[1:])
        return jnp.concatenate([jnp.where(core == 0, even, odd), jnp.where(core == 0, odd, even)], axis=0)

    index = np.arange(rows)
    tables = [tuple(own_first(jnp.asarray(part))[:half] for part in rope_tables(p)) for p in (index, index % QLEN)]
    segments = [own_first(segment[b]) for b in range(2)]

    def pick(zero, one):
        ids = jnp.where(first, segments[zero], segments[one])
        bias = jnp.where(ids[:, None] == ids[None, :half], 0.0, hidden_score).astype(f32)
        return bias, tuple(jnp.where(first, x, y) for x, y in zip(tables[zero], tables[one]))

    contexts = [pick(0, 0), pick(1, 0), pick(1, 1)]
    received = [jnp.zeros((half // 2, model), bf16)] * 2
    records, kept, outputs = [], [], []
    prelude = [w["vec_feed"], w["vec_out"], w["up_b"]] + [x for bias_of, tables_of in contexts for x in (bias_of, *tables_of)]
    for tick in range(3):
        y, record, keep = forward(flag, entering[min(tick, 1)], received, w, *contexts[tick], prelude if tick == 0 else ())
        records.append(record)
        kept.append(keep)
        outputs.append(y)
        if tick < 2:
            received = [to_section(part, [(0, 1)]) for part in y]

    doc_y, query_y = jnp.concatenate(outputs[1]), jnp.concatenate(outputs[2])
    z = dot(doc_y, proj_weight)
    inverse = lax.rsqrt(jnp.sum(z * z, axis=-1, keepdims=True) + unit_eps)
    doc_units = z * inverse
    units_own = dp_gather(doc_units.astype(bf16))
    units = jnp.stack([units_own, core_other(units_own)], axis=1).reshape(groups * rows, proj)
    alive = dp_gather((segments[0] == 0).astype(f32).reshape(rows // LANES, LANES)).reshape(groups * rows, 1)
    slots = score_grad.shape[0]
    member = (segments[1][:half, None] == jnp.arange(slots)[None, :]).astype(f32)
    grad_t = lax.dot_general(score_grad, member, (((0,), (1,)), ((), ())), precision=lax.Precision.HIGHEST, preferred_element_type=f32)
    query_dz, smooth, query_dy, terms = scores_step(outputs[2], proj_weight, units, alive, grad_t)
    board = lax.dot_general(member, smooth, (((0,), (1,)), ((), ())), precision=lax.Precision.HIGHEST, preferred_element_type=f32)
    terms = terms.reshape(groups, 2, half, proj)
    terms = terms[:, 0] + core_other(terms[:, 1])
    doc_grad = lax.psum_scatter(terms, "dp", scatter_dimension=0)
    doc_dz = (inverse * (doc_grad - doc_units * jnp.sum(doc_grad * doc_units, axis=-1, keepdims=True))).astype(bf16)
    doc_dy = dot(doc_dz, proj_weight, contract_cols)
    proj_grad = dot(doc_y, doc_dz, contract_rows) + dot(query_y, query_dz, contract_rows)
    own = (query_dy, doc_dy, jnp.zeros_like(doc_dy))
    received = [jnp.zeros((half // 2, model), bf16)] * 2
    pairs, sums = {}, {}
    vectors, ub, pb = None, None, None
    input_grads = [None, None]
    after = ()
    line = LineSum() if groups == 4 else None
    chunk_counts = (4, 4, 1, 4)
    plain = []
    board = board + core_other(board)
    proj_grad = dp_sum(proj_grad + core_other(proj_grad))

    for step in range(3):

        def hook(stage, one, two, step=step):
            if stage == "between":
                return line.step((one,)) if line is not None and step == 2 else ()
            done = []
            for place, pair in zip((0, 1) if stage == "feed" else (2, 3), (one, two)):
                pairs[step, place] = pair
                if step == 2:
                    chunks = weight_step(kept[0][place], pair, sums[place], True, chunk_counts[place])
                    if line is not None:
                        line.put(list(chunks))
                    else:
                        plain.append(lax.psum(jnp.concatenate(chunks), "dp").astype(f32))
                    done += chunks[:1]
            if step == 1 and stage == "attend":
                for place in range(4):
                    sums[place] = weight_step(kept[2][place] + kept[1][place], pairs[0, place] + pairs[1, place])
                    done.append(sums[place])
            return tuple(done)

        if step == 2:
            after = tuple(after) + (proj_grad, board)
        dh, vec, ub_now, pb_now, after = backward(flag, received, own[step], w, *contexts[2 - step], records[2 - step], hook, after)
        vectors = vec if vectors is None else vectors + vec
        ub = ub_now if ub is None else ub + ub_now
        pb = pb_now if pb is None else pb + pb_now
        if step < 2:
            received = [to_section(part.astype(bf16), [(1, 0)]) for part in dh]
        if step >= 1:
            input_grads[2 - step] = lax.dynamic_slice_in_dim(jnp.concatenate(dh), chip * share, share, 0)

    if line is not None:
        while line.busy():
            line.step()
        spread, at = [], 0
        for n in chunk_counts:
            spread.append(gathered_line(line.results[at : at + n]))
            at += n
    else:
        spread = plain
    d_down, d_up, d_out, d_qkv = spread
    units_count = up_weight.shape[-1]
    small = jnp.concatenate([vectors.reshape(6, model)], axis=0)
    small = small + core_other(small)
    ub = ub[:, :units_count] + core_other(ub[:, units_count:])
    pb = pb[:, :wide] + core_other(pb[:, wide:])
    vector = dp_sum(jnp.concatenate([ub[0], pb[0], small.reshape(-1)]).reshape(-1, LANES)).reshape(-1)
    ub = vector[:units_count][None]
    pb = vector[units_count : units_count + wide]
    small = vector[units_count + wide :].reshape(6, model)
    stack = jnp.stack(input_grads)
    swap = [(0, 1), (1, 0)]
    mid, docs = model // 2, groups // 2
    sent_input = to_section(stack[:, :, mid:], swap)
    sent_board, sent_proj = to_section((board[:, :docs], proj_grad[:mid]), swap)
    return (
        jnp.where(first, sent_board, board[:, docs:]),
        jnp.where(first, stack[:, :, :mid], sent_input),
        d_qkv.reshape(1, model, 3, width),
        pb.reshape(1, 3, width),
        d_out[None],
        d_up[None],
        ub,
        d_down[None],
        small[0:2][None],
        small[2:4][None],
        small[4:6][None],
        jnp.where(first, sent_proj, proj_grad[mid:]),
    )


def solution(mesh):
    return jax.shard_map(
        on_device,
        mesh=mesh,
        in_specs=(
            P("dp", "tensor", None),
            P("dp", None),
            P("dp", None),
            P("section", None, None, "tensor"),
            P("section", None, "tensor"),
            P("section", "tensor", None),
            P("section", None, "tensor"),
            P("section", "tensor"),
            P("section", "tensor", None),
            P("section", None, None),
            P("section", None, None),
            P("section", None, None),
            P(),
        ),
        out_specs=(
            P("dp", "section"),
            P("dp", "tensor", "section"),
            P("section", None, None, "tensor"),
            P("section", None, "tensor"),
            P("section", "tensor", None),
            P("section", None, "tensor"),
            P("section", "tensor"),
            P("section", "tensor", None),
            P("section", None, None),
            P("section", None, None),
            P("section", None, None),
            P("section", None),
        ),
        check_vma=False,
    )
```

time: 804 us -> 658 us (0.82)
  waiting for transfers between devices: 363 us -> 120 us
  Pallas kernels: 0 us -> 238 us
  matrix products: 183 us -> 3.33 us
  starting transfers between devices: 34.7 us -> 166 us
  blocking collectives: 52.6 us -> 0 us
  other arithmetic: 67 us -> 34.5 us
  local copies, waits for them, and re-layouts: 76.6 us -> 67.1 us
    pallas_call x0 -> x78, Pallas kernels: none -> 238 us  [the longest x40 163 us: call(): pl.pallas_call(body, in_specs=[SMEM if i in smem else VMEM for i in range...]
    psum x2 -> x0, waiting for transfers between devices: 160 us -> none  [the longest x1 160 us: on_device(): totals = [lax.psum(part.astype(bf16), 'dp').astype(f32) for part in totals]]
    ppermute x0 -> x47, starting transfers between devices: none -> 106 us  [the longest x13 59.4 us: launch(): self.flying.append((chunk, lax.ppermute(chunk, 'dp', [(0, 1), (3, 2)])))]
    dot_general x57 -> x4, matrix products: 96.3 us -> 2.22 us  [dot(): return lax.dot_general(left, right, contraction, preferred_element_type=f32)]
    ppermute x43 -> x69, waiting for transfers between devices: 157 us -> 70.9 us  [flip(): lax.ppermute(value, 'tensor', [(i, i ^ 1 << bit) for i in range(count)])]
    dot_general x17 -> x2, matrix products: 72.1 us -> 1.12 us  [the longest x1 0.85 us: on_device(): lax.dot_general(score_grad, member, (((0,), (1,)), ((), ())), precision=l...]
    ppermute x0 -> x47, waiting for transfers between devices: none -> 38.5 us  [the longest x13 15.9 us: step(): self.results.append((total, lax.ppermute(total, 'dp', [(1, 0), (2, 3)])))]
    ppermute x7 -> x11, waiting for transfers between devices: 44.3 us -> 10.3 us  [to_section(): return lax.ppermute(value, 'section', pairs)]
  transfers between devices with their start and end apart: 53 -> 128, of which waited for: 40 -> 34; matrix products, arithmetic and copies ran while one was open for 18% -> 9% of each run, Pallas kernels for 0% -> 34%
where the time goes in v2:
time: 658 us; the launch traced here: 646 us
  Pallas kernels  238 us (36%)
  starting transfers between devices  166 us (25%)
  waiting for transfers between devices  120 us (18%)
  local copies, waits for them, and re-layouts  67.1 us (10%)
  other arithmetic  34.5 us (5%)
  between operations  17.5 us (3%)
    pallas_call x40, Pallas kernels, call(): pl.pallas_call(body, in_specs=[SMEM if i in smem else VMEM for i in range...  163 us
    ppermute x69, waiting for transfers between devices, flip(): lax.ppermute(value, 'tensor', [(i, i ^ 1 << bit) for i in range(count)])  70.9 us
    ppermute x13, starting transfers between devices, launch(): self.flying.append((chunk, lax.ppermute(chunk, 'dp', [(0, 1), (3, 2)])))  59.4 us
    pallas_call x8, Pallas kernels, weight_step(): pl.pallas_call(body, grid=(steps,), in_specs=[spec for _, spec in ins] +...  40.3 us
    unnamed x410, local copies, waits for them, and re-layouts  40 us
    ppermute x69, starting transfers between devices, flip(): lax.ppermute(value, 'tensor', [(i, i ^ 1 << bit) for i in range(count)])  36.7 us
    pallas_call x26, Pallas kernels, add_step(): pl.pallas_call(body, in_specs=[VMEM, VMEM] + [ANY] * len(extra), out_spec...  26.4 us
    ppermute x11, starting transfers between devices, to_section(): return lax.ppermute(value, 'section', pairs)  23.4 us
  transfers between devices with their start and end apart: 128, of which 34 were waited for; matrix products, arithmetic and copies ran while one was open for 9% of the time, Pallas kernels for 34%

profile of v2, /device:TPU:0, one launch (start us, length us, event | category | flops | bytes accessed | tf_op | source)
XLA Modules:
  0.0 645.9 jit_solution(1129051978164291827)
XLA Ops:
  24.4 4.8 collective-permute-done
  29.2 5.4 collective-permute-done.1
  44.6 4.0 shard_map.259
  50.4 3.6 shard_map.264
  59.4 4.1 shard_map.262
  63.5 4.5 shard_map.265
  70.0 7.2 %collective-permute-done.13.refs_2_ = bf16[128,1024]{1,0:T(8,128)(2,1)S(1)} collective-permute-done((bf16[128,1024]{1,0:T(8,128)(2,1)S(1)}, bf16[128,1024]{1,0:T(8,128)(2,1)S(1)}, u32[]{:S(2)}, u32[]{:S(2)}) %collective-permute-start.13) | collective-permute-done | bytes 262176 | tf_op jit(solution)/shard_map/ppermute | solution.py:33
  79.4 3.7 collective-permute-start.14
  87.9 4.8 collective-permute-done.11.refs_2_
  97.5 3.9 shard_map.268
  102.9 3.6 shard_map.271
  107.0 3.5 collective-permute-done.16.refs_2_
  110.6 3.7 shard_map.269
  115.8 4.6 shard_map.272
  125.9 5.1 collective-permute-start.18
  153.4 3.9 shard_map.275
  157.2 3.8 shard_map.278
  164.0 10.8 %collective-permute-done.23.refs_2_ = bf16[128,1024]{1,0:T(8,128)(2,1)S(1)} collective-permute-done((bf16[128,1024]{1,0:T(8,128)(2,1)S(1)}, bf16[128,1024]{1,0:T(8,128)(2,1)S(1)}, u32[]{:S(2)}, u32[]{:S(2)}) %collective-permute-start.23) | collective-permute-done | bytes 262176 | tf_op jit(solution)/shard_map/ppermute | solution.py:33
  174.8 3.8 shard_map.276
  178.5 4.6 shard_map.279
  187.8 4.9 collective-permute-done.26.refs_2_
  203.7 5.2 shard_map.282
  210.2 5.8 shard_map.284
  217.6 6.1 shard_map.283
  224.5 6.9 %shard_map.285 = (f32[128,1024]{1,0:T(8,128)}, f32[128,512]{1,0:T(8,128)}, f32[3,1024]{1,0:T(4,128)}, f32[256,1024]{1,0:T(8,128)}, bf16[256,1024]{1,0:T(8,128)(2,1)}, /*index=5*/bf16[256,1024]{1,0:T(8,128)(2,1)}) custom-call(f32[128,1024]{1,0:T(8,128)} %get-tuple-element.314.refs_0_, bf16[128,1024]{1,0:T(8,128)(2,1)S(1)} %get-tuple-element.315.refs_1_, ...), custom_call_target="tpu_custom_call" | custom-call | tf_op jit(solution)/shard_map/pallas_call | solution.py:176
  236.7 3.6 shard_map.289
  244.1 5.4 collective-permute-done.41
  259.4 5.5 collective-permute-done.38.refs_1_
  269.3 5.0 shard_map.287
  274.4 6.0 shard_map.290
  282.8 6.7 %collective-permute-done.43.refs_2_ = bf16[128,1024]{1,0:T(8,128)(2,1)S(1)} collective-permute-done((bf16[128,1024]{1,0:T(8,128)(2,1)S(1)}, bf16[128,1024]{1,0:T(8,128)(2,1)S(1)}, u32[]{:S(2)}, u32[]{:S(2)}) %collective-permute-start.43) | collective-permute-done | bytes 262176 | tf_op jit(solution)/shard_map/ppermute | solution.py:33
  289.5 5.2 collective-permute-done.40.refs_2_
  294.7 6.1 shard_map.288
  300.9 6.8 %shard_map.291 = (f32[128,1024]{1,0:T(8,128)}, f32[128,512]{1,0:T(8,128)}, f32[3,1024]{1,0:T(4,128)}, f32[256,1024]{1,0:T(8,128)}, bf16[256,1024]{1,0:T(8,128)(2,1)S(1)}, /*index=5*/bf16[256,1024]{1,0:T(8,128)(2,1)}) custom-call(f32[128,1024]{1,0:T(8,128)} %get-tuple-element.346.refs_0_, bf16[128,1024]{1,0:T(8,128)(2,1)S(1)} %get-tuple-element.347.refs_1_, ...), custom_call_target="tpu_custom_call" | custom-call | tf_op jit(solution)/shard_map/pallas_call | solution.py:176
  317.9 7.1 %collective-permute-done.64 = f32[1024,128]{1,0:T(8,128)S(1)} collective-permute-done((f32[1024,128]{1,0:T(8,128)S(1)}, f32[1024,128]{1,0:T(8,128)S(1)}, u32[]{:S(2)}, u32[]{:S(2)}) %collective-permute-start.64) | collective-permute-done | bytes 524320 | tf_op jit(solution)/shard_map/ppermute | solution.py:82
  325.2 3.7 shard_map.296
  334.4 3.5 collective-permute-done.68
  341.3 5.9 shard_map.294.refs_10_.refs_4_
  347.3 5.9 shard_map.293.refs_9_.refs_4_
  353.1 3.6 shard_map.295.refs_11_.refs_4_
  357.6 5.1 shard_map.297.refs_12_.refs_4_
  368.3 5.0 shard_map.298
  373.3 5.8 shard_map.299
  382.2 5.7 shard_map.300
  394.8 5.9 shard_map.301
  400.7 6.3 shard_map.302
  409.7 5.2 collective-permute-start.84
  416.9 6.7 %shard_map.304 = (f32[128,1024]{1,0:T(8,128)}, f32[128,512]{1,0:T(8,128)}, f32[3,1024]{1,0:T(4,128)}, f32[256,1024]{1,0:T(8,128)}, bf16[256,1024]{1,0:T(8,128)(2,1)S(1)}, /*index=5*/bf16[256,1024]{1,0:T(8,128)(2,1)}) custom-call(f32[128,1024]{1,0:T(8,128)} %get-tuple-element.408.refs_0_, bf16[128,1024]{1,0:T(8,128)(2,1)S(1)} %get-tuple-element.409.refs_1_, ...), custom_call_target="tpu_custom_call" | custom-call | tf_op jit(solution)/shard_map/pallas_call | solution.py:176
  426.0 5.7 collective-permute-start.81
  446.2 7.2 %collective-permute-start.89 = (bf16[256,1024]{1,0:T(8,128)(2,1)}, bf16[256,1024]{1,0:T(8,128)(2,1)S(1)}, u32[]{:S(2)}, u32[]{:S(2)}) collective-permute-start(bf16[256,1024]{1,0:T(8,128)(2,1)} %copy-done.39), channel_id=1, source_target_pairs={{0,1},{3,2},{4,5},{7,6},{8,9},{11,10},{12,13},{15,14},{16,17},{19,... | collective-permute-start | bytes 1572872 | tf_op jit(solution)/shard_map/ppermute | solution.py:120
  458.5 5.2 collective-permute-done.90.refs_1_
  465.3 4.3 collective-permute-start.85
  471.3 4.3 collective-permute-done.87.refs_1_
  475.6 5.0 collective-permute-done.85.y_ref
  484.2 5.1 collective-permute-start.97
  498.8 3.7 shard_map.308
  505.5 7.7 %collective-permute-start.91 = (bf16[256,1024]{1,0:T(8,128)(2,1)}, bf16[256,1024]{1,0:T(8,128)(2,1)}, u32[]{:S(2)}, u32[]{:S(2)}) collective-permute-start(bf16[256,1024]{1,0:T(8,128)(2,1)} %get-tuple-element.438.x_ref), channel_id=1, source_target_pairs={{0,1},{3,2},{4,5},{7,6},{8,9},{11,10},{12,13},{15,14},{16,17},{19,... | collective-permute-start | bytes 1572872 | tf_op jit(solution)/shard_map/ppermute | solution.py:120
  526.3 6.2 collective-permute-start.105
  532.5 5.2 shard_map.316
  549.8 4.9 collective-permute-start.124
  554.9 6.5 %collective-permute-done.124 = f32[62,128]{1,0:T(8,128)S(1)} collective-permute-done((f32[62,128]{1,0:T(8,128)S(1)}, f32[62,128]{1,0:T(8,128)S(1)}, u32[]{:S(2)}, u32[]{:S(2)}) %collective-permute-start.124) | collective-permute-done | bytes 31776 | tf_op jit(solution)/shard_map/ppermute | solution.py:82
  575.1 5.1 collective-permute-start.113
  598.6 3.6 fusion.1
  607.9 3.4 fusion
  (792 shorter events, 297.6 us)
Async XLA Ops:
  7.3 249.5 %reduce-scatter.2.cloned.1.call-start = ((), (), s32[]{:S(2)}) async-start(), calls=%async_computation.1 | async-start | bytes 655360 | tf_op jit(solution)/shard_map/reduce_scatter | solution.py:802
  11.9 22.9 %collective-permute-start.2 = (bf16[1024,768]{1,0:T(8,128)(2,1)S(1)}, bf16[1024,768]{1,0:T(8,128)(2,1)}, u32[]{:S(2)}, u32[]{:S(2)}) collective-permute-start(bf16[1024,768]{1,0:T(8,128)(2,1)S(1)} %copy.63.own), channel_id=1, source_target_pairs={{0,4},{4,0},{8,12},{12,8},{1,5},{5,1},{9,13},{13,9},{2,6},{6,2},{1... | collective-permute-start | bytes 4718600 | tf_op jit(solution)/shard_map/ppermute | solution.py:33
  13.1 41.2 %collective-permute-start.8 = (bf16[1024,1024]{1,0:T(8,128)(2,1)}, bf16[1024,1024]{1,0:T(8,128)(2,1)}, u32[]{:S(2)}, u32[]{:S(2)}) collective-permute-start(bf16[1024,1024]{1,0:T(8,128)(2,1)} %bitcast.166), channel_id=1, source_target_pairs={{0,4},{4,0},{8,12},{12,8},{1,5},{5,1},{9,13},{13,9},{2,6},{6,2},{1... | collective-permute-start | bytes 6291464 | tf_op jit(solution)/shard_map/ppermute | solution.py:33
  13.1 43.2 %collective-permute-start.9 = (bf16[1024,1024]{1,0:T(8,128)(2,1)}, bf16[1024,1024]{1,0:T(8,128)(2,1)}, u32[]{:S(2)}, u32[]{:S(2)}) collective-permute-start(bf16[1024,1024]{1,0:T(8,128)(2,1)} %bitcast.168), channel_id=1, source_target_pairs={{0,4},{4,0},{8,12},{12,8},{1,5},{5,1},{9,13},{13,9},{2,6},{6,2},{1... | collective-permute-start | bytes 6291464 | tf_op jit(solution)/shard_map/ppermute | solution.py:33
  122.1 29.4 %collective-permute-start.30 = (f32[1,4,128]{2,1,0:T(4,128)}, f32[1,4,128]{2,1,0:T(4,128)}, u32[]{:S(2)}, u32[]{:S(2)}) collective-permute-start(f32[1,4,128]{2,1,0:T(4,128)} %fusion.25), channel_id=1, source_target_pairs={{0,1},{1,0},{2,3},{3,2},{4,5},{5,4},{6,7},{7,6},{8,9},{9,8},{10,11... | collective-permute-start | bytes 6152 | tf_op jit(solution)/shard_map/ppermute | solution.py:71
  125.9 15.0 %collective-permute-start.18 = (bf16[128,1024]{1,0:T(8,128)(2,1)}, bf16[128,1024]{1,0:T(8,128)(2,1)}, u32[]{:S(2)}, u32[]{:S(2)}) collective-permute-start(bf16[128,1024]{1,0:T(8,128)(2,1)} %get-tuple-element.270), channel_id=1, source_target_pairs={{0,16},{1,17},{2,18},{3,19},{4,20},{5,21},{6,22},{7,23},{8,24},{9,... | collective-permute-start | bytes 786440 | tf_op jit(solution)/shard_map/ppermute | solution.py:62
  148.8 14.2 %collective-permute-start.28 = (bf16[2,256,128]{2,1,0:T(8,128)(2,1)S(1)}, bf16[2,256,128]{2,1,0:T(8,128)(2,1)S(1)}, u32[]{:S(2)}, u32[]{:S(2)}) collective-permute-start(bf16[2,256,128]{2,1,0:T(8,128)(2,1)S(1)} %pad_maximum_fusion.5), channel_id=1, source_target_pairs={{0,2},{1,3},{2,0},{3,1},{4,6},{5,7},{6,4},{7,5},{8,10},{9,11},{10,... | collective-permute-start | bytes 393224 | tf_op jit(solution)/shard_map/ppermute | solution.py:71
  152.2 33.0 %collective-permute-start.31 = (f32[2,4,128]{2,1,0:T(4,128)S(1)}, f32[2,4,128]{2,1,0:T(4,128)S(1)}, u32[]{:S(2)}, u32[]{:S(2)}) collective-permute-start(f32[2,4,128]{2,1,0:T(4,128)S(1)} %pad_maximum_fusion.9), channel_id=1, source_target_pairs={{0,2},{1,3},{2,0},{3,1},{4,6},{5,7},{6,4},{7,5},{8,10},{9,11},{10,... | collective-permute-start | bytes 12296 | tf_op jit(solution)/shard_map/ppermute | solution.py:71
  161.0 17.5 %collective-permute-start.25 = (bf16[128,1024]{1,0:T(8,128)(2,1)S(1)}, bf16[128,1024]{1,0:T(8,128)(2,1)S(1)}, u32[]{:S(2)}, u32[]{:S(2)}) collective-permute-start(bf16[128,1024]{1,0:T(8,128)(2,1)S(1)} %get-tuple-element.289.refs_1_), channel_id=1, source_target_pairs={{0,8},{4,12},{8,0},{12,4},{1,9},{5,13},{9,1},{13,5},{2,10},{6,14},... | collective-permute-start | bytes 786440 | tf_op jit(solution)/shard_map/ppermute | solution.py:33
  164.0 22.6 %collective-permute-start.29 = (bf16[4,256,128]{2,1,0:T(8,128)(2,1)}, bf16[4,256,128]{2,1,0:T(8,128)(2,1)}, u32[]{:S(2)}, u32[]{:S(2)}) collective-permute-start(bf16[4,256,128]{2,1,0:T(8,128)(2,1)} %get-tuple-element.521), channel_id=1, source_target_pairs={{0,4},{4,0},{8,12},{12,8},{1,5},{5,1},{9,13},{13,9},{2,6},{6,2},{1... | collective-permute-start | bytes 786440 | tf_op jit(solution)/shard_map/ppermute | solution.py:33
  201.4 29.9 %collective-permute-start.39 = (f32[4,256,128]{2,1,0:T(8,128)S(1)}, f32[4,256,128]{2,1,0:T(8,128)S(1)}, u32[]{:S(2)}, u32[]{:S(2)}) collective-permute-start(f32[4,256,128]{2,1,0:T(8,128)S(1)} %slice_bitcast_fusion), channel_id=1, source_target_pairs={{0,4},{4,0},{8,12},{12,8},{1,5},{5,1},{9,13},{13,9},{2,6},{6,2},{1... | collective-permute-start | bytes 1572872 | tf_op jit(solution)/shard_map/ppermute | solution.py:33
  241.1 40.0 %collective-permute-start.60 = (bf16[256,1024]{1,0:T(8,128)(2,1)}, bf16[256,1024]{1,0:T(8,128)(2,1)}, u32[]{:S(2)}, u32[]{:S(2)}) collective-permute-start(bf16[256,1024]{1,0:T(8,128)(2,1)} %get-tuple-element.264.refs_0_.refs_2_), channel_id=1, source_target_pairs={{0,4},{4,0},{8,12},{12,8},{1,5},{5,1},{9,13},{13,9},{2,6},{6,2},{1... | collective-permute-start | bytes 1572872 | tf_op jit(solution)/shard_map/ppermute | solution.py:33
  241.1 67.1 %collective-permute-start.52 = (bf16[256,1024]{1,0:T(8,128)(2,1)}, bf16[256,1024]{1,0:T(8,128)(2,1)}, u32[]{:S(2)}, u32[]{:S(2)}) collective-permute-start(bf16[256,1024]{1,0:T(8,128)(2,1)} %get-tuple-element.366.refs_2_), channel_id=1, source_target_pairs={{0,4},{4,0},{8,12},{12,8},{1,5},{5,1},{9,13},{13,9},{2,6},{6,2},{1... | collective-permute-start | bytes 1572872 | tf_op jit(solution)/shard_map/ppermute | solution.py:33
  241.6 66.7 %collective-permute-start.48 = (bf16[256,1024]{1,0:T(8,128)(2,1)}, bf16[256,1024]{1,0:T(8,128)(2,1)}, u32[]{:S(2)}, u32[]{:S(2)}) collective-permute-start(bf16[256,1024]{1,0:T(8,128)(2,1)} %get-tuple-element.362), channel_id=1, source_target_pairs={{0,4},{4,0},{8,12},{12,8},{1,5},{5,1},{9,13},{13,9},{2,6},{6,2},{1... | collective-permute-start | bytes 1572872 | tf_op jit(solution)/shard_map/ppermute | solution.py:33
  250.3 24.0 %collective-permute-start.42 = (bf16[128,1024]{1,0:T(8,128)(2,1)}, bf16[128,1024]{1,0:T(8,128)(2,1)}, u32[]{:S(2)}, u32[]{:S(2)}) collective-permute-start(bf16[128,1024]{1,0:T(8,128)(2,1)} %add_convert_fusion), channel_id=1, source_target_pairs={{16,0},{17,1},{18,2},{19,3},{20,4},{21,5},{22,6},{23,7},{24,8},{25... | collective-permute-start | bytes 786440 | tf_op jit(solution)/shard_map/ppermute | solution.py:62
  264.9 44.1 %collective-permute-start.59 = (bf16[256,1024]{1,0:T(8,128)(2,1)}, bf16[256,1024]{1,0:T(8,128)(2,1)S(1)}, u32[]{:S(2)}, u32[]{:S(2)}) collective-permute-start(bf16[256,1024]{1,0:T(8,128)(2,1)} %get-tuple-element.280.refs_0_), channel_id=1, source_target_pairs={{0,4},{4,0},{8,12},{12,8},{1,5},{5,1},{9,13},{13,9},{2,6},{6,2},{1... | collective-permute-start | bytes 1572872 | tf_op jit(solution)/shard_map/ppermute | solution.py:33
  289.5 20.9 %collective-permute-start.63 = (f32[1024,128]{1,0:T(8,128)S(1)}, f32[1024,128]{1,0:T(8,128)S(1)}, u32[]{:S(2)}, u32[]{:S(2)}) collective-permute-start(f32[1024,128]{1,0:T(8,128)S(1)} %convolution_add_fusion), channel_id=1, source_target_pairs={{0,4},{4,0},{8,12},{12,8},{1,5},{5,1},{9,13},{13,9},{2,6},{6,2},{1... | collective-permute-start | bytes 1572872 | tf_op jit(solution)/shard_map/ppermute | solution.py:33
  312.0 16.9 %collective-permute-start.49 = (bf16[256,1024]{1,0:T(8,128)(2,1)S(1)}, bf16[256,1024]{1,0:T(8,128)(2,1)S(1)}, u32[]{:S(2)}, u32[]{:S(2)}) collective-permute-start(bf16[256,1024]{1,0:T(8,128)(2,1)S(1)} %copy-done.116), channel_id=1, source_target_pairs={{0,4},{4,0},{8,12},{12,8},{1,5},{5,1},{9,13},{13,9},{2,6},{6,2},{1... | collective-permute-start | bytes 1572872 | tf_op jit(solution)/shard_map/ppermute | solution.py:33
  331.2 25.5 %collective-permute-start.61 = (bf16[256,768]{1,0:T(8,128)(2,1)S(1)}, bf16[256,768]{1,0:T(8,128)(2,1)S(1)}, u32[]{:S(2)}, u32[]{:S(2)}) collective-permute-start(bf16[256,768]{1,0:T(8,128)(2,1)S(1)} %copy-done.197), channel_id=1, source_target_pairs={{0,4},{4,0},{8,12},{12,8},{1,5},{5,1},{9,13},{13,9},{2,6},{6,2},{1... | collective-permute-start | bytes 1179656 | tf_op jit(solution)/shard_map/ppermute | solution.py:33
  331.3 25.5 %collective-permute-start.62 = (bf16[256,768]{1,0:T(8,128)(2,1)S(1)}, bf16[256,768]{1,0:T(8,128)(2,1)S(1)}, u32[]{:S(2)}, u32[]{:S(2)}) collective-permute-start(bf16[256,768]{1,0:T(8,128)(2,1)S(1)} %copy-done.198), channel_id=1, source_target_pairs={{0,4},{4,0},{8,12},{12,8},{1,5},{5,1},{9,13},{13,9},{2,6},{6,2},{1... | collective-permute-start | bytes 1179656 | tf_op jit(solution)/shard_map/ppermute | solution.py:33
  331.9 30.9 %collective-permute-start.65 = (f32[1024,128]{1,0:T(8,128)S(1)}, f32[1024,128]{1,0:T(8,128)S(1)}, u32[]{:S(2)}, u32[]{:S(2)}) collective-permute-start(f32[1024,128]{1,0:T(8,128)S(1)} %add.181), channel_id=1, source_target_pairs={{0,2},{1,3},{2,0},{3,1},{4,6},{5,7},{6,4},{7,5},{8,10},{9,11},{10,... | collective-permute-start | bytes 1572872 | tf_op jit(solution)/shard_map/ppermute | solution.py:82
  337.8 25.0 %collective-permute-start.46 = (bf16[128,1024]{1,0:T(8,128)(2,1)S(1)}, bf16[128,1024]{1,0:T(8,128)(2,1)S(1)}, u32[]{:S(2)}, u32[]{:S(2)}) collective-permute-start(bf16[128,1024]{1,0:T(8,128)(2,1)S(1)} %get-tuple-element.510), channel_id=1, source_target_pairs={{16,0},{17,1},{18,2},{19,3},{20,4},{21,5},{22,6},{23,7},{24,8},{25... | collective-permute-start | bytes 786440 | tf_op jit(solution)/shard_map/ppermute | solution.py:62
  340.0 33.3 %collective-permute-start.69 = (bf16[128,1024]{1,0:T(8,128)(2,1)S(1)}, bf16[128,1024]{1,0:T(8,128)(2,1)S(1)}, u32[]{:S(2)}, u32[]{:S(2)}) collective-permute-start(bf16[128,1024]{1,0:T(8,128)(2,1)S(1)} %get-tuple-element.508), channel_id=1, source_target_pairs={{16,0},{17,1},{18,2},{19,3},{20,4},{21,5},{22,6},{23,7},{24,8},{25... | collective-permute-start | bytes 786440 | tf_op jit(solution)/shard_map/ppermute | solution.py:62
  356.8 23.4 %collective-permute-start.67 = (bf16[256,1024]{1,0:T(8,128)(2,1)S(1)}, bf16[256,1024]{1,0:T(8,128)(2,1)S(1)}, u32[]{:S(2)}, u32[]{:S(2)}) collective-permute-start(bf16[256,1024]{1,0:T(8,128)(2,1)S(1)} %copy-done.193), channel_id=1, source_target_pairs={{0,4},{4,0},{8,12},{12,8},{1,5},{5,1},{9,13},{13,9},{2,6},{6,2},{1... | collective-permute-start | bytes 1572872 | tf_op jit(solution)/shard_map/ppermute | solution.py:33
  387.9 19.1 %collective-permute-start.74 = (bf16[256,1024]{1,0:T(8,128)(2,1)S(1)}, bf16[256,1024]{1,0:T(8,128)(2,1)S(1)}, u32[]{:S(2)}, u32[]{:S(2)}) collective-permute-start(bf16[256,1024]{1,0:T(8,128)(2,1)S(1)} %get-tuple-element.401.refs_13_.x_ref), channel_id=1, source_target_pairs={{0,1},{3,2},{4,5},{7,6},{8,9},{11,10},{12,13},{15,14},{16,17},{19,... | collective-permute-start | bytes 1572872 | tf_op jit(solution)/shard_map/ppermute | solution.py:120
  392.3 31.3 %collective-permute-start.77 = (bf16[256,1024]{1,0:T(8,128)(2,1)S(1)}, bf16[256,1024]{1,0:T(8,128)(2,1)S(1)}, u32[]{:S(2)}, u32[]{:S(2)}) collective-permute-start(bf16[256,1024]{1,0:T(8,128)(2,1)S(1)} %get-tuple-element.419.x_ref), channel_id=1, source_target_pairs={{0,1},{3,2},{4,5},{7,6},{8,9},{11,10},{12,13},{15,14},{16,17},{19,... | collective-permute-start | bytes 1572872 | tf_op jit(solution)/shard_map/ppermute | solution.py:120
  408.1 23.6 %collective-permute-start.76 = (bf16[256,1024]{1,0:T(8,128)(2,1)S(1)}, bf16[256,1024]{1,0:T(8,128)(2,1)S(1)}, u32[]{:S(2)}, u32[]{:S(2)}) collective-permute-start(bf16[256,1024]{1,0:T(8,128)(2,1)S(1)} %get-tuple-element.416.refs_16_.refs_2_.x_ref), channel_id=1, source_target_pairs={{1,2},{2,1},{5,6},{6,5},{9,10},{10,9},{13,14},{14,13},{17,18},{18,... | collective-permute-start | bytes 1572872 | tf_op jit(solution)/shard_map/ppermute | solution.py:132
  409.7 27.5 %collective-permute-start.84 = (bf16[256,1024]{1,0:T(8,128)(2,1)}, bf16[256,1024]{1,0:T(8,128)(2,1)}, u32[]{:S(2)}, u32[]{:S(2)}) collective-permute-start(bf16[256,1024]{1,0:T(8,128)(2,1)} %get-tuple-element.430.x_ref), channel_id=1, source_target_pairs={{0,1},{3,2},{4,5},{7,6},{8,9},{11,10},{12,13},{15,14},{16,17},{19,... | collective-permute-start | bytes 1572872 | tf_op jit(solution)/shard_map/ppermute | solution.py:120
  424.5 19.0 %collective-permute-start.83 = (bf16[256,1024]{1,0:T(8,128)(2,1)}, bf16[256,1024]{1,0:T(8,128)(2,1)}, u32[]{:S(2)}, u32[]{:S(2)}) collective-permute-start(bf16[256,1024]{1,0:T(8,128)(2,1)} %get-tuple-element.421.refs_0_.x_ref), channel_id=1, source_target_pairs={{1,2},{2,1},{5,6},{6,5},{9,10},{10,9},{13,14},{14,13},{17,18},{18,... | collective-permute-start | bytes 1572872 | tf_op jit(solution)/shard_map/ppermute | solution.py:132
  426.0 20.2 %collective-permute-start.81 = (bf16[256,1024]{1,0:T(8,128)(2,1)}, bf16[256,1024]{1,0:T(8,128)(2,1)}, u32[]{:S(2)}, u32[]{:S(2)}) collective-permute-start(bf16[256,1024]{1,0:T(8,128)(2,1)} %get-tuple-element.428.x_ref), channel_id=1, source_target_pairs={{0,1},{3,2},{4,5},{7,6},{8,9},{11,10},{12,13},{15,14},{16,17},{19,... | collective-permute-start | bytes 1572872 | tf_op jit(solution)/shard_map/ppermute | solution.py:120
  432.6 20.8 %collective-permute-start.82 = (bf16[256,1024]{1,0:T(8,128)(2,1)}, bf16[256,1024]{1,0:T(8,128)(2,1)}, u32[]{:S(2)}, u32[]{:S(2)}) collective-permute-start(bf16[256,1024]{1,0:T(8,128)(2,1)} %shard_map.306.refs_6_.refs_1_), channel_id=1, source_target_pairs={{1,0},{2,3},{5,4},{6,7},{9,8},{10,11},{13,12},{14,15},{17,16},{18,... | collective-permute-start | bytes 1572872 | tf_op jit(solution)/shard_map/ppermute | solution.py:138
  437.3 46.3 %collective-permute-start.92 = (bf16[256,1024]{1,0:T(8,128)(2,1)}, bf16[256,1024]{1,0:T(8,128)(2,1)}, u32[]{:S(2)}, u32[]{:S(2)}) collective-permute-start(bf16[256,1024]{1,0:T(8,128)(2,1)} %get-tuple-element.248.refs_0_), channel_id=1, source_target_pairs={{0,4},{4,0},{8,12},{12,8},{1,5},{5,1},{9,13},{13,9},{2,6},{6,2},{1... | collective-permute-start | bytes 1572872 | tf_op jit(solution)/shard_map/ppermute | solution.py:33
  441.2 14.6 %collective-permute-start.86 = (bf16[256,1024]{1,0:T(8,128)(2,1)}, bf16[256,1024]{1,0:T(8,128)(2,1)}, u32[]{:S(2)}, u32[]{:S(2)}) collective-permute-start(bf16[256,1024]{1,0:T(8,128)(2,1)} %get-tuple-element.431.refs_0_.x_ref), channel_id=1, source_target_pairs={{1,2},{2,1},{5,6},{6,5},{9,10},{10,9},{13,14},{14,13},{17,18},{18,... | collective-permute-start | bytes 1572872 | tf_op jit(solution)/shard_map/ppermute | solution.py:132
  444.9 18.9 %collective-permute-start.90 = (bf16[256,1024]{1,0:T(8,128)(2,1)S(1)}, bf16[256,1024]{1,0:T(8,128)(2,1)S(1)}, u32[]{:S(2)}, u32[]{:S(2)}) collective-permute-start(bf16[256,1024]{1,0:T(8,128)(2,1)S(1)} %shard_map.310.refs_2_), channel_id=1, source_target_pairs={{1,0},{2,3},{5,4},{6,7},{9,8},{10,11},{13,12},{14,15},{17,16},{18,... | collective-permute-start | bytes 1572872 | tf_op jit(solution)/shard_map/ppermute | solution.py:138
  446.2 19.1 %collective-permute-start.89 = (bf16[256,1024]{1,0:T(8,128)(2,1)}, bf16[256,1024]{1,0:T(8,128)(2,1)S(1)}, u32[]{:S(2)}, u32[]{:S(2)}) collective-permute-start(bf16[256,1024]{1,0:T(8,128)(2,1)} %copy-done.39), channel_id=1, source_target_pairs={{0,1},{3,2},{4,5},{7,6},{8,9},{11,10},{12,13},{15,14},{16,17},{19,... | collective-permute-start | bytes 1572872 | tf_op jit(solution)/shard_map/ppermute | solution.py:120
  454.9 14.8 %collective-permute-start.88 = (bf16[256,1024]{1,0:T(8,128)(2,1)S(1)}, bf16[256,1024]{1,0:T(8,128)(2,1)S(1)}, u32[]{:S(2)}, u32[]{:S(2)}) collective-permute-start(bf16[256,1024]{1,0:T(8,128)(2,1)S(1)} %get-tuple-element.434.refs_0_.x_ref), channel_id=1, source_target_pairs={{1,2},{2,1},{5,6},{6,5},{9,10},{10,9},{13,14},{14,13},{17,18},{18,... | collective-permute-start | bytes 1572872 | tf_op jit(solution)/shard_map/ppermute | solution.py:132
  457.2 18.4 %collective-permute-start.87 = (bf16[256,1024]{1,0:T(8,128)(2,1)S(1)}, bf16[256,1024]{1,0:T(8,128)(2,1)S(1)}, u32[]{:S(2)}, u32[]{:S(2)}) collective-permute-start(bf16[256,1024]{1,0:T(8,128)(2,1)S(1)} %shard_map.312.refs_2_), channel_id=1, source_target_pairs={{1,0},{2,3},{5,4},{6,7},{9,8},{10,11},{13,12},{14,15},{17,16},{18,... | collective-permute-start | bytes 1572872 | tf_op jit(solution)/shard_map/ppermute | solution.py:138
  463.8 25.5 %collective-permute-start.75 = (bf16[256,1024]{1,0:T(8,128)(2,1)S(1)}, bf16[256,1024]{1,0:T(8,128)(2,1)S(1)}, u32[]{:S(2)}, u32[]{:S(2)}) collective-permute-start(bf16[256,1024]{1,0:T(8,128)(2,1)S(1)} %copy-done.85), channel_id=1, source_target_pairs={{0,4},{4,0},{8,12},{12,8},{1,5},{5,1},{9,13},{13,9},{2,6},{6,2},{1... | collective-permute-start | bytes 1572872 | tf_op jit(solution)/shard_map/ppermute | solution.py:33
  465.3 15.3 %collective-permute-start.85 = (bf16[256,1024]{1,0:T(8,128)(2,1)}, bf16[256,1024]{1,0:T(8,128)(2,1)S(1)}, u32[]{:S(2)}, u32[]{:S(2)}) collective-permute-start(bf16[256,1024]{1,0:T(8,128)(2,1)} %get-tuple-element.432.x_ref), channel_id=1, source_target_pairs={{0,1},{3,2},{4,5},{7,6},{8,9},{11,10},{12,13},{15,14},{16,17},{19,... | collective-permute-start | bytes 1572872 | tf_op jit(solution)/shard_map/ppermute | solution.py:120
  469.8 20.7 %collective-permute-start.94 = (bf16[256,1024]{1,0:T(8,128)(2,1)S(1)}, bf16[256,1024]{1,0:T(8,128)(2,1)S(1)}, u32[]{:S(2)}, u32[]{:S(2)}) collective-permute-start(bf16[256,1024]{1,0:T(8,128)(2,1)S(1)} %get-tuple-element.437.refs_0_.x_ref), channel_id=1, source_target_pairs={{1,2},{2,1},{5,6},{6,5},{9,10},{10,9},{13,14},{14,13},{17,18},{18,... | collective-permute-start | bytes 1572872 | tf_op jit(solution)/shard_map/ppermute | solution.py:132
  475.6 27.2 %collective-permute-start.99 = (bf16[256,1024]{1,0:T(8,128)(2,1)}, bf16[256,1024]{1,0:T(8,128)(2,1)}, u32[]{:S(2)}, u32[]{:S(2)}) collective-permute-start(bf16[256,1024]{1,0:T(8,128)(2,1)} %get-tuple-element.446.refs_2_), channel_id=1, source_target_pairs={{0,4},{4,0},{8,12},{12,8},{1,5},{5,1},{9,13},{13,9},{2,6},{6,2},{1... | collective-permute-start | bytes 1572872 | tf_op jit(solution)/shard_map/ppermute | solution.py:33
  483.6 19.1 %collective-permute-start.121 = (f32[1,1024]{1,0:T(1,128)}, f32[1,1024]{1,0:T(1,128)S(1)}, u32[]{:S(2)}, u32[]{:S(2)}) collective-permute-start(f32[1,1024]{1,0:T(1,128)} %slice.227), channel_id=1, source_target_pairs={{0,4},{4,0},{8,12},{12,8},{1,5},{5,1},{9,13},{13,9},{2,6},{6,2},{1... | collective-permute-start | bytes 12296 | tf_op jit(solution)/shard_map/ppermute | solution.py:33
  484.2 20.7 %collective-permute-start.97 = (bf16[256,1024]{1,0:T(8,128)(2,1)}, bf16[256,1024]{1,0:T(8,128)(2,1)}, u32[]{:S(2)}, u32[]{:S(2)}) collective-permute-start(bf16[256,1024]{1,0:T(8,128)(2,1)} %get-tuple-element.443.x_ref), channel_id=1, source_target_pairs={{0,1},{3,2},{4,5},{7,6},{8,9},{11,10},{12,13},{15,14},{16,17},{19,... | collective-permute-start | bytes 1572872 | tf_op jit(solution)/shard_map/ppermute | solution.py:120
  489.2 16.2 %collective-permute-start.100 = (bf16[256,1024]{1,0:T(8,128)(2,1)}, bf16[256,1024]{1,0:T(8,128)(2,1)}, u32[]{:S(2)}, u32[]{:S(2)}) collective-permute-start(bf16[256,1024]{1,0:T(8,128)(2,1)} %shard_map.314.refs_2_), channel_id=1, source_target_pairs={{1,0},{2,3},{5,4},{6,7},{9,8},{10,11},{13,12},{14,15},{17,16},{18,... | collective-permute-start | bytes 1572872 | tf_op jit(solution)/shard_map/ppermute | solution.py:138
  502.7 21.5 %collective-permute-start.93 = (bf16[256,768]{1,0:T(8,128)(2,1)}, bf16[256,768]{1,0:T(8,128)(2,1)S(1)}, u32[]{:S(2)}, u32[]{:S(2)}) collective-permute-start(bf16[256,768]{1,0:T(8,128)(2,1)} %get-tuple-element.440), channel_id=1, source_target_pairs={{0,4},{4,0},{8,12},{12,8},{1,5},{5,1},{9,13},{13,9},{2,6},{6,2},{1... | collective-permute-start | bytes 1179656 | tf_op jit(solution)/shard_map/ppermute | solution.py:33
  502.8 22.7 %collective-permute-start.95 = (bf16[256,1024]{1,0:T(8,128)(2,1)S(1)}, bf16[256,1024]{1,0:T(8,128)(2,1)S(1)}, u32[]{:S(2)}, u32[]{:S(2)}) collective-permute-start(bf16[256,1024]{1,0:T(8,128)(2,1)S(1)} %shard_map.317.refs_2_), channel_id=1, source_target_pairs={{1,0},{2,3},{5,4},{6,7},{9,8},{10,11},{13,12},{14,15},{17,16},{18,... | collective-permute-start | bytes 1572872 | tf_op jit(solution)/shard_map/ppermute | solution.py:138
  504.9 16.4 %collective-permute-start.123 = (f32[6,1024]{1,0:T(8,128)S(1)}, f32[6,1024]{1,0:T(8,128)S(1)}, u32[]{:S(2)}, u32[]{:S(2)}) collective-permute-start(f32[6,1024]{1,0:T(8,128)S(1)} %copy-done.148), channel_id=1, source_target_pairs={{0,4},{4,0},{8,12},{12,8},{1,5},{5,1},{9,13},{13,9},{2,6},{6,2},{1... | collective-permute-start | bytes 73736 | tf_op jit(solution)/shard_map/ppermute | solution.py:33
  505.4 17.3 %collective-permute-start.122 = (f32[1,768]{1,0:T(1,128)S(1)}, f32[1,768]{1,0:T(1,128)S(1)}, u32[]{:S(2)}, u32[]{:S(2)}) collective-permute-start(f32[1,768]{1,0:T(1,128)S(1)} %slice.229), channel_id=1, source_target_pairs={{0,4},{4,0},{8,12},{12,8},{1,5},{5,1},{9,13},{13,9},{2,6},{6,2},{1... | collective-permute-start | bytes 9224 | tf_op jit(solution)/shard_map/ppermute | solution.py:33
  505.5 32.2 %collective-permute-start.91 = (bf16[256,1024]{1,0:T(8,128)(2,1)}, bf16[256,1024]{1,0:T(8,128)(2,1)}, u32[]{:S(2)}, u32[]{:S(2)}) collective-permute-start(bf16[256,1024]{1,0:T(8,128)(2,1)} %get-tuple-element.438.x_ref), channel_id=1, source_target_pairs={{0,1},{3,2},{4,5},{7,6},{8,9},{11,10},{12,13},{15,14},{16,17},{19,... | collective-permute-start | bytes 1572872 | tf_op jit(solution)/shard_map/ppermute | solution.py:120
  521.3 18.6 %collective-permute-start.79 = (bf16[128,1024]{1,0:T(8,128)(2,1)}, bf16[128,1024]{1,0:T(8,128)(2,1)S(1)}, u32[]{:S(2)}, u32[]{:S(2)}) collective-permute-start(bf16[128,1024]{1,0:T(8,128)(2,1)} %get-tuple-element.427), channel_id=1, source_target_pairs={{0,8},{4,12},{8,0},{12,4},{1,9},{5,13},{9,1},{13,5},{2,10},{6,14},... | collective-permute-start | bytes 786440 | tf_op jit(solution)/shard_map/ppermute | solution.py:33
  522.7 19.1 %collective-permute-start.102 = (bf16[256,1024]{1,0:T(8,128)(2,1)}, bf16[256,1024]{1,0:T(8,128)(2,1)}, u32[]{:S(2)}, u32[]{:S(2)}) collective-permute-start(bf16[256,1024]{1,0:T(8,128)(2,1)} %get-tuple-element.447.refs_0_.x_ref), channel_id=1, source_target_pairs={{1,2},{2,1},{5,6},{6,5},{9,10},{10,9},{13,14},{14,13},{17,18},{18,... | collective-permute-start | bytes 1572872 | tf_op jit(solution)/shard_map/ppermute | solution.py:132
  524.2 19.1 %collective-permute-start.106 = (bf16[256,1024]{1,0:T(8,128)(2,1)S(1)}, bf16[256,1024]{1,0:T(8,128)(2,1)}, u32[]{:S(2)}, u32[]{:S(2)}) collective-permute-start(bf16[256,1024]{1,0:T(8,128)(2,1)S(1)} %shard_map.320.refs_2_), channel_id=1, source_target_pairs={{1,0},{2,3},{5,4},{6,7},{9,8},{10,11},{13,12},{14,15},{17,16},{18,... | collective-permute-start | bytes 1572872 | tf_op jit(solution)/shard_map/ppermute | solution.py:138
  526.3 19.9 %collective-permute-start.105 = (bf16[256,1024]{1,0:T(8,128)(2,1)}, bf16[256,1024]{1,0:T(8,128)(2,1)}, u32[]{:S(2)}, u32[]{:S(2)}) collective-permute-start(bf16[256,1024]{1,0:T(8,128)(2,1)} %get-tuple-element.451.x_ref), channel_id=1, source_target_pairs={{0,1},{3,2},{4,5},{7,6},{8,9},{11,10},{12,13},{15,14},{16,17},{19,... | collective-permute-start | bytes 1572872 | tf_op jit(solution)/shard_map/ppermute | solution.py:120
  541.8 25.5 %collective-permute-start.126 = (f32[512,128]{1,0:T(8,128)S(1)}, f32[512,128]{1,0:T(8,128)S(1)}, u32[]{:S(2)}, u32[]{:S(2)}) collective-permute-start(f32[512,128]{1,0:T(8,128)S(1)} %copy-done.144), channel_id=1, source_target_pairs={{0,16},{16,0},{1,17},{17,1},{2,18},{18,2},{3,19},{19,3},{4,20},{20... | collective-permute-start | bytes 786440 | tf_op jit(solution)/shard_map/ppermute | solution.py:62
  543.2 19.9 %collective-permute-start.101 = (bf16[256,768]{1,0:T(8,128)(2,1)S(1)}, bf16[256,768]{1,0:T(8,128)(2,1)S(1)}, u32[]{:S(2)}, u32[]{:S(2)}) collective-permute-start(bf16[256,768]{1,0:T(8,128)(2,1)S(1)} %get-tuple-element.448.x_ref), channel_id=1, source_target_pairs={{0,1},{3,2},{4,5},{7,6},{8,9},{11,10},{12,13},{15,14},{16,17},{19,... | collective-permute-start | bytes 1179656 | tf_op jit(solution)/shard_map/ppermute | solution.py:120
  546.2 18.2 %collective-permute-start.103 = (bf16[256,1024]{1,0:T(8,128)(2,1)S(1)}, bf16[256,1024]{1,0:T(8,128)(2,1)S(1)}, u32[]{:S(2)}, u32[]{:S(2)}) collective-permute-start(bf16[256,1024]{1,0:T(8,128)(2,1)S(1)} %shard_map.322.refs_2_), channel_id=1, source_target_pairs={{1,0},{2,3},{5,4},{6,7},{9,8},{10,11},{13,12},{14,15},{17,16},{18,... | collective-permute-start | bytes 1572872 | tf_op jit(solution)/shard_map/ppermute | solution.py:138
  548.9 20.4 %collective-permute-start.110 = (bf16[256,1024]{1,0:T(8,128)(2,1)S(1)}, bf16[256,1024]{1,0:T(8,128)(2,1)S(1)}, u32[]{:S(2)}, u32[]{:S(2)}) collective-permute-start(bf16[256,1024]{1,0:T(8,128)(2,1)S(1)} %get-tuple-element.453.refs_0_.x_ref), channel_id=1, source_target_pairs={{1,2},{2,1},{5,6},{6,5},{9,10},{10,9},{13,14},{14,13},{17,18},{18,... | collective-permute-start | bytes 1572872 | tf_op jit(solution)/shard_map/ppermute | solution.py:132
  561.4 24.5 %collective-permute-start.80 = (f32[2,128,512]{2,1,0:T(8,128)S(1)}, f32[2,128,512]{2,1,0:T(8,128)S(1)}, u32[]{:S(2)}, u32[]{:S(2)}) collective-permute-start(f32[2,128,512]{2,1,0:T(8,128)S(1)} %pad_maximum_fusion), channel_id=1, source_target_pairs={{0,16},{16,0},{1,17},{17,1},{2,18},{18,2},{3,19},{19,3},{4,20},{20... | collective-permute-start | bytes 1572872 | tf_op jit(solution)/shard_map/ppermute | solution.py:62
  563.2 17.1 %collective-permute-start.109 = (bf16[256,1024]{1,0:T(8,128)(2,1)S(1)}, bf16[256,1024]{1,0:T(8,128)(2,1)S(1)}, u32[]{:S(2)}, u32[]{:S(2)}) collective-permute-start(bf16[256,1024]{1,0:T(8,128)(2,1)S(1)} %shard_map.324.refs_2_), channel_id=1, source_target_pairs={{1,0},{2,3},{5,4},{6,7},{9,8},{10,11},{13,12},{14,15},{17,16},{18,... | collective-permute-start | bytes 1572872 | tf_op jit(solution)/shard_map/ppermute | solution.py:138
  570.9 21.5 %collective-permute-start.114 = (bf16[256,1024]{1,0:T(8,128)(2,1)S(1)}, bf16[256,1024]{1,0:T(8,128)(2,1)}, u32[]{:S(2)}, u32[]{:S(2)}) collective-permute-start(bf16[256,1024]{1,0:T(8,128)(2,1)S(1)} %shard_map.326.refs_2_), channel_id=1, source_target_pairs={{1,0},{2,3},{5,4},{6,7},{9,8},{10,11},{13,12},{14,15},{17,16},{18,... | collective-permute-start | bytes 1572872 | tf_op jit(solution)/shard_map/ppermute | solution.py:138
  575.1 17.2 %collective-permute-start.113 = (bf16[256,768]{1,0:T(8,128)(2,1)}, bf16[256,768]{1,0:T(8,128)(2,1)}, u32[]{:S(2)}, u32[]{:S(2)}) collective-permute-start(bf16[256,768]{1,0:T(8,128)(2,1)} %get-tuple-element.458.x_ref), channel_id=1, source_target_pairs={{0,1},{3,2},{4,5},{7,6},{8,9},{11,10},{12,13},{15,14},{16,17},{19,... | collective-permute-start | bytes 1179656 | tf_op jit(solution)/shard_map/ppermute | solution.py:120
  602.2 19.4 %collective-permute-start.115 = (bf16[256,768]{1,0:T(8,128)(2,1)}, bf16[256,768]{1,0:T(8,128)(2,1)}, u32[]{:S(2)}, u32[]{:S(2)}) collective-permute-start(bf16[256,768]{1,0:T(8,128)(2,1)} %shard_map.330.refs_1_), channel_id=1, source_target_pairs={{1,0},{2,3},{5,4},{6,7},{9,8},{10,11},{13,12},{14,15},{17,16},{18,... | collective-permute-start | bytes 1179656 | tf_op jit(solution)/shard_map/ppermute | solution.py:138
  604.5 23.4 %collective-permute-start.118 = (bf16[256,768]{1,0:T(8,128)(2,1)}, bf16[256,768]{1,0:T(8,128)(2,1)}, u32[]{:S(2)}, u32[]{:S(2)}) collective-permute-start(bf16[256,768]{1,0:T(8,128)(2,1)} %shard_map.332.refs_0_), channel_id=1, source_target_pairs={{1,0},{2,3},{5,4},{6,7},{9,8},{10,11},{13,12},{14,15},{17,16},{18,... | collective-permute-start | bytes 1179656 | tf_op jit(solution)/shard_map/ppermute | solution.py:138
  606.6 25.5 %collective-permute-start.120 = (bf16[256,768]{1,0:T(8,128)(2,1)}, bf16[256,768]{1,0:T(8,128)(2,1)}, u32[]{:S(2)}, u32[]{:S(2)}) collective-permute-start(bf16[256,768]{1,0:T(8,128)(2,1)} %shard_map.333), channel_id=1, source_target_pairs={{1,0},{2,3},{5,4},{6,7},{9,8},{10,11},{13,12},{14,15},{17,16},{18,... | collective-permute-start | bytes 1179656 | tf_op jit(solution)/shard_map/ppermute | solution.py:138
  (266 other events, 2754.5 us)
Sparse Core Ops, SparseCore 0:
  232.3 21.9 reduce-scatter.1
